TPU v7x, 32 devices: a whole 2x2x4 slice. The times are simulated.
32 devices in a mesh: seq: 16 (over z, y, x), wa: 2 (over core).
Axes of the slice: x: 2, y: 2, z: 4, core: 2. Of those that a mesh axis runs over, the one named last changes fastest.
Arguments:
- tokens: bfloat16 [16384, 1024], P(('seq', 'wa')), may hold values from -6 to 6
- cotangent: bfloat16 [16384, 1024], P(('seq', 'wa')), may hold values from -6 to 6
- doc_lengths: int32 [32], replicated, may hold values from 1 to 4096, as said below
- norm_gain: bfloat16 [1024], P('wa'), may hold values from 0.25 to 1.75
- in_weight: bfloat16 [1024, 3072], P('wa'), may hold values from -0.1875 to 0.1875
- conv_taps: bfloat16 [1024, 3], P('wa'), may hold values from -3.5 to 3.5
- out_weight: bfloat16 [1024, 1024], P('wa'), may hold values from -0.1875 to 0.1875
- ffn_gain: bfloat16 [1024], P('wa'), may hold values from 0.25 to 1.75
- gate_weight: bfloat16 [1024, 4608], P('wa'), may hold values from -0.1875 to 0.1875
- up_weight: bfloat16 [1024, 4608], P('wa'), may hold values from -0.1875 to 0.1875
- down_weight: bfloat16 [4608, 1024], P('wa'), may hold values from -0.09375 to 0.09375
Outputs:
- block_out: bfloat16 [16384, 1024], P(('seq', 'wa'))
- input_grad: bfloat16 [16384, 1024], P(('seq', 'wa'))
- norm_gain_grad: float32 [1024], P(('seq', 'wa'))
- in_weight_grad: float32 [1024, 3072], P(('seq', 'wa'))
- conv_taps_grad: float32 [1024, 3], P(('seq', 'wa'))
- out_weight_grad: float32 [1024, 1024], P(('seq', 'wa'))
- ffn_gain_grad: float32 [1024], P(('seq', 'wa'))
- gate_weight_grad: float32 [1024, 4608], P(('seq', 'wa'))
- up_weight_grad: float32 [1024, 4608], P(('seq', 'wa'))
- down_weight_grad: float32 [4608, 1024], P(('seq', 'wa'))
Inputs may be any that keep to these rules, and one draw needn't show every extreme that they name: `doc_lengths`: lengths of the 32 documents laid end to end in stream order, summing to 16384; the first document has exactly 4096 tokens.
All inputs are finite; a program needn't handle non-finite values.
Results may differ from a plain program's by a relative error of at most 0.0086.
Values may be sent and summed in bfloat16 or wider, within the bound.
No kernel may reach another device: no remote copies, remote signals or barrier semaphores. Data moves between devices by JAX's collectives and lax.ppermute only.
A program may use at most 256 MiB of HBM per device.

v0:
```python
import functools
import math

import jax
import jax.numpy as jnp
from jax import lax
from jax.experimental import pallas as pl
from jax.experimental.pallas import tpu as pltpu
from jax.sharding import PartitionSpec as P

epsilon = 1e-05
AXES = ("seq", "wa")
HALO = 16
TILE = 256
VMEM_LIMIT = 58 * 2**20
NN = ((1,), (0,))
NT = ((1,), (1,))
TN = ((0,), (0,))


def shifted(value, steps):
    count = lax.axis_size(AXES)
    first, last = (max(0, -steps), min(count, count - steps))
    return lax.ppermute(value, AXES, [(source, source + steps) for source in range(first, last)])


def partner(value):
    return lax.ppermute(value, "wa", [(0, 1), (1, 0)])


def across(value, bit):
    count = lax.axis_size("seq")
    return lax.ppermute(value, "seq", [(place, place ^ (1 << bit)) for place in range(count)])


def dot(left, right, dims):
    return lax.dot_general(left, right, (dims, ((), ())), preferred_element_type=jnp.float32)


def take(value, index, axis):
    return lax.dynamic_index_in_dim(value, index, axis, keepdims=False)


def total(terms):
    result = terms[0].astype(jnp.float32)
    for term in terms[1:]:
        result = result + term.astype(jnp.float32)
    return result


def chosen(test, value, other):
    return jnp.where(test, value, other)


def swapped(value):
    half = value.shape[1] // 2
    return jnp.concatenate([value[:, half:], value[:, :half]], axis=1)


def params(**extra):
    return dict(
        compiler_params=pltpu.CompilerParams(vmem_limit_bytes=VMEM_LIMIT),
        cost_estimate=pl.CostEstimate(flops=1000, bytes_accessed=1000, transcendentals=0),
        **extra,
    )


def conv_rows(mixed, keep_one, keep_two, taps, count):
    now = mixed[pl.ds(HALO, count), :]
    one = mixed[pl.ds(HALO - 1, count), :] * keep_one
    two = mixed[pl.ds(HALO - 2, count), :] * keep_two
    conv = taps[2:3, :] * now + taps[3:4, :] * one + taps[4:5, :] * two
    return now, one, two, conv


def join_rows(weights, own, other):
    half = own[0].shape[0]
    for index, (upper, lower) in enumerate(zip(own, other)):
        weights[:half, index * TILE : (index + 1) * TILE] = upper[...]
        weights[half:, index * TILE : (index + 1) * TILE] = lower[...]


def forward_kernel(
    info,
    tokens,
    before,
    after,
    small,
    taps,
    keeps,
    own_b,
    own_c,
    own_x,
    other_b,
    other_c,
    other_x,
    out_own,
    out_other,
    b_ref,
    c_ref,
    x_ref,
    hidden,
    norm_own,
    norm_send,
    normed,
    weights,
    mixed,
    gated,
    total_ref,
):
    step = pl.program_id(0)
    first_core = info[0] == 0
    rows, width = tokens.shape
    half = width // 2
    ext = rows + HALO

    @pl.when(step == 0)
    def _():
        for start, ref in ((0, before), (HALO, tokens), (HALO + rows, after)):
            resid = ref[:, :width].astype(jnp.float32)
            scale = lax.rsqrt(jnp.mean(resid * resid, axis=-1, keepdims=True) + epsilon)
            norm = resid * scale * small[0:1, :]
            place = pl.ds(start, ref.shape[0])
            normed[place, :half] = chosen(first_core, norm[:, :half], norm[:, half:]).astype(
                jnp.bfloat16
            )
            normed[place, half:] = chosen(first_core, norm[:, half:], norm[:, :half]).astype(
                jnp.bfloat16
            )
        total_ref[:rows, :] = tokens[...].astype(jnp.float32)
        total_ref[rows:, :] = after[:, :width].astype(jnp.float32)

    join_rows(weights, (own_b, own_c, own_x), (other_b, other_c, other_x))
    proj = dot(normed[...], weights[...], NN)
    b_part, c_part, x_part = proj[:, :TILE], proj[:, TILE : 2 * TILE], proj[:, 2 * TILE :]
    b_ref[...] = b_part
    c_ref[...] = c_part
    x_ref[...] = x_part
    mixed[...] = b_part * x_part
    conv = conv_rows(mixed, keeps[:, 0:1], keeps[:, 1:2], taps, ext)[3]
    gated[...] = (c_ref[pl.ds(HALO, ext), :] * conv).astype(jnp.bfloat16)
    here = pl.num_programs(0) // 2

    @pl.when(step < here)
    def _():
        total_ref[...] += dot(gated[...], out_own[...], NN)

    @pl.when(step >= here)
    def _():
        total_ref[...] += dot(gated[...], out_other[...], NN)

    @pl.when(step == pl.num_programs(0) - 1)
    def _():
        resid = total_ref[...]
        hidden[...] = resid
        scale = lax.rsqrt(jnp.mean(resid * resid, axis=-1, keepdims=True) + epsilon)
        norm = resid * scale * small[1:2, :]
        low = chosen(first_core, norm[:, :half], norm[:, half:]).astype(jnp.bfloat16)
        high = chosen(first_core, norm[:, half:], norm[:, :half]).astype(jnp.bfloat16)
        norm_own[:, :half] = low
        norm_own[:, half:] = high
        norm_send[:, :half] = high
        norm_send[:, half:] = low


def channel_specs(width):
    steps = width // TILE
    half = width // 2

    def at(j, info):
        return lax.rem(info[0] * (steps // 2) + j, steps)

    thirds = [
        pl.BlockSpec((half, TILE), lambda j, info, k=k: (0, k * steps + at(j, info)))
        for k in range(3)
    ]
    out_own = pl.BlockSpec((TILE, width), lambda j, info: (jnp.minimum(j, steps // 2 - 1), 0))
    out_other = pl.BlockSpec((TILE, width), lambda j, info: (jnp.maximum(j - steps // 2, 0), 0))
    return steps, at, thirds * 2 + [out_own, out_other]


def fixed(*shape):
    return pl.BlockSpec(shape, lambda j, info: (0,) * len(shape))


def conv_forward(info, tokens, before, after, small, keeps, w_in, w_in_other, w_out, w_out_other):
    rows, width = tokens.shape
    ext = rows + HALO
    steps, at, weight_specs = channel_specs(width)
    column = pl.BlockSpec((ext + HALO, TILE), lambda j, info: (0, at(j, info)))
    return pl.pallas_call(
        forward_kernel,
        out_shape=[jax.ShapeDtypeStruct((ext + HALO, width), jnp.float32)] * 3
        + [jax.ShapeDtypeStruct((ext, width), jnp.float32)]
        + [jax.ShapeDtypeStruct((ext, width), jnp.bfloat16)] * 2,
        grid_spec=pltpu.PrefetchScalarGridSpec(
            num_scalar_prefetch=1,
            grid=(steps,),
            in_specs=[
                fixed(rows, width),
                fixed(HALO, width),
                fixed(*after.shape),
                fixed(*small.shape),
                pl.BlockSpec((small.shape[0], TILE), lambda j, info: (0, at(j, info))),
                fixed(*keeps.shape),
            ]
            + weight_specs,
            out_specs=[column] * 3 + [fixed(ext, width)] * 3,
            scratch_shapes=[
                pltpu.VMEM((ext + HALO, width), jnp.bfloat16),
                pltpu.VMEM((width, 3 * TILE), jnp.bfloat16),
                pltpu.VMEM((ext + HALO, TILE), jnp.float32),
                pltpu.VMEM((ext, TILE), jnp.bfloat16),
                pltpu.VMEM((ext, width), jnp.float32),
            ],
        ),
        name="conv_forward",
        **params(),
    )(
        info,
        tokens,
        before,
        after,
        small,
        small,
        keeps,
        *[w_in] * 3,
        *[w_in_other] * 3,
        w_out,
        w_out_other,
    )


def backward_kernel(
    info,
    tokens,
    hidden,
    cotangent,
    back,
    came,
    small,
    taps,
    keeps,
    b_ref,
    c_ref,
    x_ref,
    own_b,
    own_c,
    own_x,
    other_b,
    other_c,
    other_x,
    out_own,
    out_other,
    input_grad,
    send,
    b_keep,
    out_keep,
    c_keep,
    x_keep,
    vector_keep,
    vectors,
    d_hidden,
    d_branch,
    norm_in,
    d_norm_in,
    weights,
    mixed,
    d_gated,
    along_one,
    along_two,
    d_proj,
):
    step = pl.program_id(0)
    core = info[0]
    first_core = core == 0
    rows, width = tokens.shape
    half = width // 2
    ext = rows + HALO

    def token_norm():
        resid = tokens[...].astype(jnp.float32)
        scale = lax.rsqrt(jnp.mean(resid * resid, axis=-1, keepdims=True) + epsilon)
        return resid * scale, scale

    def back_through(grad, normed, scale, gain):
        inner = grad * gain
        return scale * (inner - normed * jnp.mean(inner * normed, axis=-1, keepdims=True))

    def in_order(own, other):
        return jnp.concatenate(
            [chosen(first_core, own, other), chosen(first_core, other, own)], axis=1
        )

    @pl.when(step == 0)
    def _():
        vectors[...] = jnp.zeros(vectors.shape, jnp.float32)
        grad = in_order(back[:, :half] + came[:, half:], back[:, half:] + came[:, :half])
        resid = hidden[...]
        scale = lax.rsqrt(jnp.mean(resid * resid, axis=-1, keepdims=True) + epsilon)
        normed = resid * scale
        vectors[1:2, :] = jnp.sum(grad[:rows] * normed[:rows], axis=0, keepdims=True)
        result = cotangent[...].astype(jnp.float32) + back_through(
            grad, normed, scale, small[1:2, :]
        )
        d_hidden[...] = result
        d_branch[...] = result.astype(jnp.bfloat16)
        norm_in[...] = (token_norm()[0] * small[0:1, :]).astype(jnp.bfloat16)
        d_norm_in[...] = jnp.zeros(d_norm_in.shape, jnp.float32)

    here = pl.num_programs(0) // 2

    @pl.when(step < here)
    def _():
        d_gated[...] = dot(d_branch[...], out_own[...], NT)

    @pl.when(step >= here)
    def _():
        d_gated[...] = dot(d_branch[...], out_other[...], NT)

    join_rows(weights, (own_b, own_c, own_x), (other_b, other_c, other_x))
    mixed[...] = b_ref[...] * x_ref[...]
    now, one, two, conv = conv_rows(mixed, keeps[:, 0:1], keeps[:, 1:2], taps, ext)
    c_part = c_ref[pl.ds(HALO, ext), :]
    grad = d_gated[...]
    gated = (c_part[:rows] * conv[:rows]).astype(jnp.bfloat16)
    d_conv = grad * c_part
    block = lax.rem(core * here + step, pl.num_programs(0))
    lanes = pl.ds(pl.multiple_of(block * TILE, TILE), TILE)
    for index, view in enumerate((now, one, two)):
        vectors[2 + index : 3 + index, lanes] = jnp.sum(
            d_conv[:rows] * view[:rows], axis=0, keepdims=True
        )
    along_one[...] = keeps[:, 0:1] * d_conv * taps[3:4, :]
    along_two[...] = keeps[:, 1:2] * d_conv * taps[4:5, :]
    d_mixed = (
        taps[2:3, :] * d_conv[:rows] + along_one[pl.ds(1, rows), :] + along_two[pl.ds(2, rows), :]
    )
    d_proj[:, :TILE] = (d_mixed * x_ref[pl.ds(HALO, rows), :]).astype(jnp.bfloat16)
    d_proj[:, TILE : 2 * TILE] = (grad[:rows] * conv[:rows]).astype(jnp.bfloat16)
    d_proj[:, 2 * TILE :] = (d_mixed * b_ref[pl.ds(HALO, rows), :]).astype(jnp.bfloat16)
    out_grad = dot(gated, d_branch[:rows, :], TN)
    in_grad = dot(norm_in[...], d_proj[...], TN)
    d_norm_in[...] += dot(d_proj[...], weights[...], NT)
    groups, per, _ = send.shape
    few = groups // pl.num_programs(0)

    def divide(value, keep, group, at):
        pair = value.reshape(value.shape[0] // (2 * per), 2, per, value.shape[1]).astype(send.dtype)
        for side in range(2):

            @pl.when(core == side)
            def _():
                send[group, :, at] = pair[:, 1 - side]
                keep[...] = pair[:, side]

    every = slice(None)
    for index, keep in enumerate((b_keep, None, c_keep, x_keep)):
        if keep is None:
            divide(out_grad, out_keep, pl.ds(block * few, few), pl.ds(width, width))
        else:
            third = index and index - 1
            at = pl.multiple_of(index * width + block * TILE, TILE)
            divide(in_grad[:, third * TILE : (third + 1) * TILE], keep, every, pl.ds(at, TILE))

    @pl.when(step == pl.num_programs(0) - 1)
    def _():
        final = in_order(d_norm_in[:, :half], d_norm_in[:, half:])
        normed, scale = token_norm()
        vectors[0:1, :] = jnp.sum(final * normed, axis=0, keepdims=True)
        input_grad[...] = (
            d_hidden[:rows, :] + back_through(final, normed, scale, small[0:1, :])
        ).astype(jnp.bfloat16)
        divide(vectors[...].T, vector_keep, every, pl.ds(4 * width, vectors.shape[0]))


def conv_backward(
    info,
    tokens,
    hidden,
    cotangent,
    back,
    came,
    small,
    keeps,
    parts,
    w_in,
    w_in_other,
    w_out,
    w_out_other,
    devices,
):
    rows, width = tokens.shape
    ext = rows + HALO
    steps, at, weight_specs = channel_specs(width)
    column = pl.BlockSpec((ext + HALO, TILE), lambda j, info: (0, at(j, info)))
    per = width // devices
    kind = jnp.bfloat16 if per % 16 == 0 else jnp.float32
    groups = devices // 2
    by_columns = pl.BlockSpec((groups, per, TILE), lambda j, info: (0, 0, at(j, info)))
    by_rows = pl.BlockSpec((groups // steps, per, width), lambda j, info: (at(j, info), 0, 0))
    return pl.pallas_call(
        backward_kernel,
        out_shape=[
            jax.ShapeDtypeStruct((rows, width), jnp.bfloat16),
            jax.ShapeDtypeStruct((groups, per, 4 * width + 128), kind),
        ]
        + [jax.ShapeDtypeStruct((groups, per, width), kind)] * 4
        + [jax.ShapeDtypeStruct((groups, per, 128), kind)],
        grid_spec=pltpu.PrefetchScalarGridSpec(
            num_scalar_prefetch=1,
            grid=(steps,),
            in_specs=[
                fixed(rows, width),
                fixed(ext, width),
                fixed(ext, width),
                fixed(ext, width),
                fixed(ext, width),
                fixed(*small.shape),
                pl.BlockSpec((small.shape[0], TILE), lambda j, info: (0, at(j, info))),
                fixed(*keeps.shape),
            ]
            + [column] * 3
            + weight_specs,
            out_specs=[
                fixed(rows, width),
                fixed(groups, per, 4 * width + 128),
                by_columns,
                by_rows,
                by_columns,
                by_columns,
                fixed(groups, per, 128),
            ],
            scratch_shapes=[
                pltpu.VMEM((128, width), jnp.float32),
                pltpu.VMEM((ext, width), jnp.float32),
                pltpu.VMEM((ext, width), jnp.bfloat16),
                pltpu.VMEM((rows, width), jnp.bfloat16),
                pltpu.VMEM((rows, width), jnp.float32),
                pltpu.VMEM((width, 3 * TILE), jnp.bfloat16),
                pltpu.VMEM((ext + HALO, TILE), jnp.float32),
                pltpu.VMEM((ext, TILE), jnp.float32),
                pltpu.VMEM((ext, TILE), jnp.float32),
                pltpu.VMEM((ext, TILE), jnp.float32),
                pltpu.VMEM((rows, 3 * TILE), jnp.bfloat16),
            ],
        ),
        name="conv_backward",
        **params(),
    )(
        info,
        tokens,
        hidden,
        cotangent,
        back,
        came,
        small,
        small,
        keeps,
        *parts,
        *[w_in] * 3,
        *[w_in_other] * 3,
        w_out,
        w_out_other,
    )


def ffn_kernel(
    real,
    pieces,
    chained,
    joined,
    info,
    n_own,
    n_other,
    g_own,
    g_other,
    gate_own,
    gate_other,
    up_own,
    up_other,
    down_ref,
    *refs,
):
    before, refs = (refs[:2], refs[2:]) if chained else ((), refs)
    act_ref, back_keep, back_send = refs[:3]
    results, (n_all, g_all, back, weights, grads) = refs[3:-5], refs[-5:]
    rows = n_all.shape[0]
    block = real // 2
    tile = down_ref.shape[0]
    places = (
        (pl.ds(0, block), 0, pl.ds(0, block)),
        (pl.ds(real, HALO), 0, pl.ds(block, HALO)),
        (pl.ds(block, block), 1, pl.ds(0, block)),
        (pl.ds(real + HALO, HALO), 1, pl.ds(block, HALO)),
    )

    @pl.when(pl.program_id(0) == 0)
    def _():
        for place, which, source in places:
            n_all[place, :] = (n_own, n_other)[which][source, :]
            g_all[place, :] = (g_own, g_other)[which][source, :]
            if chained:
                back[place, :] = before[which][source, :]
            else:
                back[place, :] = jnp.zeros((place.size, back.shape[1]), jnp.float32)

    join_rows(weights, (gate_own, up_own), (gate_other, up_other))
    size = -(-rows // pieces // 16) * 16
    for start in range(0, rows, size):
        part = pl.ds(start, min(size, rows - start))
        proj = dot(n_all[part, :], weights[...], NN)
        d_act = dot(g_all[part, :], down_ref[...], NT)
        gate = proj[:, :tile]
        up_val = proj[:, tile:]
        sigma = 0.5 * jnp.tanh(0.5 * gate) + 0.5
        silu = gate * sigma
        act_ref[part, :] = (silu * up_val).astype(jnp.bfloat16)
        grads[part, tile:] = (d_act * silu).astype(jnp.bfloat16)
        grads[part, :tile] = (d_act * up_val * (sigma + silu * (1.0 - sigma))).astype(jnp.bfloat16)
        back[part, :] += dot(grads[part, :], weights[...], NT)
    summed = dot(n_all[:real, :], grads[:real, :], TN).astype(jnp.bfloat16)
    if joined:
        (out,) = results
        half = summed.shape[0] // 2

        @pl.when(info[0] == 0)
        def _():
            out[...] = summed

        @pl.when(info[0] != 0)
        def _():
            out[:half, :] = summed[half:, :]
            out[half:, :] = summed[:half, :]

    else:
        for index, grad in enumerate((summed[:, :tile], summed[:, tile:])):
            send, keep = results[2 * index : 2 * index + 2]
            groups, per, columns = send.shape
            pair = grad.reshape(groups, 2, per, columns)
            for value in range(2):

                @pl.when(info[1 + index] == value)
                def _():
                    send[...] = pair[:, 1 - value]
                    keep[...] = pair[:, value]

    @pl.when(pl.program_id(0) == pl.num_programs(0) - 1)
    def _():
        for place, which, source in places:
            (back_keep, back_send)[which][source, :] = back[place, :]


def ffn_part(info, acts, weights, down, before, first, count, pers):
    ext, width = acts[0].shape
    rows, real = 2 * ext, 2 * (ext - HALO)
    half = width // 2
    blocks = down.shape[0] // TILE
    own = pl.BlockSpec((half, TILE), lambda j, info: (0, info[0] * blocks + first + j))
    other = pl.BlockSpec((half, TILE), lambda j, info: (0, first + j))
    shapes = [jax.ShapeDtypeStruct((rows, count * TILE), jnp.bfloat16)]
    specs = [pl.BlockSpec((rows, TILE), lambda j, info: (0, j))]
    for _ in range(2):
        shapes.append(jax.ShapeDtypeStruct((ext, width), jnp.float32))
        specs.append(fixed(ext, width))
    for per in pers:
        for _ in range(2):
            groups = width // (2 * per)
            shapes.append(jax.ShapeDtypeStruct((groups, per, count * TILE), jnp.bfloat16))
            specs.append(pl.BlockSpec((groups, per, TILE), lambda j, info: (0, 0, j)))
    if not pers:
        shapes.append(jax.ShapeDtypeStruct((width, 2 * count * TILE), jnp.bfloat16))
        specs.append(pl.BlockSpec((width, 2 * TILE), lambda j, info: (0, j)))
    return pl.pallas_call(
        functools.partial(ffn_kernel, real, 2, bool(before), not pers),
        out_shape=shapes,
        grid_spec=pltpu.PrefetchScalarGridSpec(
            num_scalar_prefetch=1,
            grid=(count,),
            in_specs=[fixed(ext, width)] * 4
            + [own, other, own, other]
            + [pl.BlockSpec((TILE, width), lambda j, info: (first + j, 0))]
            + [fixed(ext, width)] * len(before),
            out_specs=specs,
            scratch_shapes=[
                pltpu.VMEM((rows, width), jnp.bfloat16),
                pltpu.VMEM((rows, width), jnp.bfloat16),
                pltpu.VMEM((rows, width), jnp.float32),
                pltpu.VMEM((width, 2 * TILE), jnp.bfloat16),
                pltpu.VMEM((rows, 2 * TILE), jnp.bfloat16),
            ],
        ),
        name="ffn",
        **params(),
    )(info, *acts, *weights, down, *before)


def down_kernel(
    info,
    act_one,
    act_two,
    g_own,
    g_other,
    down_ref,
    out_keep,
    out_send,
    low_send,
    low_keep,
    high_send,
    high_keep,
    rhs,
    grad,
):
    step = pl.program_id(0)
    block = out_keep.shape[0]
    real = 2 * block
    cut = act_one.shape[1]
    rhs[:block, :] = g_own[:block, :]
    rhs[block:, :] = g_other[:block, :]
    result = dot(act_one[:real, :], down_ref[:cut, :], NN) + dot(
        act_two[:real, :], down_ref[cut:, :], NN
    )
    out_keep[...] = result[:block]
    out_send[...] = result[block:]
    grad[:cut, :] = dot(act_one[:real, :], rhs[...], TN).astype(grad.dtype)
    grad[cut:, :] = dot(act_two[:real, :], rhs[...], TN).astype(grad.dtype)
    here = pl.num_programs(0) // 2
    outs = ((step < here, low_send, low_keep, info[1]), (step >= here, high_send, high_keep, info[2]))
    for now, send, keep, mine in outs:
        groups, per, _ = send.shape
        for value in range(2):

            @pl.when(jnp.logical_and(now, mine == value))
            def _():
                for group in range(groups):
                    start = 2 * group * per
                    send[group] = grad[pl.ds(start + (1 - value) * per, per), :]
                    keep[group] = grad[pl.ds(start + value * per, per), :]


def down_part(info, act_one, act_two, g_own, g_other, down, pers, block):
    hidden, width = down.shape
    steps = width // TILE
    here = steps // 2
    kind = jnp.bfloat16 if min(pers) % 16 == 0 else jnp.float32
    tile = pl.BlockSpec((block, TILE), lambda j, info: (0, j))
    shapes = [jax.ShapeDtypeStruct((block, width), jnp.float32)] * 2
    specs = [tile] * 2
    for index, per in enumerate(pers):
        groups = hidden // (2 * per)
        for _ in range(2):
            shapes.append(jax.ShapeDtypeStruct((groups, per, width // 2), kind))
            if index == 0:
                specs.append(
                    pl.BlockSpec(
                        (groups, per, TILE), lambda j, info: (0, 0, jnp.minimum(j, here - 1))
                    )
                )
            else:
                specs.append(
                    pl.BlockSpec((groups, per, TILE), lambda j, info: (0, 0, jnp.maximum(j - here, 0)))
                )
    ext = g_own.shape[0]
    return pl.pallas_call(
        down_kernel,
        out_shape=shapes,
        grid_spec=pltpu.PrefetchScalarGridSpec(
            num_scalar_prefetch=1,
            grid=(steps,),
            in_specs=[
                fixed(*act_one.shape),
                fixed(*act_two.shape),
                pl.BlockSpec((ext, TILE), lambda j, info: (0, j)),
                pl.BlockSpec((ext, TILE), lambda j, info: (0, j)),
                pl.BlockSpec((hidden, TILE), lambda j, info: (0, j)),
            ],
            out_specs=specs,
            scratch_shapes=[
                pltpu.VMEM((2 * block, TILE), jnp.bfloat16),
                pltpu.VMEM((hidden, TILE), kind),
            ],
        ),
        name="down",
        **params(),
    )(info, act_one, act_two, g_own, g_other, down)


def combine_kernel(plan, info, *refs):
    refs = list(refs)
    inputs = [[[refs.pop(0) for _ in range(count)] for count in counts] for counts in plan]
    for members, out in zip(inputs, refs):
        edge = 0
        for terms in members:
            size = terms[0].shape[-1]
            value = terms[0][...].astype(jnp.float32)
            for term in terms[1:]:
                value = value + term[...].astype(jnp.float32)
            out[..., edge : edge + size] = value.reshape(out.shape[:-1] + (size,)).astype(out.dtype)
            edge += size


def combine(info, slots, jobs, flip=False):
    plan, arrays, specs, shapes, out_specs = [], [], [], [], []
    lefts = []
    for bit, members in jobs:
        common = members[0][0][1]
        for terms in members:
            for _, names, _, _ in terms:
                common = [name for name in common if name in names]
        lefts.append([name for name in common if name != bit])
    gridded = all(lefts)
    for (bit, members), left in zip(jobs, lefts):
        for terms in members:
            for array, names, block, size in terms:
                rows = array.size // array.shape[-1] >> len(names)
                arrays.append(array.reshape([2] * len(names) + [rows, array.shape[-1]]))
                shape, picks = [], []
                for name in names:
                    if name == bit:
                        shape.append(None)
                        picks.append(("other", slots[name]))
                    elif name not in left:
                        shape.append(None)
                        picks.append(("mine", slots[name]))
                    elif gridded and name == left[0]:
                        shape.append(None)
                        picks.append(("step", 0))
                    else:
                        shape.append(2)
                        picks.append(("all", 0))

                def index_map(j, info, picks=picks, block=block):
                    where = []
                    for kind, slot in picks:
                        if kind == "all":
                            where.append(0)
                        elif kind == "step":
                            where.append(lax.rem(j + info[0], 2) if flip else j)
                        else:
                            where.append(info[slot] if kind == "mine" else 1 - info[slot])
                    return (*where, 0, block)

                specs.append(pl.BlockSpec((*shape, rows, size), index_map))
        width = sum(terms[0][3] for terms in members)
        kind = jnp.bfloat16 if rows % 16 == 0 else jnp.float32
        outer = 1 << len(left)
        shapes.append(jax.ShapeDtypeStruct((outer, rows, width), kind))
        inner = outer // 2 if gridded else outer
        out_specs.append(pl.BlockSpec((inner, rows, width), lambda j, info: (j, 0, 0)))
        plan.append([len(terms) for terms in members])
    results = pl.pallas_call(
        functools.partial(combine_kernel, plan),
        out_shape=shapes,
        grid_spec=pltpu.PrefetchScalarGridSpec(
            num_scalar_prefetch=1,
            grid=(2 if gridded else 1,),
            in_specs=specs,
            out_specs=out_specs,
        ),
        name="combine",
        **params(),
    )(info, *arrays)
    return list(zip(results, lefts))


def finish_kernel(counts, tiles, info, *refs):
    *inputs, mine, send, scratch = refs
    place = 0
    for count in counts:
        value = inputs[0][...].astype(jnp.float32)
        for term in inputs[1:count]:
            value = value + term[...].astype(jnp.float32)
        inputs = inputs[count:]
        for tile in range(value.shape[1] // TILE):
            start = tiles[place] * TILE
            scratch[:, start : start + TILE] = value[:, tile * TILE : (tile + 1) * TILE]
            place += 1
    rows = mine.shape[0]
    for side, out in ((info[0], mine), (1 - info[0], send)):
        out[...] = scratch[pl.ds(pl.multiple_of(side * rows, rows), rows), :]


def picked(slots, terms):
    arrays, specs = [], []
    for array, names, block, size in terms:
        rows = array.size // array.shape[-1] >> len(names)
        arrays.append(array.reshape([2] * len(names) + [rows, array.shape[-1]]))
        specs.append(
            pl.BlockSpec(
                (*[None] * len(names), rows, size),
                lambda j, info, names=names, block=block: (
                    *[info[slots[name]] for name in names],
                    0,
                    block,
                ),
            )
        )
    return arrays, specs


def settle_kernel(plan, info, *refs):
    refs = list(refs)
    inputs = [[[refs.pop(0) for _ in range(count)] for count in counts] for counts, _ in plan]
    for members, (_, kinds) in zip(inputs, plan):
        outs = [refs.pop(0) for _ in kinds]
        edge = 0
        for terms in members:
            size = terms[0].shape[-1]
            value = terms[0][...].astype(jnp.float32)
            for term in terms[1:]:
                value = value + term[...].astype(jnp.float32)
            for out in outs:
                out[:, edge : edge + size] = value.astype(out.dtype)
            edge += size


def settle(info, slots, groups):
    arrays, specs, shapes, plan = [], [], [], []
    for members, kinds in groups:
        for terms in members:
            views, view_specs = picked(slots, terms)
            arrays += views
            specs += view_specs
        rows = views[0].shape[-2]
        width = sum(terms[0][3] for terms in members)
        shapes += [jax.ShapeDtypeStruct((rows, width), kind) for kind in kinds]
        plan.append(([len(terms) for terms in members], kinds))
    return pl.pallas_call(
        functools.partial(settle_kernel, plan),
        out_shape=shapes,
        grid_spec=pltpu.PrefetchScalarGridSpec(
            num_scalar_prefetch=1,
            grid=(1,),
            in_specs=specs,
            out_specs=[fixed(*shape.shape) for shape in shapes],
        ),
        name="settle",
        **params(),
    )(info, *arrays)


def finish(info, slots, members, tiles):
    columns = len(tiles) * TILE
    arrays, specs = [], []
    for terms in members:
        views, view_specs = picked(slots, terms)
        rows = views[0].shape[-2]
        arrays += views
        specs += view_specs
    return pl.pallas_call(
        functools.partial(finish_kernel, [len(terms) for terms in members], tiles),
        out_shape=[jax.ShapeDtypeStruct((rows // 2, columns), jnp.float32)] * 2,
        grid_spec=pltpu.PrefetchScalarGridSpec(
            num_scalar_prefetch=1,
            grid=(1,),
            in_specs=specs,
            out_specs=[fixed(rows // 2, columns)] * 2,
            scratch_shapes=[pltpu.VMEM((rows, columns), jnp.float32)],
        ),
        name="finish",
        **params(),
    )(info, *arrays)


def local(
    tokens,
    cotangent,
    doc_lengths,
    norm_gain,
    in_weight,
    conv_taps,
    out_weight,
    ffn_gain,
    gate_weight,
    up_weight,
    down_weight,
):
    rows, width = tokens.shape
    hidden = down_weight.shape[0]
    chips = lax.axis_size("seq")
    top = chips.bit_length() - 2
    lower = list(range(top))
    bits = list(range(top, -1, -1))
    chip = lax.axis_index("seq")
    core = lax.axis_index("wa")
    coords = {bit: (chip >> bit) & 1 for bit in range(top + 1)}
    turned = dict(coords)
    turned[top] = coords[top] ^ core
    ordering = lax.optimization_barrier

    def after(value, *gates):
        return ordering((value, gates))[0]

    def ordered(low, high):
        return jnp.where(core == 0, low, high)

    def both(own, other, axis):
        return ordered(
            jnp.concatenate([own, other], axis=axis), jnp.concatenate([other, own], axis=axis)
        )

    w_in_other = partner(in_weight)
    small = jnp.concatenate([norm_gain[None], ffn_gain[None], conv_taps.T], axis=0)
    small = jnp.pad(small, ((0, 3), (0, 0)))
    small = both(small, partner(small), 1).astype(jnp.float32)
    before_rows = shifted(tokens[rows - HALO :], 1)
    after_rows = shifted(jnp.concatenate([tokens[:HALO], cotangent[:HALO]], axis=1), -1)
    w_out_other = partner(out_weight)
    gate_late, up_late = after((gate_weight, up_weight), before_rows, after_rows, w_out_other)
    gate_other = partner(lax.dynamic_slice_in_dim(gate_late, (1 - core) * hidden, hidden, 1))
    up_other = partner(lax.dynamic_slice_in_dim(up_late, (1 - core) * hidden, hidden, 1))
    cot_own = jnp.concatenate([cotangent, after_rows[:, width:]], axis=0)
    cot_other = partner(cot_own)

    place = lax.axis_index(AXES) * rows + jnp.arange(rows + HALO, dtype=jnp.int32)
    starts = jnp.cumsum(doc_lengths) - doc_lengths
    first = jnp.any(place[:, None] == starts[None, :], axis=1)
    before = jnp.any((place - 1)[:, None] == starts[None, :], axis=1)
    keep_one = jnp.where(first, 0.0, 1.0)
    keep_two = jnp.where(jnp.logical_or(first, before), 0.0, 1.0)
    keeps = jnp.stack([keep_one, keep_two], axis=1).astype(jnp.float32)
    info = [core] + [coords[bit] for bit in lower] + [coords[top], turned[top]]
    info = jnp.stack(info).astype(jnp.int32)

    *parts, hidden_res, norm_own, norm_send = conv_forward(
        info,
        tokens,
        before_rows,
        after_rows,
        small,
        keeps,
        in_weight,
        w_in_other,
        out_weight,
        w_out_other,
    )
    norm_other = partner(norm_send)
    per_chip = width // chips
    pers = (per_chip << lower[0], per_chip << lower[1])
    tiles = hidden // TILE
    split = tiles * 5 // 9
    counts = (split, tiles - split)
    orders = (lower, [lower[1], lower[0]] + lower[2:])

    acts = (norm_own, norm_other, cot_own, cot_other)
    weights = (gate_weight, gate_other, up_weight, up_other)
    one = ffn_part(info, acts, weights, down_weight, (), 0, counts[0], pers)
    one_x = across(one[3], orders[0][0])
    one_y = across(one[5], orders[1][0])
    two = ffn_part(info, acts, weights, down_weight, one[1:3], split, counts[1], ())
    two, one_x, one_y = ordering((two, one_x, one_y))
    came = partner(two[2])

    groups = [
        [low + (level << (top - 1)) for level in range(4)] for low in range(1 << (top - 1))
    ]
    quarter = lax.psum_scatter(
        two[3], "seq", scatter_dimension=0, axis_index_groups=groups, tiled=True
    )

    slots = {bit: 1 + bit for bit in bits}
    turned_slots = dict(slots)
    turned_slots[top] = 2 + top

    def plain(array, names):
        return (array, names, 0, array.shape[-1])

    def gated(streams, *gates):
        held = after([terms[-1][0] for terms in streams], gates)
        return [
            terms[:-1] + [(array, *terms[-1][1:])] for terms, array in zip(streams, held)
        ]

    def without(names, *taken):
        return [name for name in names if name not in taken]

    def send_on(streams, names, use=slots):
        results = combine(info, use, streams)
        return [send for send, _ in results], [
            (across(send, bit), left) for (bit, _), (send, left) in zip(streams, results)
        ]

    def upper_sum(value):
        value = value.reshape(-1, value.shape[-1])
        return lax.psum_scatter(
            value, "seq", scatter_dimension=0, axis_index_groups=groups, tiled=True
        )

    one_terms = [
        [plain(keep, without(bits, order[0])), plain(got, without(bits, order[0]))]
        for keep, got, order in ((one[4], one_x, orders[0]), (one[6], one_y, orders[1]))
    ]
    one_sent, one_got = send_on(
        [(order[1], [terms]) for terms, order in zip(one_terms, orders)], bits, turned_slots
    )
    down_pers = [2 * hidden // chips << bit for bit in (lower[0], lower[1])]
    out_keep, out_send, *down_halves = down_part(
        info, one[0], after(two[0], one_sent), cot_own, cot_other, down_weight, down_pers, rows
    )
    one_got = [got for got, _ in one_got]
    came, one_got, out_send, down_halves = ordering((came, one_got, out_send, down_halves))

    down_x = across(down_halves[0], orders[0][0])
    down_y = across(down_halves[2], orders[1][0])
    out_came = partner(out_send)

    def side_by_side(streams, order, use=slots):
        sent = None
        for bit in order:
            sent, ((got, left),) = send_on([(bit, streams)], None, use)
            edge, members = 0, []
            for terms in streams:
                size = terms[0][3]
                members.append(terms + [(got, left, edge, size)])
                edge += size
            for terms in members:
                array, left, edge, size = terms[-1]
                if edge % size:
                    array, edge = array[..., edge : edge + size], 0
                terms[-1] = (array, left, edge // size, size)
            streams = members
        return sent, streams

    one_streams = [
        terms + [plain(got, without(bits, *order[:2]))]
        for terms, got, order in zip(one_terms, one_got, orders)
    ]
    _, one_streams = side_by_side(one_streams, lower[2 : top - 1], turned_slots)
    ((one_all, _),) = combine(info, turned_slots, [(None, one_streams)], flip=True)
    came, one_all = ordering((came, one_all))
    one_done = upper_sum(one_all)
    input_grad, conv_send, *conv_keeps = conv_backward(
        info,
        tokens,
        hidden_res,
        cot_own,
        two[1],
        came,
        small,
        keeps,
        parts,
        in_weight,
        w_in_other,
        out_weight,
        w_out_other,
        2 * chips,
    )
    conv_send, conv_keeps, down_x, down_y = ordering((conv_send, conv_keeps, down_x, down_y))

    conv_came = partner(conv_send)
    down_bits = bits[1:]
    down_terms = [
        [plain(keep, without(down_bits, order[0])), plain(got, without(down_bits, order[0]))]
        for keep, got, order in (
            (down_halves[1], down_x, orders[0]),
            (down_halves[3], down_y, orders[1]),
        )
    ]
    down_sent, down_got = send_on(
        [(order[1], [terms]) for terms, order in zip(down_terms, orders)], down_bits
    )
    down_got = [got for got, _ in down_got]
    conv_came, down_got = ordering((conv_came, down_got))

    conv_members = [
        [
            [plain(conv_keeps[member], bits), (conv_came, bits, member * width // size, size)]
            for member, size in members
        ]
        for members in (((0, width), (1, width)), ((2, width), (3, width), (4, 128)))
    ]
    conv_sent, conv_got = send_on(
        [(order[0], members) for members, order in zip(conv_members, orders)], bits
    )
    conv_got = [got for got, _ in conv_got]

    block_out = (hidden_res[:rows] + out_keep + out_came).astype(jnp.bfloat16)
    down_streams = [
        terms + [plain(got, without(down_bits, *order[:2]))]
        for terms, got, order in zip(down_terms, down_got, orders)
    ]
    down_sent, down_streams = side_by_side(down_streams, lower[2:])
    conv_got = after(conv_got, block_out)

    for index, (members, order) in enumerate(zip(conv_members, orders)):
        edge = 0
        for terms in members:
            size = terms[0][3]
            terms.append((conv_got[index], without(bits, order[0]), edge // size, size))
            edge += size
    conv_sent, conv_two = send_on(
        [(order[1], members) for members, order in zip(conv_members, orders)], bits
    )
    quarter = after(quarter, conv_sent)
    down_streams = gated(down_streams, conv_sent)
    part, down_last = settle(info, slots, [(down_streams, (jnp.float32, jnp.bfloat16))])
    pairs = [
        (source * 2 + side, (source ^ (1 << top)) * 2 + side)
        for source in range(chips)
        for side in range(2)
        if (source >> top) & 1 != side
    ]
    down_far = lax.ppermute(down_last, AXES, pairs)
    edge = counts[1] * TILE
    two_terms = [[(quarter, bits[2:], block, edge)] for block in range(2)]
    two_sent, two_got = send_on(
        [(order[0], [terms]) for terms, order in zip(two_terms, orders)], bits[2:]
    )
    two_got = [got for got, _ in two_got]

    conv_two, down_far = ordering(([got for got, _ in conv_two], down_far))
    part = part + down_far.astype(jnp.float32)
    part = part.reshape(2, -1, width)
    down_out = jnp.where(
        coords[top] == core, take(part, core, 0), partner(take(part, 1 - core, 0))
    )

    conv_streams = []
    for members, got, order in zip(conv_members, conv_two, orders):
        edge = 0
        for terms in members:
            size = terms[0][3]
            conv_streams.append(terms + [(got, without(bits, *order[:2]), edge // size, size)])
            edge += size
    _, conv_streams = side_by_side(conv_streams, lower[2 : top - 1])
    ((conv_all, _),) = combine(info, slots, [(None, conv_streams)])
    two_got = after(two_got, conv_all)
    two_terms = [
        terms + [plain(got, without(bits[2:], order[0]))]
        for terms, got, order in zip(two_terms, two_got, orders)
    ]
    two_sent, two_got = send_on(
        [(order[1], [terms]) for terms, order in zip(two_terms, orders)], bits[2:]
    )
    two_streams = [terms + [plain(*got)] for terms, got in zip(two_terms, two_got)]
    _, two_streams = side_by_side(two_streams, lower[2 : top - 1])

    conv_done = upper_sum(conv_all)
    two_streams = gated(two_streams, conv_all)
    b_out, out_out, c_out, x_out, vectors = (
        [(conv_done, [], member * width // size, size)]
        for member, size in enumerate([width] * 4 + [128])
    )
    in_out, out_out, vectors = settle(
        info,
        slots,
        [
            ([b_out, c_out, x_out], (jnp.float32,)),
            ([out_out], (jnp.float32,)),
            ([vectors], (jnp.float32,)),
        ],
    )

    gate_tiles = [tile for tile in range(counts[0])] + [tiles + tile for tile in range(counts[0])]
    for tile in range(counts[1]):
        gate_tiles += [counts[0] + tile, tiles + counts[0] + tile]
    two_streams = gated(two_streams, conv_sent)
    kept, send = finish(info, slots, [[plain(one_done, [])]] + two_streams, gate_tiles)
    other = partner(send)
    gate_out = both(kept[:, :hidden], other[:, :hidden], 1)
    up_out = both(kept[:, hidden:], other[:, hidden:], 1)
    return (
        block_out,
        input_grad,
        vectors[:, 0],
        in_out,
        vectors[:, 2:5],
        out_out,
        vectors[:, 1],
        gate_out,
        up_out,
        down_out,
    )


def solution(mesh):
    placed = (
        P(AXES, None),
        P(AXES, None),
        P(),
        P("wa"),
        P("wa", None),
        P("wa", None),
        P("wa", None),
        P("wa"),
        P("wa", None),
        P("wa", None),
        P("wa", None),
    )
    return jax.shard_map(
        local,
        mesh=mesh,
        in_specs=placed,
        out_specs=(
            P(AXES, None),
            P(AXES, None),
            P(AXES),
            P(AXES, None),
            P(AXES, None),
            P(AXES, None),
            P(AXES),
            P(AXES, None),
            P(AXES, None),
            P(AXES, None),
        ),
        check_vma=False,
    )
```

profile of v0, /device:TPU:0, one launch (start us, length us, event | category | flops | bytes accessed | tf_op | source)
XLA Modules:
  0.0 309.0 jit_solution(6536439414319277043)
XLA Ops:
  10.7 3.0 collective-permute-start
  14.6 3.8 %constant_dynamic-slice_fusion.1 = bf16[512,2304]{1,0:T(8,128)(2,1)} fusion(bf16[512,4608]{1,0:T(8,128)(2,1)} %gate_own.3, s32[]{:T(128)S(6)} %select_n.72), kind=kLoop, calls=%fused_computation.26 | loop fusion | bytes 4718596 | tf_op jit(solution)/shard_map/dynamic_slice | solution.py:910
  20.1 2.7 collective-permute-start.8
  31.1 14.0 %conv_forward.1 = (f32[544,1024]{1,0:T(8,128)}, f32[544,1024]{1,0:T(8,128)}, f32[544,1024]{1,0:T(8,128)}, f32[528,1024]{1,0:T(8,128)}, bf16[528,1024]{1,0:T(8,128)(2,1)}, /*index=5*/bf16[528,1024]{1,0:T(8,128)(2,1)}) custom-call(s32[6]{0:T(128)} %stack.32.info, bf16[512,1024]{1,0:T(8,128)(2,1)} %tokens.3, bf16[16,1024]{1,0:T(8,128)(2,1)} %copy-done.26, ...), custom_call_target="tpu_custom_call" | custom-call | flops 1000 | bytes 1000 | tf_op jit(solution)/shard_map/conv_forward/pallas_call | solution.py:191
  45.3 2.7 collective-permute-done.5.n_other
  49.0 31.4 %ffn.2 = (bf16[1056,1280]{1,0:T(8,128)(2,1)}, f32[528,1024]{1,0:T(8,128)}, f32[528,1024]{1,0:T(8,128)}, bf16[8,64,1280]{2,1,0:T(8,128)(2,1)}, bf16[8,64,1280]{2,...) custom-call(s32[6]{0:T(128)} %stack.32.info, ...), custom_call_target="tpu_custom_call" | custom-call | flops 1000 | bytes 1000 | tf_op jit(solution)/shard_map/ffn/pallas_call | solution.py:574
  80.4 2.8 collective-permute-start.9
  83.2 2.3 collective-permute-start.10
  85.5 27.9 %ffn.3 = (bf16[1056,1024]{1,0:T(8,128)(2,1)}, f32[528,1024]{1,0:T(8,128)}, f32[528,1024]{1,0:T(8,128)}, bf16[1024,2048]{1,0:T(8,128)(2,1)}) custom-call(s32[6]{0:T(128)} %stack.32.info, bf16[528,1024]{1,0:T(8,128)(2,1)} %get-tuple-element.104.n_own, bf16[528,1024]{1,0:T(8,128)(2,1)} %copy-done.12, bf16[528,1024]{1,0:T(8,128)(2,1)} %copy-done.3, ...), custom_call_target="tpu_custom_call" | custom-call | flops 1000 | bytes 1000 | tf_op jit(solution)/shard_map/ffn/pallas_call | solution.py:574
  115.6 3.3 %combine.9 = (bf16[4,64,1280]{2,1,0:T(8,128)(2,1)}, bf16[4,64,1280]{2,1,0:T(8,128)(2,1)}) custom-call(s32[6]{0:T(128)} %stack.32.info, bf16[2,2,2,64,1280]{4,3,2,1,0:T(8,128)(2,1)} %bitcast.81, bf16[2,2,2,64,1280]{4,3,2,1,0:T(8,128)(2,1)} %bitcast.85, bf16[2,2,2,64,1280]{4,3,2,1,0:T(8,128)(2,1)} %bitcast.83, bf16[2,2,2,64,1280]{4,3,2,1,0:T(8,128)(2,1)} %bitcast.87), custom_call_target="tpu_custom_call" | custom-call | flops 1000 | bytes 1000 | tf_op jit(solution)/shard_map/combine/pallas_call | solution.py:751
  121.8 17.0 %down.1 = (f32[512,1024]{1,0:T(8,128)}, f32[512,1024]{1,0:T(8,128)}, bf16[4,288,512]{2,1,0:T(8,128)(2,1)}, bf16[4,288,512]{2,1,0:T(8,128)(2,1)}, bf16[2,576,512]...) custom-call(s32[6]{0:T(128)} %stack.32.info, bf16[1056,1280]{1,0:T(8,128)(2,1)} %get-tuple-element.108.act_one, ...), custom_call_target="tpu_custom_call" | custom-call | flops 1000 | bytes 1000 | tf_op jit(solution)/shard_map/down/pallas_call | solution.py:664
  140.4 3.9 %combine.10 = bf16[4,64,2560]{2,1,0:T(8,128)(2,1)} custom-call(s32[6]{0:T(128)} %stack.32.info, bf16[2,2,2,64,1280]{4,3,2,1,0:T(8,128)(2,1)} %bitcast.82, bf16[2,2,2,64,1280]{4,3,2,1,0:T(8,128)(2,1)} %bitcast.86, bf16[2,2,64,1280]{3,2,1,0:T(8,128)(2,1)} %bitcast.102, bf16[2,2,2,64,1280]{4,3,2,1,0:T(8,128)(2,1)} %bitcast.84, ...), custom_call_target="tpu_custom_call" | custom-call | flops 1000 | bytes 1000 | tf_op jit(solution)/shard_map/combine/pallas_call | solution.py:751
  144.3 27.1 %conv_backward.1 = (bf16[512,1024]{1,0:T(8,128)(2,1)}, bf16[16,32,4224]{2,1,0:T(8,128)(2,1)}, bf16[16,32,1024]{2,1,0:T(8,128)(2,1)}, bf16[16,32,1024]{2,1,0:T(8,...) custom-call(s32[6]{0:T(128)} %stack.32.info, ...), custom_call_target="tpu_custom_call" | custom-call | flops 1000 | bytes 1000 | tf_op jit(solution)/shard_map/conv_backward/pallas_call | solution.py:402
  172.8 3.2 %combine.11 = (bf16[2,288,512]{2,1,0:T(8,128)(2,1)}, bf16[2,288,512]{2,1,0:T(8,128)(2,1)}) custom-call(s32[6]{0:T(128)} %stack.32.info, bf16[2,2,288,512]{3,2,1,0:T(8,128)(2,1)} %bitcast.56, bf16[2,2,288,512]{3,2,1,0:T(8,128)(2,1)} %bitcast.62, bf16[2,2,288,512]{3,2,1,0:T(8,128)(2,1)} %bitcast.59, bf16[2,2,288,512]{3,2,1,0:T(8,128)(2,1)} %bitcast.65), custom_call_target="tpu_custom_call" | custom-call | flops 1000 | bytes 1000 | tf_op jit(solution)/shard_map/combine/pallas_call | solution.py:751
  178.6 12.3 %collective-permute-done.18.refs_2_ = bf16[2,288,512]{2,1,0:T(8,128)(2,1)S(1)} collective-permute-done((bf16[2,288,512]{2,1,0:T(8,128)(2,1)}, bf16[2,288,512]{2,1,0:T(8,128)(2,1)S(1)}, u32[]{:S(2)}, u32[]{:S(2)}) %collective-permute-start.18) | collective-permute-done | bytes 589856 | tf_op jit(solution)/shard_map/ppermute | solution.py:33
  192.3 4.4 %combine.12 = (bf16[8,32,2048]{2,1,0:T(8,128)(2,1)}, bf16[8,32,2176]{2,1,0:T(8,128)(2,1)}) custom-call(s32[6]{0:T(128)} %stack.32.info, bf16[2,2,2,2,32,1024]{5,4,3,2,1,0:T(8,128)(2,1)} %bitcast.68, bf16[2,2,2,2,32,4224]{5,4,3,2,1,0:T(8,128)(2,1)} %bitcast.19.refs_1_.refs_3_.refs_5_.refs_7_.refs_9_.refs_4_.refs_10_.refs_13_.refs_17_, ...), custom_call_target="tpu_custom_call" | custom-call | flops 1000 | bytes 1000 | tf_op jit(solution)/shard_map/combine/pallas_call | solution.py:751
  198.1 3.1 %combine.14 = bf16[1,288,1024]{2,1,0:T(8,128)(2,1)} custom-call(s32[6]{0:T(128)} %stack.32.info, bf16[2,2,288,512]{3,2,1,0:T(8,128)(2,1)} %bitcast.57, bf16[2,2,288,512]{3,2,1,0:T(8,128)(2,1)} %bitcast.63, bf16[2,288,512]{2,1,0:T(8,128)(2,1)} %copy-done.13, bf16[2,2,288,512]{3,2,1,0:T(8,128)(2,1)} %bitcast.60, bf16[2,2,288,512]{3,2,1,0:T(8,128)(2,1)} %bitcast.66, ...), custom_call_target="tpu_custom_call" | custom-call | flops 1000 | bytes 1000 | tf_op jit(solution)/shard_map/combine/pallas_call | solution.py:751
  201.2 2.9 collective-permute-start.24
  204.2 3.7 %add_convert_fusion = bf16[512,1024]{1,0:T(8,128)(2,1)} fusion(f32[512,1024]{1,0:T(8,128)} %collective-permute-done.14, f32[512,1024]{1,0:T(8,128)} %get-tuple-element.125, f32[528,1024]{1,0:T(8,128)S(1)} %copy-done.8), kind=kLoop, calls=%fused_computation | loop fusion | flops 1572864 | bytes 7340032 | tf_op jit(solution)/shard_map/convert_element_type | solution.py:1077
  207.9 12.6 %collective-permute-done.20 = bf16[8,32,2048]{2,1,0:T(8,128)(2,1)S(1)} collective-permute-done((bf16[8,32,2048]{2,1,0:T(8,128)(2,1)}, bf16[8,32,2048]{2,1,0:T(8,128)(2,1)S(1)}, u32[]{:S(2)}, u32[]{:S(2)}) %collective-permute-start.20) | collective-permute-done | bytes 1048608 | tf_op jit(solution)/shard_map/ppermute | solution.py:33
  222.7 3.7 %combine.13 = (bf16[4,32,2048]{2,1,0:T(8,128)(2,1)}, bf16[4,32,2176]{2,1,0:T(8,128)(2,1)}) custom-call(s32[6]{0:T(128)} %stack.32.info, bf16[2,2,2,2,32,1024]{5,4,3,2,1,0:T(8,128)(2,1)} %bitcast.69, bf16[2,2,2,2,32,4224]{5,4,3,2,1,0:T(8,128)(2,1)} %bitcast.19.refs_1_.refs_3_.refs_5_.refs_7_.refs_9_.refs_4_.refs_10_.refs_13_.refs_17_, ...), custom_call_target="tpu_custom_call" | custom-call | flops 1000 | bytes 1000 | tf_op jit(solution)/shard_map/combine/pallas_call | solution.py:751
  226.5 8.5 %collective-permute-done.24 = bf16[1,288,1024]{2,1,0:T(8,128)(2,1)S(1)} collective-permute-done((bf16[1,288,1024]{2,1,0:T(8,128)(2,1)}, bf16[1,288,1024]{2,1,0:T(8,128)(2,1)S(1)}, u32[]{:S(2)}, u32[]{:S(2)}) %collective-permute-start.24) | collective-permute-done | bytes 589856 | tf_op jit(solution)/shard_map/ppermute | solution.py:33
  235.8 4.0 %settle.2 = (f32[288,1024]{1,0:T(8,128)}, bf16[288,1024]{1,0:T(8,128)(2,1)}) custom-call(s32[6]{0:T(128)} %stack.32.info, bf16[2,2,288,512]{3,2,1,0:T(8,128)(2,1)} %bitcast.58, bf16[2,2,288,512]{3,2,1,0:T(8,128)(2,1)} %bitcast.64, bf16[2,288,512]{2,1,0:T(8,128)(2,1)} %copy-done.13, bf16[288,1024]{1,0:T(8,128)(2,1)} %bitcast.95, ...), custom_call_target="tpu_custom_call" | custom-call | flops 1000 | bytes 1000 | tf_op jit(solution)/shard_map/settle/pallas_call | solution.py:828
  242.7 2.5 combine.16
  247.7 9.3 %collective-permute-done.22 = bf16[4,32,2048]{2,1,0:T(8,128)(2,1)S(1)} collective-permute-done((bf16[4,32,2048]{2,1,0:T(8,128)(2,1)S(1)}, bf16[4,32,2048]{2,1,0:T(8,128)(2,1)S(1)}, u32[]{:S(2)}, u32[]{:S(2)}) %collective-permute-start.22) | collective-permute-done | bytes 524320 | tf_op jit(solution)/shard_map/ppermute | solution.py:33
  257.0 2.0 collective-permute-done.25
  259.0 4.2 %combine.15 = bf16[4,32,4224]{2,1,0:T(8,128)(2,1)} custom-call(s32[6]{0:T(128)} %stack.32.info, bf16[2,2,2,2,32,1024]{5,4,3,2,1,0:T(8,128)(2,1)} %bitcast.70, bf16[2,2,2,2,32,4224]{5,4,3,2,1,0:T(8,128)(2,1)} %bitcast.19.refs_1_.refs_3_.refs_5_.refs_7_.refs_9_.refs_4_.refs_10_.refs_13_.refs_17_, bf16[2,2,2,32,2048]{4,3,2,1,0:T(8,128)(2,1)} %bitcast.54, ...), custom_call_target="tpu_custom_call" | custom-call | flops 1000 | bytes 1000 | tf_op jit(solution)/shard_map/combine/pallas_call | solution.py:751
  264.6 2.5 combine.17
  269.0 3.3 %collective-permute-done.28 = bf16[1,64,1024]{2,1,0:T(8,128)(2,1)S(1)} collective-permute-done((bf16[1,64,1024]{2,1,0:T(8,128)(2,1)}, bf16[1,64,1024]{2,1,0:T(8,128)(2,1)S(1)}, u32[]{:S(2)}, u32[]{:S(2)}) %collective-permute-start.28) | collective-permute-done | bytes 131104 | tf_op jit(solution)/shard_map/ppermute | solution.py:33
  273.5 3.2 %finish.1 = (f32[32,4608]{1,0:T(8,128)}, f32[32,4608]{1,0:T(8,128)}) custom-call(s32[6]{0:T(128)} %stack.32.info, bf16[64,2560]{1,0:T(8,128)(2,1)} %reduce-scatter.6.cloned.1.call-done.refs_0_, bf16[2,2,64,2048]{3,2,1,0:T(8,128)(2,1)} %bitcast.50, bf16[2,64,1024]{2,1,0:T(8,128)(2,1)} %copy-done.19, bf16[64,1024]{1,0:T(8,128)(2,1)} %bitcast.104, ...), custom_call_target="tpu_custom_call" | custom-call | flops 1000 | bytes 1000 | tf_op jit(solution)/shard_map/finish/pallas_call | solution.py:850
  280.2 16.9 %reduce-scatter.4.cloned.1.call-done.refs_0_.refs_1_.refs_2_.refs_3_.refs_4_ = bf16[32,4224]{1,0:T(8,128)(2,1)} async-done(((bf16[128,4224]{1,0:T(8,128)(2,1)}), bf16[32,4224]{1,0:T(8,128)(2,1)}) %reduce-scatter.4.cloned.1.call-update) | async-done | bytes 270352 | tf_op jit(solution)/shard_map/reduce_scatter | solution.py:985
  297.1 2.4 settle.3
  (158 shorter events, 48.2 us)
Async XLA Ops:
  7.2 235.5 %reduce-scatter.8.cloned.1.call-start = ((), (), s32[]{:S(2)}) async-start(), calls=%async_computation.5 | async-start | bytes 5242880 | tf_op jit(solution)/shard_map/reduce_scatter | solution.py:957
  7.2 7.4 %collective-permute-start.4 = (bf16[512,1024]{1,0:T(8,128)(2,1)}, bf16[512,1024]{1,0:T(8,128)(2,1)}, u32[]{:S(2)}, u32[]{:S(2)}) collective-permute-start(bf16[512,1024]{1,0:T(8,128)(2,1)} %out_own.3), channel_id=1, source_target_pairs={{0,1},{1,0},{2,3},{3,2},{4,5},{5,4},{6,7},{7,6},{8,9},{9,8},{10,11... | collective-permute-start | bytes 3145736 | tf_op jit(solution)/shard_map/ppermute | solution.py:28
  7.7 21.5 %collective-permute-start.3 = (bf16[512,3072]{1,0:T(8,128)(2,1)}, bf16[512,3072]{1,0:T(8,128)(2,1)S(1)}, u32[]{:S(2)}, u32[]{:S(2)}) collective-permute-start(bf16[512,3072]{1,0:T(8,128)(2,1)} %own_x.3), channel_id=1, source_target_pairs={{0,1},{1,0},{2,3},{3,2},{4,5},{5,4},{6,7},{7,6},{8,9},{9,8},{10,11... | collective-permute-start | bytes 9437192 | tf_op jit(solution)/shard_map/ppermute | solution.py:28
  9.4 5.2 %collective-permute-start.1 = (bf16[16,2048]{1,0:T(8,128)(2,1)S(1)}, bf16[16,2048]{1,0:T(8,128)(2,1)S(1)}, u32[]{:S(2)}, u32[]{:S(2)}) collective-permute-start(bf16[16,2048]{1,0:T(8,128)(2,1)S(1)} %pad_maximum_fusion.1), channel_id=1, source_target_pairs={{1,0},{2,1},{3,2},{4,3},{5,4},{6,5},{7,6},{8,7},{9,8},{10,9},{11,1... | collective-permute-start | bytes 196616 | tf_op jit(solution)/shard_map/ppermute | solution.py:24
  20.1 25.3 %collective-permute-start.8 = (bf16[512,2304]{1,0:T(8,128)(2,1)}, bf16[512,2304]{1,0:T(8,128)(2,1)}, u32[]{:S(2)}, u32[]{:S(2)}) collective-permute-start(bf16[512,2304]{1,0:T(8,128)(2,1)} %constant_dynamic-slice_fusion), channel_id=1, source_target_pairs={{0,1},{1,0},{2,3},{3,2},{4,5},{5,4},{6,7},{7,6},{8,9},{9,8},{10,11... | collective-permute-start | bytes 7077896 | tf_op jit(solution)/shard_map/ppermute | solution.py:28
  22.7 22.6 %collective-permute-start.7 = (bf16[512,2304]{1,0:T(8,128)(2,1)}, bf16[512,2304]{1,0:T(8,128)(2,1)}, u32[]{:S(2)}, u32[]{:S(2)}) collective-permute-start(bf16[512,2304]{1,0:T(8,128)(2,1)} %constant_dynamic-slice_fusion.1), channel_id=1, source_target_pairs={{0,1},{1,0},{2,3},{3,2},{4,5},{5,4},{6,7},{7,6},{8,9},{9,8},{10,11... | collective-permute-start | bytes 7077896 | tf_op jit(solution)/shard_map/ppermute | solution.py:28
  22.8 4.1 %collective-permute-start.2 = (bf16[8,512]{1,0:T(8,128)(2,1)S(1)}, bf16[8,512]{1,0:T(8,128)(2,1)S(1)}, u32[]{:S(2)}, u32[]{:S(2)}) collective-permute-start(bf16[8,512]{1,0:T(8,128)(2,1)S(1)} %fusion.5), channel_id=1, source_target_pairs={{0,1},{1,0},{2,3},{3,2},{4,5},{5,4},{6,7},{7,6},{8,9},{9,8},{10,11... | collective-permute-start | bytes 24584 | tf_op jit(solution)/shard_map/ppermute | solution.py:28
  28.8 16.5 %collective-permute-start.6 = (bf16[528,1024]{1,0:T(8,128)(2,1)S(1)}, bf16[528,1024]{1,0:T(8,128)(2,1)S(1)}, u32[]{:S(2)}, u32[]{:S(2)}) collective-permute-start(bf16[528,1024]{1,0:T(8,128)(2,1)S(1)} %pad_maximum_fusion.g_own.cotangent), channel_id=1, source_target_pairs={{0,1},{1,0},{2,3},{3,2},{4,5},{5,4},{6,7},{7,6},{8,9},{9,8},{10,11... | collective-permute-start | bytes 3244040 | tf_op jit(solution)/shard_map/ppermute | solution.py:28
  80.4 33.0 %collective-permute-start.9 = (bf16[8,64,1280]{2,1,0:T(8,128)(2,1)}, bf16[8,64,1280]{2,1,0:T(8,128)(2,1)S(1)}, u32[]{:S(2)}, u32[]{:S(2)}) collective-permute-start(bf16[8,64,1280]{2,1,0:T(8,128)(2,1)} %get-tuple-element.115), channel_id=1, source_target_pairs={{0,2},{2,0},{4,6},{6,4},{8,10},{10,8},{12,14},{14,12},{16,18},{18,... | collective-permute-start | bytes 3932168 | tf_op jit(solution)/shard_map/ppermute | solution.py:33
  83.2 31.3 %collective-permute-start.10 = (bf16[4,128,1280]{2,1,0:T(8,128)(2,1)}, bf16[4,128,1280]{2,1,0:T(8,128)(2,1)S(1)}, u32[]{:S(2)}, u32[]{:S(2)}) collective-permute-start(bf16[4,128,1280]{2,1,0:T(8,128)(2,1)} %get-tuple-element.116), channel_id=1, source_target_pairs={{0,4},{2,6},{4,0},{6,2},{8,12},{10,14},{12,8},{14,10},{16,20},{18,... | collective-permute-start | bytes 3932168 | tf_op jit(solution)/shard_map/ppermute | solution.py:33
  115.6 157.3 %reduce-scatter.6.cloned.1.call-start = ((), (), s32[]{:S(2)}) async-start(), calls=%async_computation.4 | async-start | bytes 1638400 | tf_op jit(solution)/shard_map/reduce_scatter | solution.py:985
  115.6 23.2 %collective-permute-start.11 = (f32[528,1024]{1,0:T(8,128)}, f32[528,1024]{1,0:T(8,128)S(1)}, u32[]{:S(2)}, u32[]{:S(2)}) collective-permute-start(f32[528,1024]{1,0:T(8,128)} %get-tuple-element.126), channel_id=1, source_target_pairs={{0,1},{1,0},{2,3},{3,2},{4,5},{5,4},{6,7},{7,6},{8,9},{9,8},{10,11... | collective-permute-start | bytes 6488072 | tf_op jit(solution)/shard_map/ppermute | solution.py:28
  118.9 19.8 %collective-permute-start.12 = (bf16[4,64,1280]{2,1,0:T(8,128)(2,1)}, bf16[4,64,1280]{2,1,0:T(8,128)(2,1)S(1)}, u32[]{:S(2)}, u32[]{:S(2)}) collective-permute-start(bf16[4,64,1280]{2,1,0:T(8,128)(2,1)} %get-tuple-element.122), channel_id=1, source_target_pairs={{0,4},{2,6},{4,0},{6,2},{8,12},{10,14},{12,8},{14,10},{16,20},{18,... | collective-permute-start | bytes 1966088 | tf_op jit(solution)/shard_map/ppermute | solution.py:33
  120.6 18.1 %collective-permute-start.13 = (bf16[4,64,1280]{2,1,0:T(8,128)(2,1)}, bf16[4,64,1280]{2,1,0:T(8,128)(2,1)S(1)}, u32[]{:S(2)}, u32[]{:S(2)}) collective-permute-start(bf16[4,64,1280]{2,1,0:T(8,128)(2,1)} %get-tuple-element.123), channel_id=1, source_target_pairs={{0,2},{2,0},{4,6},{6,4},{8,10},{10,8},{12,14},{14,12},{16,18},{18,... | collective-permute-start | bytes 1966088 | tf_op jit(solution)/shard_map/ppermute | solution.py:33
  138.8 32.6 %collective-permute-start.15 = (bf16[4,288,512]{2,1,0:T(8,128)(2,1)}, bf16[4,288,512]{2,1,0:T(8,128)(2,1)S(1)}, u32[]{:S(2)}, u32[]{:S(2)}) collective-permute-start(bf16[4,288,512]{2,1,0:T(8,128)(2,1)} %get-tuple-element.148), channel_id=1, source_target_pairs={{0,2},{2,0},{4,6},{6,4},{8,10},{10,8},{12,14},{14,12},{16,18},{18,... | collective-permute-start | bytes 3538952 | tf_op jit(solution)/shard_map/ppermute | solution.py:33
  140.2 31.2 %collective-permute-start.16 = (bf16[2,576,512]{2,1,0:T(8,128)(2,1)}, bf16[2,576,512]{2,1,0:T(8,128)(2,1)S(1)}, u32[]{:S(2)}, u32[]{:S(2)}) collective-permute-start(bf16[2,576,512]{2,1,0:T(8,128)(2,1)} %get-tuple-element.149), channel_id=1, source_target_pairs={{0,4},{2,6},{4,0},{6,2},{8,12},{10,14},{12,8},{14,10},{16,20},{18,... | collective-permute-start | bytes 3538952 | tf_op jit(solution)/shard_map/ppermute | solution.py:33
  171.4 20.9 %collective-permute-start.17 = (bf16[16,32,4224]{2,1,0:T(8,128)(2,1)}, bf16[16,32,4224]{2,1,0:T(8,128)(2,1)}, u32[]{:S(2)}, u32[]{:S(2)}) collective-permute-start(bf16[16,32,4224]{2,1,0:T(8,128)(2,1)} %get-tuple-element.151), channel_id=1, source_target_pairs={{0,1},{1,0},{2,3},{3,2},{4,5},{5,4},{6,7},{7,6},{8,9},{9,8},{10,11... | collective-permute-start | bytes 12976136 | tf_op jit(solution)/shard_map/ppermute | solution.py:28
  171.5 32.7 %collective-permute-start.14 = (f32[512,1024]{1,0:T(8,128)}, f32[512,1024]{1,0:T(8,128)}, u32[]{:S(2)}, u32[]{:S(2)}) collective-permute-start(f32[512,1024]{1,0:T(8,128)} %get-tuple-element.132), channel_id=1, source_target_pairs={{0,1},{1,0},{2,3},{3,2},{4,5},{5,4},{6,7},{7,6},{8,9},{9,8},{10,11... | collective-permute-start | bytes 6291464 | tf_op jit(solution)/shard_map/ppermute | solution.py:28
  176.0 14.9 %collective-permute-start.18 = (bf16[2,288,512]{2,1,0:T(8,128)(2,1)}, bf16[2,288,512]{2,1,0:T(8,128)(2,1)S(1)}, u32[]{:S(2)}, u32[]{:S(2)}) collective-permute-start(bf16[2,288,512]{2,1,0:T(8,128)(2,1)} %get-tuple-element.156), channel_id=1, source_target_pairs={{0,4},{2,6},{4,0},{6,2},{8,12},{10,14},{12,8},{14,10},{16,20},{18,... | collective-permute-start | bytes 1769480 | tf_op jit(solution)/shard_map/ppermute | solution.py:33
  177.9 14.5 %collective-permute-start.19 = (bf16[2,288,512]{2,1,0:T(8,128)(2,1)}, bf16[2,288,512]{2,1,0:T(8,128)(2,1)S(1)}, u32[]{:S(2)}, u32[]{:S(2)}) collective-permute-start(bf16[2,288,512]{2,1,0:T(8,128)(2,1)} %get-tuple-element.157), channel_id=1, source_target_pairs={{0,2},{2,0},{4,6},{6,4},{8,10},{10,8},{12,14},{14,12},{16,18},{18,... | collective-permute-start | bytes 1769480 | tf_op jit(solution)/shard_map/ppermute | solution.py:33
  178.5 118.6 %reduce-scatter.4.cloned.1.call-start = ((), (), s32[]{:S(2)}) async-start(), calls=%async_computation.3 | async-start | bytes 1351680 | tf_op jit(solution)/shard_map/reduce_scatter | solution.py:985
  196.7 25.0 %collective-permute-start.21 = (bf16[8,32,2176]{2,1,0:T(8,128)(2,1)}, bf16[8,32,2176]{2,1,0:T(8,128)(2,1)S(1)}, u32[]{:S(2)}, u32[]{:S(2)}) collective-permute-start(bf16[8,32,2176]{2,1,0:T(8,128)(2,1)} %get-tuple-element.164), channel_id=1, source_target_pairs={{0,4},{2,6},{4,0},{6,2},{8,12},{10,14},{12,8},{14,10},{16,20},{18,... | collective-permute-start | bytes 3342344 | tf_op jit(solution)/shard_map/ppermute | solution.py:33
  197.2 23.3 %collective-permute-start.20 = (bf16[8,32,2048]{2,1,0:T(8,128)(2,1)}, bf16[8,32,2048]{2,1,0:T(8,128)(2,1)S(1)}, u32[]{:S(2)}, u32[]{:S(2)}) collective-permute-start(bf16[8,32,2048]{2,1,0:T(8,128)(2,1)} %get-tuple-element.163), channel_id=1, source_target_pairs={{0,2},{2,0},{4,6},{6,4},{8,10},{10,8},{12,14},{14,12},{16,18},{18,... | collective-permute-start | bytes 3145736 | tf_op jit(solution)/shard_map/ppermute | solution.py:33
  201.2 33.7 %collective-permute-start.24 = (bf16[1,288,1024]{2,1,0:T(8,128)(2,1)}, bf16[1,288,1024]{2,1,0:T(8,128)(2,1)S(1)}, u32[]{:S(2)}, u32[]{:S(2)}) collective-permute-start(bf16[1,288,1024]{2,1,0:T(8,128)(2,1)} %combine.14), channel_id=1, source_target_pairs={{0,8},{2,10},{4,12},{6,14},{8,0},{10,2},{12,4},{14,6},{16,24},{18,... | collective-permute-start | bytes 1769480 | tf_op jit(solution)/shard_map/ppermute | solution.py:33
  239.8 19.2 %collective-permute-start.25 = (bf16[288,1024]{1,0:T(8,128)(2,1)}, bf16[288,1024]{1,0:T(8,128)(2,1)S(1)}, u32[]{:S(2)}, u32[]{:S(2)}) collective-permute-start(bf16[288,1024]{1,0:T(8,128)(2,1)} %get-tuple-element.173), channel_id=1, source_target_pairs={{1,17},{3,19},{5,21},{7,23},{9,25},{11,27},{13,29},{15,31},{16,0},... | collective-permute-start | bytes 1769480 | tf_op jit(solution)/shard_map/ppermute | solution.py:1103
  241.1 15.9 %collective-permute-start.23 = (bf16[4,32,2176]{2,1,0:T(8,128)(2,1)S(1)}, bf16[4,32,2176]{2,1,0:T(8,128)(2,1)S(1)}, u32[]{:S(2)}, u32[]{:S(2)}) collective-permute-start(bf16[4,32,2176]{2,1,0:T(8,128)(2,1)S(1)} %copy-done.31), channel_id=1, source_target_pairs={{0,2},{2,0},{4,6},{6,4},{8,10},{10,8},{12,14},{14,12},{16,18},{18,... | collective-permute-start | bytes 1671176 | tf_op jit(solution)/shard_map/ppermute | solution.py:33
  242.1 14.8 %collective-permute-start.22 = (bf16[4,32,2048]{2,1,0:T(8,128)(2,1)S(1)}, bf16[4,32,2048]{2,1,0:T(8,128)(2,1)S(1)}, u32[]{:S(2)}, u32[]{:S(2)}) collective-permute-start(bf16[4,32,2048]{2,1,0:T(8,128)(2,1)S(1)} %copy-done.32), channel_id=1, source_target_pairs={{0,4},{2,6},{4,0},{6,2},{8,12},{10,14},{12,8},{14,10},{16,20},{18,... | collective-permute-start | bytes 1572872 | tf_op jit(solution)/shard_map/ppermute | solution.py:33
  245.2 18.0 %collective-permute-start.26 = (bf16[2,64,1024]{2,1,0:T(8,128)(2,1)}, bf16[2,64,1024]{2,1,0:T(8,128)(2,1)S(1)}, u32[]{:S(2)}, u32[]{:S(2)}) collective-permute-start(bf16[2,64,1024]{2,1,0:T(8,128)(2,1)} %get-tuple-element.182), channel_id=1, source_target_pairs={{0,2},{2,0},{4,6},{6,4},{8,10},{10,8},{12,14},{14,12},{16,18},{18,... | collective-permute-start | bytes 786440 | tf_op jit(solution)/shard_map/ppermute | solution.py:33
  246.3 17.0 %collective-permute-start.27 = (bf16[2,64,1024]{2,1,0:T(8,128)(2,1)}, bf16[2,64,1024]{2,1,0:T(8,128)(2,1)S(1)}, u32[]{:S(2)}, u32[]{:S(2)}) collective-permute-start(bf16[2,64,1024]{2,1,0:T(8,128)(2,1)} %get-tuple-element.183), channel_id=1, source_target_pairs={{0,4},{2,6},{4,0},{6,2},{8,12},{10,14},{12,8},{14,10},{16,20},{18,... | collective-permute-start | bytes 786440 | tf_op jit(solution)/shard_map/ppermute | solution.py:33
  267.1 5.2 %collective-permute-start.28 = (bf16[1,64,1024]{2,1,0:T(8,128)(2,1)}, bf16[1,64,1024]{2,1,0:T(8,128)(2,1)S(1)}, u32[]{:S(2)}, u32[]{:S(2)}) collective-permute-start(bf16[1,64,1024]{2,1,0:T(8,128)(2,1)} %get-tuple-element.186), channel_id=1, source_target_pairs={{0,4},{2,6},{4,0},{6,2},{8,12},{10,14},{12,8},{14,10},{16,20},{18,... | collective-permute-start | bytes 393224 | tf_op jit(solution)/shard_map/ppermute | solution.py:33
  267.7 5.2 %collective-permute-start.29 = (bf16[1,64,1024]{2,1,0:T(8,128)(2,1)}, bf16[1,64,1024]{2,1,0:T(8,128)(2,1)S(1)}, u32[]{:S(2)}, u32[]{:S(2)}) collective-permute-start(bf16[1,64,1024]{2,1,0:T(8,128)(2,1)} %get-tuple-element.187), channel_id=1, source_target_pairs={{0,2},{2,0},{4,6},{6,4},{8,10},{10,8},{12,14},{14,12},{16,18},{18,... | collective-permute-start | bytes 393224 | tf_op jit(solution)/shard_map/ppermute | solution.py:33
  268.9 9.0 %collective-permute-start.31 = (f32[144,1024]{1,0:T(8,128)S(1)}, f32[144,1024]{1,0:T(8,128)S(1)}, u32[]{:S(2)}, u32[]{:S(2)}) collective-permute-start(f32[144,1024]{1,0:T(8,128)S(1)} %dynamic-slice_bitcast_fusion), channel_id=1, source_target_pairs={{0,1},{1,0},{2,3},{3,2},{4,5},{5,4},{6,7},{7,6},{8,9},{9,8},{10,11... | collective-permute-start | bytes 1769480 | tf_op jit(solution)/shard_map/ppermute | solution.py:28
  (36 other events, 127.7 us)
Sparse Core Ops, SparseCore 0:
  114.7 78.6 reduce-scatter.7
  195.8 43.0 reduce-scatter.5
  269.1 27.9 reduce-scatter.3
where the time goes:
time: 310 us; the launch traced here: 309 us
  Pallas kernels  158 us (51%)
  waiting for transfers between devices  74.6 us (24%)
  starting transfers between devices  33 us (11%)
  local copies, waits for them, and re-layouts  21.3 us (7%)
  between operations  14.2 us (5%)
  other arithmetic  8.16 us (3%)
    pallas_call x2, Pallas kernels, ffn_part(): pl.pallas_call(functools.partial(ffn_kernel, real, 2, bool(before), not p...  59.3 us
    ppermute x17, waiting for transfers between devices, across(): lax.ppermute(value, 'seq', [(place, place ^ 1 << bit) for place in range(...  50.3 us
    pallas_call x9, Pallas kernels, combine(): pl.pallas_call(functools.partial(combine_kernel, plan), out_shape=shapes,...  30.8 us
    pallas_call x1, Pallas kernels, conv_backward(): pl.pallas_call(backward_kernel, out_shape=[jax.ShapeDtypeStruct((rows, wi...  27.1 us
    ppermute x17, starting transfers between devices, across(): lax.ppermute(value, 'seq', [(place, place ^ 1 << bit) for place in range(...  22.1 us
    pallas_call x1, Pallas kernels, down_part(): pl.pallas_call(down_kernel, out_shape=shapes, grid_spec=pltpu.PrefetchSca...  17 us
    reduce_scatter x2, waiting for transfers between devices, upper_sum(): lax.psum_scatter(value, 'seq', scatter_dimension=0, axis_index_groups=gro...  16.9 us
    pallas_call x1, Pallas kernels, conv_forward(): pl.pallas_call(forward_kernel, out_shape=[jax.ShapeDtypeStruct((ext + HAL...  14 us
  transfers between devices with their start and end apart: 35, of which 15 were waited for; matrix products, arithmetic and copies ran while one was open for 6% of the time, Pallas kernels for 40%

commit v1 on v0

--- a/solution.py
+++ b/solution.py
@@ -12,7 +12,7 @@
 AXES = ("seq", "wa")
 HALO = 16
 TILE = 256
-VMEM_LIMIT = 58 * 2**20
+VMEM_LIMIT = 63 * 2**20
 NN = ((1,), (0,))
 NT = ((1,), (1,))
 TN = ((0,), (0,))
@@ -236,6 +236,7 @@
     tokens,
     hidden,
     cotangent,
+    after,
     back,
     came,
     small,
@@ -300,9 +301,8 @@
         scale = lax.rsqrt(jnp.mean(resid * resid, axis=-1, keepdims=True) + epsilon)
         normed = resid * scale
         vectors[1:2, :] = jnp.sum(grad[:rows] * normed[:rows], axis=0, keepdims=True)
-        result = cotangent[...].astype(jnp.float32) + back_through(
-            grad, normed, scale, small[1:2, :]
-        )
+        result = back_through(grad, normed, scale, small[1:2, :])
+        result = result + jnp.concatenate([cotangent[...], after[...]], axis=0).astype(jnp.float32)
         d_hidden[...] = result
         d_branch[...] = result.astype(jnp.bfloat16)
         norm_in[...] = (token_norm()[0] * small[0:1, :]).astype(jnp.bfloat16)
@@ -379,6 +379,7 @@
     tokens,
     hidden,
     cotangent,
+    after,
     back,
     came,
     small,
@@ -413,7 +414,8 @@
             in_specs=[
                 fixed(rows, width),
                 fixed(ext, width),
-                fixed(ext, width),
+                fixed(rows, width),
+                pl.BlockSpec((HALO, width), lambda j, info: (0, 1)),
                 fixed(ext, width),
                 fixed(ext, width),
                 fixed(*small.shape),
@@ -452,6 +454,7 @@
         tokens,
         hidden,
         cotangent,
+        after,
         back,
         came,
         small,
@@ -466,44 +469,52 @@
 
 
 def ffn_kernel(
-    real,
     pieces,
-    chained,
-    joined,
+    split,
     info,
     n_own,
     n_other,
     g_own,
+    g_after,
     g_other,
+    g_other_after,
     gate_own,
     gate_other,
     up_own,
     up_other,
     down_ref,
-    *refs,
+    act_ref,
+    back_keep,
+    back_send,
+    gate_send,
+    gate_keep,
+    up_send,
+    up_keep,
+    whole,
+    n_all,
+    g_all,
+    back,
+    weights,
+    grads,
 ):
-    before, refs = (refs[:2], refs[2:]) if chained else ((), refs)
-    act_ref, back_keep, back_send = refs[:3]
-    results, (n_all, g_all, back, weights, grads) = refs[3:-5], refs[-5:]
+    step = pl.program_id(0)
     rows = n_all.shape[0]
-    block = real // 2
+    block = g_own.shape[0]
+    real = 2 * block
     tile = down_ref.shape[0]
     places = (
-        (pl.ds(0, block), 0, pl.ds(0, block)),
-        (pl.ds(real, HALO), 0, pl.ds(block, HALO)),
-        (pl.ds(block, block), 1, pl.ds(0, block)),
-        (pl.ds(real + HALO, HALO), 1, pl.ds(block, HALO)),
-    )
-
-    @pl.when(pl.program_id(0) == 0)
+        (pl.ds(0, block), 0, pl.ds(0, block), g_own),
+        (pl.ds(real, HALO), 0, pl.ds(block, HALO), g_after),
+        (pl.ds(block, block), 1, pl.ds(0, block), g_other),
+        (pl.ds(real + HALO, HALO), 1, pl.ds(block, HALO), g_other_after),
+    )
+
+    @pl.when(step == 0)
     def _():
-        for place, which, source in places:
+        back[...] = jnp.zeros(back.shape, jnp.float32)
+        for place, which, source, grad in places:
             n_all[place, :] = (n_own, n_other)[which][source, :]
-            g_all[place, :] = (g_own, g_other)[which][source, :]
-            if chained:
-                back[place, :] = before[which][source, :]
-            else:
-                back[place, :] = jnp.zeros((place.size, back.shape[1]), jnp.float32)
+            g_all[place, :] = grad[...]
 
     join_rows(weights, (gate_own, up_own), (gate_other, up_other))
     size = -(-rows // pieces // 16) * 16
@@ -520,44 +531,36 @@
         grads[part, :tile] = (d_act * up_val * (sigma + silu * (1.0 - sigma))).astype(jnp.bfloat16)
         back[part, :] += dot(grads[part, :], weights[...], NT)
     summed = dot(n_all[:real, :], grads[:real, :], TN).astype(jnp.bfloat16)
-    if joined:
-        (out,) = results
-        half = summed.shape[0] // 2
-
-        @pl.when(info[0] == 0)
+    half = summed.shape[0] // 2
+    for core in range(2):
+
+        @pl.when(jnp.logical_and(step >= split, info[0] == core))
         def _():
-            out[...] = summed
-
-        @pl.when(info[0] != 0)
-        def _():
-            out[:half, :] = summed[half:, :]
-            out[half:, :] = summed[:half, :]
-
-    else:
-        for index, grad in enumerate((summed[:, :tile], summed[:, tile:])):
-            send, keep = results[2 * index : 2 * index + 2]
-            groups, per, columns = send.shape
-            pair = grad.reshape(groups, 2, per, columns)
-            for value in range(2):
-
-                @pl.when(info[1 + index] == value)
-                def _():
-                    send[...] = pair[:, 1 - value]
-                    keep[...] = pair[:, value]
-
-    @pl.when(pl.program_id(0) == pl.num_programs(0) - 1)
+            whole[:half, :] = summed[core * half : (core + 1) * half, :]
+            whole[half:, :] = summed[(1 - core) * half : (2 - core) * half, :]
+
+    for index, (send, keep) in enumerate(((gate_send, gate_keep), (up_send, up_keep))):
+        groups, per, columns = send.shape
+        pair = summed[:, index * tile : (index + 1) * tile].reshape(groups, 2, per, columns)
+        for value in range(2):
+
+            @pl.when(jnp.logical_and(step < split, info[1 + index] == value))
+            def _():
+                send[...] = pair[:, 1 - value]
+                keep[...] = pair[:, value]
+
+    @pl.when(step == pl.num_programs(0) - 1)
     def _():
-        for place, which, source in places:
+        for place, which, source, _ in places:
             (back_keep, back_send)[which][source, :] = back[place, :]
 
 
-def ffn_part(info, acts, weights, down, before, first, count, pers):
-    ext, width = acts[0].shape
-    rows, real = 2 * ext, 2 * (ext - HALO)
+def ffn(info, norms, grads, weights, down, split, pers):
+    ext, width = norms[0].shape
+    rows = 2 * ext
     half = width // 2
-    blocks = down.shape[0] // TILE
-    own = pl.BlockSpec((half, TILE), lambda j, info: (0, info[0] * blocks + first + j))
-    other = pl.BlockSpec((half, TILE), lambda j, info: (0, first + j))
+    count = down.shape[0] // TILE
+    column = pl.BlockSpec((half, TILE), lambda j, info: (0, info[0] * count + j))
     shapes = [jax.ShapeDtypeStruct((rows, count * TILE), jnp.bfloat16)]
     specs = [pl.BlockSpec((rows, TILE), lambda j, info: (0, j))]
     for _ in range(2):
@@ -566,21 +569,25 @@
     for per in pers:
         for _ in range(2):
             groups = width // (2 * per)
-            shapes.append(jax.ShapeDtypeStruct((groups, per, count * TILE), jnp.bfloat16))
-            specs.append(pl.BlockSpec((groups, per, TILE), lambda j, info: (0, 0, j)))
-    if not pers:
-        shapes.append(jax.ShapeDtypeStruct((width, 2 * count * TILE), jnp.bfloat16))
-        specs.append(pl.BlockSpec((width, 2 * TILE), lambda j, info: (0, j)))
+            shapes.append(jax.ShapeDtypeStruct((groups, per, split * TILE), jnp.bfloat16))
+            specs.append(
+                pl.BlockSpec(
+                    (groups, per, TILE), lambda j, info: (0, 0, jnp.minimum(j, split - 1))
+                )
+            )
+    shapes.append(jax.ShapeDtypeStruct((width, 2 * (count - split) * TILE), jnp.bfloat16))
+    specs.append(pl.BlockSpec((width, 2 * TILE), lambda j, info: (0, jnp.maximum(j - split, 0))))
+    after = pl.BlockSpec((HALO, width), lambda j, info: (0, 1))
     return pl.pallas_call(
-        functools.partial(ffn_kernel, real, 2, bool(before), not pers),
+        functools.partial(ffn_kernel, 2, split),
         out_shape=shapes,
         grid_spec=pltpu.PrefetchScalarGridSpec(
             num_scalar_prefetch=1,
             grid=(count,),
-            in_specs=[fixed(ext, width)] * 4
-            + [own, other, own, other]
-            + [pl.BlockSpec((TILE, width), lambda j, info: (first + j, 0))]
-            + [fixed(ext, width)] * len(before),
+            in_specs=[fixed(ext, width)] * 2
+            + [fixed(ext - HALO, width), after] * 2
+            + [column] * 4
+            + [pl.BlockSpec((TILE, width), lambda j, info: (j, 0))],
             out_specs=specs,
             scratch_shapes=[
                 pltpu.VMEM((rows, width), jnp.bfloat16),
@@ -592,13 +599,12 @@
         ),
         name="ffn",
         **params(),
-    )(info, *acts, *weights, down, *before)
+    )(info, *norms, *grads, *weights, down)
 
 
 def down_kernel(
     info,
-    act_one,
-    act_two,
+    act,
     g_own,
     g_other,
     down_ref,
@@ -614,16 +620,12 @@
     step = pl.program_id(0)
     block = out_keep.shape[0]
     real = 2 * block
-    cut = act_one.shape[1]
-    rhs[:block, :] = g_own[:block, :]
-    rhs[block:, :] = g_other[:block, :]
-    result = dot(act_one[:real, :], down_ref[:cut, :], NN) + dot(
-        act_two[:real, :], down_ref[cut:, :], NN
-    )
+    rhs[:block, :] = g_own[...]
+    rhs[block:, :] = g_other[...]
+    result = dot(act[:real, :], down_ref[...], NN)
     out_keep[...] = result[:block]
     out_send[...] = result[block:]
-    grad[:cut, :] = dot(act_one[:real, :], rhs[...], TN).astype(grad.dtype)
-    grad[cut:, :] = dot(act_two[:real, :], rhs[...], TN).astype(grad.dtype)
+    grad[...] = dot(act[:real, :], rhs[...], TN).astype(grad.dtype)
     here = pl.num_programs(0) // 2
     outs = ((step < here, low_send, low_keep, info[1]), (step >= here, high_send, high_keep, info[2]))
     for now, send, keep, mine in outs:
@@ -638,10 +640,11 @@
                     keep[group] = grad[pl.ds(start + value * per, per), :]
 
 
-def down_part(info, act_one, act_two, g_own, g_other, down, pers, block):
+def down_part(info, act, g_own, g_other, down, pers):
     hidden, width = down.shape
     steps = width // TILE
     here = steps // 2
+    block = g_own.shape[0]
     kind = jnp.bfloat16 if min(pers) % 16 == 0 else jnp.float32
     tile = pl.BlockSpec((block, TILE), lambda j, info: (0, j))
     shapes = [jax.ShapeDtypeStruct((block, width), jnp.float32)] * 2
@@ -660,7 +663,6 @@
                 specs.append(
                     pl.BlockSpec((groups, per, TILE), lambda j, info: (0, 0, jnp.maximum(j - here, 0)))
                 )
-    ext = g_own.shape[0]
     return pl.pallas_call(
         down_kernel,
         out_shape=shapes,
@@ -668,10 +670,9 @@
             num_scalar_prefetch=1,
             grid=(steps,),
             in_specs=[
-                fixed(*act_one.shape),
-                fixed(*act_two.shape),
-                pl.BlockSpec((ext, TILE), lambda j, info: (0, j)),
-                pl.BlockSpec((ext, TILE), lambda j, info: (0, j)),
+                fixed(*act.shape),
+                tile,
+                tile,
                 pl.BlockSpec((hidden, TILE), lambda j, info: (0, j)),
             ],
             out_specs=specs,
@@ -682,7 +683,7 @@
         ),
         name="down",
         **params(),
-    )(info, act_one, act_two, g_own, g_other, down)
+    )(info, act, g_own, g_other, down)
 
 
 def combine_kernel(plan, info, *refs):
@@ -906,11 +907,10 @@
     before_rows = shifted(tokens[rows - HALO :], 1)
     after_rows = shifted(jnp.concatenate([tokens[:HALO], cotangent[:HALO]], axis=1), -1)
     w_out_other = partner(out_weight)
-    gate_late, up_late = after((gate_weight, up_weight), before_rows, after_rows, w_out_other)
-    gate_other = partner(lax.dynamic_slice_in_dim(gate_late, (1 - core) * hidden, hidden, 1))
-    up_other = partner(lax.dynamic_slice_in_dim(up_late, (1 - core) * hidden, hidden, 1))
-    cot_own = jnp.concatenate([cotangent, after_rows[:, width:]], axis=0)
-    cot_other = partner(cot_own)
+    cot_other = partner(cotangent)
+    after_other = partner(after_rows)
+    gate_other = partner(gate_weight)
+    up_other = partner(up_weight)
 
     place = lax.axis_index(AXES) * rows + jnp.arange(rows + HALO, dtype=jnp.int32)
     starts = jnp.cumsum(doc_lengths) - doc_lengths
@@ -938,24 +938,28 @@
     per_chip = width // chips
     pers = (per_chip << lower[0], per_chip << lower[1])
     tiles = hidden // TILE
-    split = tiles * 5 // 9
+    split = tiles * 4 // 9
     counts = (split, tiles - split)
     orders = (lower, [lower[1], lower[0]] + lower[2:])
 
-    acts = (norm_own, norm_other, cot_own, cot_other)
-    weights = (gate_weight, gate_other, up_weight, up_other)
-    one = ffn_part(info, acts, weights, down_weight, (), 0, counts[0], pers)
-    one_x = across(one[3], orders[0][0])
-    one_y = across(one[5], orders[1][0])
-    two = ffn_part(info, acts, weights, down_weight, one[1:3], split, counts[1], ())
-    two, one_x, one_y = ordering((two, one_x, one_y))
-    came = partner(two[2])
+    act, back_keep, back_send, *one, whole = ffn(
+        info,
+        (norm_own, norm_other),
+        (cotangent, after_rows, cot_other, after_other),
+        (gate_weight, gate_other, up_weight, up_other),
+        down_weight,
+        split,
+        pers,
+    )
+    one_x = across(one[0], orders[0][0])
+    one_y = across(one[2], orders[1][0])
+    came = partner(back_send)
 
     groups = [
         [low + (level << (top - 1)) for level in range(4)] for low in range(1 << (top - 1))
     ]
     quarter = lax.psum_scatter(
-        two[3], "seq", scatter_dimension=0, axis_index_groups=groups, tiled=True
+        whole, "seq", scatter_dimension=0, axis_index_groups=groups, tiled=True
     )
 
     slots = {bit: 1 + bit for bit in bits}
@@ -986,23 +990,26 @@
             value, "seq", scatter_dimension=0, axis_index_groups=groups, tiled=True
         )
 
+    down_pers = [2 * hidden // chips << bit for bit in (lower[0], lower[1])]
+    out_keep, out_send, *down_halves = down_part(
+        info, act, cotangent, cot_other, down_weight, down_pers
+    )
+    came, out_send, down_halves, one_x, one_y = ordering(
+        (came, out_send, down_halves, one_x, one_y)
+    )
+
+    down_x = across(down_halves[0], orders[0][0])
+    down_y = across(down_halves[2], orders[1][0])
+    out_came = partner(out_send)
     one_terms = [
         [plain(keep, without(bits, order[0])), plain(got, without(bits, order[0]))]
-        for keep, got, order in ((one[4], one_x, orders[0]), (one[6], one_y, orders[1]))
+        for keep, got, order in ((one[1], one_x, orders[0]), (one[3], one_y, orders[1]))
     ]
     one_sent, one_got = send_on(
         [(order[1], [terms]) for terms, order in zip(one_terms, orders)], bits, turned_slots
     )
-    down_pers = [2 * hidden // chips << bit for bit in (lower[0], lower[1])]
-    out_keep, out_send, *down_halves = down_part(
-        info, one[0], after(two[0], one_sent), cot_own, cot_other, down_weight, down_pers, rows
-    )
     one_got = [got for got, _ in one_got]
-    came, one_got, out_send, down_halves = ordering((came, one_got, out_send, down_halves))
-
-    down_x = across(down_halves[0], orders[0][0])
-    down_y = across(down_halves[2], orders[1][0])
-    out_came = partner(out_send)
+    came = after(came, one_sent)
 
     def side_by_side(streams, order, use=slots):
         sent = None
@@ -1021,20 +1028,13 @@
             streams = members
         return sent, streams
 
-    one_streams = [
-        terms + [plain(got, without(bits, *order[:2]))]
-        for terms, got, order in zip(one_terms, one_got, orders)
-    ]
-    _, one_streams = side_by_side(one_streams, lower[2 : top - 1], turned_slots)
-    ((one_all, _),) = combine(info, turned_slots, [(None, one_streams)], flip=True)
-    came, one_all = ordering((came, one_all))
-    one_done = upper_sum(one_all)
     input_grad, conv_send, *conv_keeps = conv_backward(
         info,
         tokens,
         hidden_res,
-        cot_own,
-        two[1],
+        cotangent,
+        after_rows,
+        back_keep,
         came,
         small,
         keeps,
@@ -1045,9 +1045,11 @@
         w_out_other,
         2 * chips,
     )
-    conv_send, conv_keeps, down_x, down_y = ordering((conv_send, conv_keeps, down_x, down_y))
-
+    conv_send, conv_keeps, down_x, down_y, out_came = ordering(
+        (conv_send, conv_keeps, down_x, down_y, out_came)
+    )
     conv_came = partner(conv_send)
+
     down_bits = bits[1:]
     down_terms = [
         [plain(keep, without(down_bits, order[0])), plain(got, without(down_bits, order[0]))]
@@ -1060,8 +1062,8 @@
         [(order[1], [terms]) for terms, order in zip(down_terms, orders)], down_bits
     )
     down_got = [got for got, _ in down_got]
-    conv_came, down_got = ordering((conv_came, down_got))
-
+
+    conv_came = after(conv_came, down_sent)
     conv_members = [
         [
             [plain(conv_keeps[member], bits), (conv_came, bits, member * width // size, size)]
@@ -1074,14 +1076,35 @@
     )
     conv_got = [got for got, _ in conv_got]
 
-    block_out = (hidden_res[:rows] + out_keep + out_came).astype(jnp.bfloat16)
+    one_got = after(one_got, conv_sent)
+    one_streams = [
+        terms + [plain(got, without(bits, *order[:2]))]
+        for terms, got, order in zip(one_terms, one_got, orders)
+    ]
+    _, one_streams = side_by_side(one_streams, lower[2 : top - 1], turned_slots)
+    ((one_all, _),) = combine(info, turned_slots, [(None, one_streams)], flip=True)
+    one_done = upper_sum(one_all)
+
+    down_got = after(down_got, one_all)
     down_streams = [
         terms + [plain(got, without(down_bits, *order[:2]))]
         for terms, got, order in zip(down_terms, down_got, orders)
     ]
     down_sent, down_streams = side_by_side(down_streams, lower[2:])
-    conv_got = after(conv_got, block_out)
-
+    out_came = after(out_came, down_sent)
+    block_out = (hidden_res[:rows] + out_keep + out_came).astype(jnp.bfloat16)
+
+    down_streams = gated(down_streams, block_out)
+    part, down_last = settle(info, slots, [(down_streams, (jnp.float32, jnp.bfloat16))])
+    pairs = [
+        (source * 2 + side, (source ^ (1 << top)) * 2 + side)
+        for source in range(chips)
+        for side in range(2)
+        if (source >> top) & 1 != side
+    ]
+    down_far = lax.ppermute(down_last, AXES, pairs)
+
+    conv_got = after(conv_got, down_last)
     for index, (members, order) in enumerate(zip(conv_members, orders)):
         edge = 0
         for terms in members:
@@ -1091,30 +1114,16 @@
     conv_sent, conv_two = send_on(
         [(order[1], members) for members, order in zip(conv_members, orders)], bits
     )
+    conv_two = [got for got, _ in conv_two]
+
     quarter = after(quarter, conv_sent)
-    down_streams = gated(down_streams, conv_sent)
-    part, down_last = settle(info, slots, [(down_streams, (jnp.float32, jnp.bfloat16))])
-    pairs = [
-        (source * 2 + side, (source ^ (1 << top)) * 2 + side)
-        for source in range(chips)
-        for side in range(2)
-        if (source >> top) & 1 != side
-    ]
-    down_far = lax.ppermute(down_last, AXES, pairs)
     edge = counts[1] * TILE
     two_terms = [[(quarter, bits[2:], block, edge)] for block in range(2)]
     two_sent, two_got = send_on(
         [(order[0], [terms]) for terms, order in zip(two_terms, orders)], bits[2:]
     )
     two_got = [got for got, _ in two_got]
-
-    conv_two, down_far = ordering(([got for got, _ in conv_two], down_far))
-    part = part + down_far.astype(jnp.float32)
-    part = part.reshape(2, -1, width)
-    down_out = jnp.where(
-        coords[top] == core, take(part, core, 0), partner(take(part, 1 - core, 0))
-    )
-
+    conv_two = after(conv_two, two_sent)
     conv_streams = []
     for members, got, order in zip(conv_members, conv_two, orders):
         edge = 0
@@ -1124,6 +1133,7 @@
             edge += size
     _, conv_streams = side_by_side(conv_streams, lower[2 : top - 1])
     ((conv_all, _),) = combine(info, slots, [(None, conv_streams)])
+    conv_done = upper_sum(conv_all)
     two_got = after(two_got, conv_all)
     two_terms = [
         terms + [plain(got, without(bits[2:], order[0]))]
@@ -1135,8 +1145,12 @@
     two_streams = [terms + [plain(*got)] for terms, got in zip(two_terms, two_got)]
     _, two_streams = side_by_side(two_streams, lower[2 : top - 1])
 
-    conv_done = upper_sum(conv_all)
-    two_streams = gated(two_streams, conv_all)
+    part, down_far = after((part, down_far), conv_all)
+    part = part + down_far.astype(jnp.float32)
+    part = part.reshape(2, -1, width)
+    down_out = jnp.where(
+        coords[top] == core, take(part, core, 0), partner(take(part, 1 - core, 0))
+    )
     b_out, out_out, c_out, x_out, vectors = (
         [(conv_done, [], member * width // size, size)]
         for member, size in enumerate([width] * 4 + [128])
@@ -1154,7 +1168,6 @@
     gate_tiles = [tile for tile in range(counts[0])] + [tiles + tile for tile in range(counts[0])]
     for tile in range(counts[1]):
         gate_tiles += [counts[0] + tile, tiles + counts[0] + tile]
-    two_streams = gated(two_streams, conv_sent)
     kept, send = finish(info, slots, [[plain(one_done, [])]] + two_streams, gate_tiles)
     other = partner(send)
     gate_out = both(kept[:, :hidden], other[:, :hidden], 1)

time: 310 us -> 290 us (0.935)
  Pallas kernels: 158 us -> 151 us
  local copies, waits for them, and re-layouts: 21.3 us -> 14.5 us
  waiting for transfers between devices: 74.6 us -> 69.3 us
  starting transfers between devices: 33 us -> 29.4 us
  other arithmetic: 8.16 us -> 11.4 us
    ppermute x17, waiting for transfers between devices: 50.3 us -> 38.8 us  [across(): lax.ppermute(value, 'seq', [(place, place ^ 1 << bit) for place in range(...]
    pallas_call x2 -> x1, Pallas kernels: 59.3 us -> 52 us  [ffn(): pl.pallas_call(functools.partial(ffn_kernel, 2, split), out_shape=shapes,...]
    dynamic_slice x2 -> x0, local copies, waits for them, and re-layouts: 5.44 us -> none  [the longest x1 3.77 us: local(): lax.dynamic_slice_in_dim(gate_late, (1 - core) * hidden, hidden, 1)]
    ppermute x2, waiting for transfers between devices: 0.85 us -> 5.6 us  [shifted(): lax.ppermute(value, AXES, [(source, source + steps) for source in range(f...]
    unnamed x67 -> x21, local copies, waits for them, and re-layouts: 9.2 us -> 5.04 us
    ppermute x12 -> x13, waiting for transfers between devices: 4.49 us -> 7.08 us  [partner(): return lax.ppermute(value, 'wa', [(0, 1), (1, 0)])]
  transfers between devices with their start and end apart: 35 -> 36, of which waited for: 15 -> 19; matrix products, arithmetic and copies ran while one was open for 6% -> 6% of each run, Pallas kernels for 40% -> 33%
where the time goes in v1:
time: 290 us; the launch traced here: 289 us
  Pallas kernels  151 us (52%)
  waiting for transfers between devices  69.3 us (24%)
  starting transfers between devices  29.4 us (10%)
  local copies, waits for them, and re-layouts  14.5 us (5%)
  between operations  14 us (5%)
  other arithmetic  11.4 us (4%)
    pallas_call x1, Pallas kernels, ffn(): pl.pallas_call(functools.partial(ffn_kernel, 2, split), out_shape=shapes,...  52 us
    ppermute x17, waiting for transfers between devices, across(): lax.ppermute(value, 'seq', [(place, place ^ 1 << bit) for place in range(...  38.8 us
    pallas_call x9, Pallas kernels, combine(): pl.pallas_call(functools.partial(combine_kernel, plan), out_shape=shapes,...  30.2 us
    pallas_call x1, Pallas kernels, conv_backward(): pl.pallas_call(backward_kernel, out_shape=[jax.ShapeDtypeStruct((rows, wi...  27.3 us
    ppermute x17, starting transfers between devices, across(): lax.ppermute(value, 'seq', [(place, place ^ 1 << bit) for place in range(...  20.8 us
    reduce_scatter x2, waiting for transfers between devices, upper_sum(): lax.psum_scatter(value, 'seq', scatter_dimension=0, axis_index_groups=gro...  17.8 us
    pallas_call x1, Pallas kernels, down_part(): pl.pallas_call(down_kernel, out_shape=shapes, grid_spec=pltpu.PrefetchSca...  17.7 us
    pallas_call x1, Pallas kernels, conv_forward(): pl.pallas_call(forward_kernel, out_shape=[jax.ShapeDtypeStruct((ext + HAL...  14 us
  transfers between devices with their start and end apart: 36, of which 19 were waited for; matrix products, arithmetic and copies ran while one was open for 6% of the time, Pallas kernels for 33%

profile of v1, /device:TPU:0, one launch (start us, length us, event | category | flops | bytes accessed | tf_op | source)
XLA Modules:
  0.0 289.2 jit_solution(1119964730481491692)
XLA Ops:
  15.3 2.3 collective-permute-start
  19.1 3.0 %collective-permute-done.before = bf16[16,1024]{1,0:T(8,128)(2,1)S(1)} collective-permute-done((bf16[16,1024]{1,0:T(8,128)(2,1)S(1)}, bf16[16,1024]{1,0:T(8,128)(2,1)S(1)}, u32[]{:S(2)}, u32[]{:S(2)}) %collective-permute-start) | collective-permute-done | bytes 32800 | tf_op jit(solution)/shard_map/ppermute | solution.py:24
  24.0 2.6 collective-permute-done.1.after.g_after
  28.4 14.0 %conv_forward.1 = (f32[544,1024]{1,0:T(8,128)}, f32[544,1024]{1,0:T(8,128)}, f32[544,1024]{1,0:T(8,128)}, f32[528,1024]{1,0:T(8,128)}, bf16[528,1024]{1,0:T(8,128)(2,1)}, /*index=5*/bf16[528,1024]{1,0:T(8,128)(2,1)}) custom-call(s32[6]{0:T(128)} %stack.32.info, bf16[512,1024]{1,0:T(8,128)(2,1)} %tokens.3, bf16[16,1024]{1,0:T(8,128)(2,1)} %copy-done.9, ...), custom_call_target="tpu_custom_call" | custom-call | flops 1000 | bytes 1000 | tf_op jit(solution)/shard_map/conv_forward/pallas_call | solution.py:191
  43.7 2.2 collective-permute-done.7.g_other_after
  47.5 52.0 %ffn.1 = (bf16[1056,2304]{1,0:T(8,128)(2,1)}, f32[528,1024]{1,0:T(8,128)}, f32[528,1024]{1,0:T(8,128)}, bf16[8,64,1024]{2,1,0:T(8,128)(2,1)}, bf16[8,64,1024]{2,...) custom-call(s32[6]{0:T(128)} %stack.32.info, ...), custom_call_target="tpu_custom_call" | custom-call | flops 1000 | bytes 1000 | tf_op jit(solution)/shard_map/ffn/pallas_call | solution.py:581
  100.0 2.9 %collective-permute-start.11 = (bf16[8,64,1024]{2,1,0:T(8,128)(2,1)}, bf16[8,64,1024]{2,1,0:T(8,128)(2,1)}, u32[]{:S(2)}, u32[]{:S(2)}) collective-permute-start(bf16[8,64,1024]{2,1,0:T(8,128)(2,1)} %get-tuple-element.103), channel_id=1, source_target_pairs={{0,2},{2,0},{4,6},{6,4},{8,10},{10,8},{12,14},{14,12},{16,18},{18,... | collective-permute-start | bytes 3145736 | tf_op jit(solution)/shard_map/ppermute | solution.py:33
  102.9 2.4 collective-permute-start.12
  105.3 17.7 %down.1 = (f32[512,1024]{1,0:T(8,128)}, f32[512,1024]{1,0:T(8,128)}, bf16[4,288,512]{2,1,0:T(8,128)(2,1)}, bf16[4,288,512]{2,1,0:T(8,128)(2,1)}, bf16[2,576,512]...) custom-call(s32[6]{0:T(128)} %stack.32.info, bf16[1056,2304]{1,0:T(8,128)(2,1)} %get-tuple-element.94.act, ...), custom_call_target="tpu_custom_call" | custom-call | flops 1000 | bytes 1000 | tf_op jit(solution)/shard_map/down/pallas_call | solution.py:666
  123.0 3.7 %collective-permute-done.11 = bf16[8,64,1024]{2,1,0:T(8,128)(2,1)} collective-permute-done((bf16[8,64,1024]{2,1,0:T(8,128)(2,1)}, bf16[8,64,1024]{2,1,0:T(8,128)(2,1)}, u32[]{:S(2)}, u32[]{:S(2)}) %collective-permute-start.11) | collective-permute-done | bytes 1048608 | tf_op jit(solution)/shard_map/ppermute | solution.py:33
  126.7 2.1 collective-permute-done.12
  130.9 3.1 %combine.9 = (bf16[4,64,1024]{2,1,0:T(8,128)(2,1)}, bf16[4,64,1024]{2,1,0:T(8,128)(2,1)}) custom-call(s32[6]{0:T(128)} %stack.32.info, bf16[2,2,2,64,1024]{4,3,2,1,0:T(8,128)(2,1)} %bitcast.70, bf16[2,2,2,64,1024]{4,3,2,1,0:T(8,128)(2,1)} %bitcast.9.refs_1_, bf16[2,2,2,64,1024]{4,3,2,1,0:T(8,128)(2,1)} %bitcast.72, ...), custom_call_target="tpu_custom_call" | custom-call | flops 1000 | bytes 1000 | tf_op jit(solution)/shard_map/combine/pallas_call | solution.py:752
  134.0 27.3 %conv_backward.1 = (bf16[512,1024]{1,0:T(8,128)(2,1)}, bf16[16,32,4224]{2,1,0:T(8,128)(2,1)}, bf16[16,32,1024]{2,1,0:T(8,128)(2,1)}, bf16[16,32,1024]{2,1,0:T(8,...) custom-call(s32[6]{0:T(128)} %stack.32.info, ...), custom_call_target="tpu_custom_call" | custom-call | flops 1000 | bytes 1000 | tf_op jit(solution)/shard_map/conv_backward/pallas_call | solution.py:403
  163.4 3.2 %combine.10 = (bf16[2,288,512]{2,1,0:T(8,128)(2,1)}, bf16[2,288,512]{2,1,0:T(8,128)(2,1)}) custom-call(s32[6]{0:T(128)} %stack.32.info, bf16[2,2,288,512]{3,2,1,0:T(8,128)(2,1)} %bitcast.46, bf16[2,2,288,512]{3,2,1,0:T(8,128)(2,1)} %bitcast.13.refs_1_, bf16[2,2,288,512]{3,2,1,0:T(8,128)(2,1)} %bitcast.49, ...), custom_call_target="tpu_custom_call" | custom-call | flops 1000 | bytes 1000 | tf_op jit(solution)/shard_map/combine/pallas_call | solution.py:752
  169.1 4.1 %combine.11 = (bf16[8,32,2048]{2,1,0:T(8,128)(2,1)}, bf16[8,32,2176]{2,1,0:T(8,128)(2,1)}) custom-call(s32[6]{0:T(128)} %stack.32.info, bf16[2,2,2,2,32,1024]{5,4,3,2,1,0:T(8,128)(2,1)} %bitcast.52, bf16[2,2,2,2,32,4224]{5,4,3,2,1,0:T(8,128)(2,1)} %bitcast.17.refs_1_.refs_3_.refs_5_.refs_7_.refs_9_.refs_4_.refs_10_.refs_13_.refs_17_, ...), custom_call_target="tpu_custom_call" | custom-call | flops 1000 | bytes 1000 | tf_op jit(solution)/shard_map/combine/pallas_call | solution.py:752
  173.5 3.0 %collective-permute-done.18 = bf16[4,64,1024]{2,1,0:T(8,128)(2,1)} collective-permute-done((bf16[4,64,1024]{2,1,0:T(8,128)(2,1)}, bf16[4,64,1024]{2,1,0:T(8,128)(2,1)}, u32[]{:S(2)}, u32[]{:S(2)}) %collective-permute-start.18) | collective-permute-done | bytes 524320 | tf_op jit(solution)/shard_map/ppermute | solution.py:33
  176.7 3.6 %combine.12 = bf16[4,64,2048]{2,1,0:T(8,128)(2,1)} custom-call(s32[6]{0:T(128)} %stack.32.info, bf16[2,2,2,64,1024]{4,3,2,1,0:T(8,128)(2,1)} %bitcast.71, bf16[2,2,2,64,1024]{4,3,2,1,0:T(8,128)(2,1)} %bitcast.9.refs_1_, bf16[2,2,64,1024]{3,2,1,0:T(8,128)(2,1)} %bitcast.22.refs_2_, bf16[2,2,2,64,1024]{4,3,2,1,0:T(8,128)(2,1)} %bitcast.73, ...), custom_call_target="tpu_custom_call" | custom-call | flops 1000 | bytes 1000 | tf_op jit(solution)/shard_map/combine/pallas_call | solution.py:752
  182.4 6.6 %collective-permute-done.16.refs_2_ = bf16[2,288,512]{2,1,0:T(8,128)(2,1)S(1)} collective-permute-done((bf16[2,288,512]{2,1,0:T(8,128)(2,1)}, bf16[2,288,512]{2,1,0:T(8,128)(2,1)S(1)}, u32[]{:S(2)}, u32[]{:S(2)}) %collective-permute-start.16) | collective-permute-done | bytes 589856 | tf_op jit(solution)/shard_map/ppermute | solution.py:33
  189.8 3.1 %combine.13 = bf16[1,288,1024]{2,1,0:T(8,128)(2,1)} custom-call(s32[6]{0:T(128)} %stack.32.info, bf16[2,2,288,512]{3,2,1,0:T(8,128)(2,1)} %bitcast.47, bf16[2,2,288,512]{3,2,1,0:T(8,128)(2,1)} %bitcast.13.refs_1_, bf16[2,288,512]{2,1,0:T(8,128)(2,1)} %copy-done.2, bf16[2,2,288,512]{3,2,1,0:T(8,128)(2,1)} %bitcast.50, ...), custom_call_target="tpu_custom_call" | custom-call | flops 1000 | bytes 1000 | tf_op jit(solution)/shard_map/combine/pallas_call | solution.py:752
  194.5 4.5 %add_convert_fusion = bf16[512,1024]{1,0:T(8,128)(2,1)} fusion(f32[512,1024]{1,0:T(8,128)} %collective-permute-done.15, f32[512,1024]{1,0:T(8,128)} %get-tuple-element.95, f32[528,1024]{1,0:T(8,128)} %get-tuple-element.91.hidden), kind=kLoop, calls=%fused_computation | loop fusion | flops 1572864 | bytes 7340032 | tf_op jit(solution)/shard_map/convert_element_type | solution.py:1095
  199.0 11.4 %collective-permute-done.23 = bf16[1,288,1024]{2,1,0:T(8,128)(2,1)S(1)} collective-permute-done((bf16[1,288,1024]{2,1,0:T(8,128)(2,1)}, bf16[1,288,1024]{2,1,0:T(8,128)(2,1)S(1)}, u32[]{:S(2)}, u32[]{:S(2)}) %collective-permute-start.23) | collective-permute-done | bytes 589856 | tf_op jit(solution)/shard_map/ppermute | solution.py:33
  211.3 3.8 %settle.2 = (f32[288,1024]{1,0:T(8,128)}, bf16[288,1024]{1,0:T(8,128)(2,1)}) custom-call(s32[6]{0:T(128)} %stack.32.info, bf16[2,2,288,512]{3,2,1,0:T(8,128)(2,1)} %bitcast.48, bf16[2,2,288,512]{3,2,1,0:T(8,128)(2,1)} %bitcast.13.refs_1_, bf16[2,288,512]{2,1,0:T(8,128)(2,1)} %copy-done.2, bf16[288,1024]{1,0:T(8,128)(2,1)} %bitcast.75, ...), custom_call_target="tpu_custom_call" | custom-call | flops 1000 | bytes 1000 | tf_op jit(solution)/shard_map/settle/pallas_call | solution.py:829
  216.4 3.8 %combine.14 = (bf16[4,32,2048]{2,1,0:T(8,128)(2,1)}, bf16[4,32,2176]{2,1,0:T(8,128)(2,1)}) custom-call(s32[6]{0:T(128)} %stack.32.info, bf16[2,2,2,2,32,1024]{5,4,3,2,1,0:T(8,128)(2,1)} %bitcast.53, bf16[2,2,2,2,32,4224]{5,4,3,2,1,0:T(8,128)(2,1)} %bitcast.17.refs_1_.refs_3_.refs_5_.refs_7_.refs_9_.refs_4_.refs_10_.refs_13_.refs_17_, ...), custom_call_target="tpu_custom_call" | custom-call | flops 1000 | bytes 1000 | tf_op jit(solution)/shard_map/combine/pallas_call | solution.py:752
  221.8 2.6 combine.15
  224.8 2.0 collective-permute-start.27
  226.8 10.2 %collective-permute-done.24 = bf16[4,32,2048]{2,1,0:T(8,128)(2,1)} collective-permute-done((bf16[4,32,2048]{2,1,0:T(8,128)(2,1)}, bf16[4,32,2048]{2,1,0:T(8,128)(2,1)}, u32[]{:S(2)}, u32[]{:S(2)}) %collective-permute-start.24) | collective-permute-done | bytes 524320 | tf_op jit(solution)/shard_map/ppermute | solution.py:33
  237.8 4.2 %combine.16 = bf16[4,32,4224]{2,1,0:T(8,128)(2,1)} custom-call(s32[6]{0:T(128)} %stack.32.info, bf16[2,2,2,2,32,1024]{5,4,3,2,1,0:T(8,128)(2,1)} %bitcast.54, bf16[2,2,2,2,32,4224]{5,4,3,2,1,0:T(8,128)(2,1)} %bitcast.17.refs_1_.refs_3_.refs_5_.refs_7_.refs_9_.refs_4_.refs_10_.refs_13_.refs_17_, bf16[2,2,2,32,2048]{4,3,2,1,0:T(8,128)(2,1)} %bitcast.26.refs_2_.refs_5_.refs_6_, ...), custom_call_target="tpu_custom_call" | custom-call | flops 1000 | bytes 1000 | tf_op jit(solution)/shard_map/combine/pallas_call | solution.py:752
  242.8 2.6 combine.17
  252.0 3.3 %finish.1 = (f32[32,4608]{1,0:T(8,128)}, f32[32,4608]{1,0:T(8,128)}) custom-call(s32[6]{0:T(128)} %stack.32.info, bf16[64,2048]{1,0:T(8,128)(2,1)} %reduce-scatter.8.cloned.1.call-done.refs_0_, bf16[2,2,64,2560]{3,2,1,0:T(8,128)(2,1)} %bitcast.44, bf16[2,64,1280]{2,1,0:T(8,128)(2,1)} %copy-done.4, bf16[64,1280]{1,0:T(8,128)(2,1)} %bitcast.80, ...), custom_call_target="tpu_custom_call" | custom-call | flops 1000 | bytes 1000 | tf_op jit(solution)/shard_map/finish/pallas_call | solution.py:851
  256.4 2.0 bitcast_select_fusion
  259.6 17.8 %reduce-scatter.6.cloned.1.call-done.refs_0_.refs_1_.refs_2_.refs_3_.refs_4_ = bf16[32,4224]{1,0:T(8,128)(2,1)} async-done(((bf16[128,4224]{1,0:T(8,128)(2,1)}), bf16[32,4224]{1,0:T(8,128)(2,1)}) %reduce-scatter.6.cloned.1.call-update) | async-done | bytes 270352 | tf_op jit(solution)/shard_map/reduce_scatter | solution.py:989
  277.3 2.4 settle.3
  (109 shorter events, 45.8 us)
Async XLA Ops:
  7.2 214.7 %reduce-scatter.4.cloned.1.call-start = ((), (), s32[]{:S(2)}) async-start(), calls=%async_computation.3 | async-start | bytes 6553600 | tf_op jit(solution)/shard_map/reduce_scatter | solution.py:961
  7.2 40.3 %collective-permute-start.8 = (bf16[512,4608]{1,0:T(8,128)(2,1)}, bf16[512,4608]{1,0:T(8,128)(2,1)}, u32[]{:S(2)}, u32[]{:S(2)}) collective-permute-start(bf16[512,4608]{1,0:T(8,128)(2,1)} %gate_own.1), channel_id=1, source_target_pairs={{0,1},{1,0},{2,3},{3,2},{4,5},{5,4},{6,7},{7,6},{8,9},{9,8},{10,11... | collective-permute-start | bytes 14155784 | tf_op jit(solution)/shard_map/ppermute | solution.py:28
  7.7 39.8 %collective-permute-start.9 = (bf16[512,4608]{1,0:T(8,128)(2,1)}, bf16[512,4608]{1,0:T(8,128)(2,1)}, u32[]{:S(2)}, u32[]{:S(2)}) collective-permute-start(bf16[512,4608]{1,0:T(8,128)(2,1)} %up_own.1), channel_id=1, source_target_pairs={{0,1},{1,0},{2,3},{3,2},{4,5},{5,4},{6,7},{7,6},{8,9},{9,8},{10,11... | collective-permute-start | bytes 14155784 | tf_op jit(solution)/shard_map/ppermute | solution.py:28
  7.8 20.6 %collective-permute-start.3 = (bf16[512,3072]{1,0:T(8,128)(2,1)}, bf16[512,3072]{1,0:T(8,128)(2,1)}, u32[]{:S(2)}, u32[]{:S(2)}) collective-permute-start(bf16[512,3072]{1,0:T(8,128)(2,1)} %own_x.3), channel_id=1, source_target_pairs={{0,1},{1,0},{2,3},{3,2},{4,5},{5,4},{6,7},{7,6},{8,9},{9,8},{10,11... | collective-permute-start | bytes 9437192 | tf_op jit(solution)/shard_map/ppermute | solution.py:28
  10.3 5.0 %collective-permute-start.2 = (bf16[8,512]{1,0:T(8,128)(2,1)S(1)}, bf16[8,512]{1,0:T(8,128)(2,1)S(1)}, u32[]{:S(2)}, u32[]{:S(2)}) collective-permute-start(bf16[8,512]{1,0:T(8,128)(2,1)S(1)} %fusion.5), channel_id=1, source_target_pairs={{0,1},{1,0},{2,3},{3,2},{4,5},{5,4},{6,7},{7,6},{8,9},{9,8},{10,11... | collective-permute-start | bytes 24584 | tf_op jit(solution)/shard_map/ppermute | solution.py:28
  10.5 18.0 %collective-permute-start.4 = (bf16[512,1024]{1,0:T(8,128)(2,1)}, bf16[512,1024]{1,0:T(8,128)(2,1)}, u32[]{:S(2)}, u32[]{:S(2)}) collective-permute-start(bf16[512,1024]{1,0:T(8,128)(2,1)} %out_own.3), channel_id=1, source_target_pairs={{0,1},{1,0},{2,3},{3,2},{4,5},{5,4},{6,7},{7,6},{8,9},{9,8},{10,11... | collective-permute-start | bytes 3145736 | tf_op jit(solution)/shard_map/ppermute | solution.py:28
  15.3 6.8 %collective-permute-start = (bf16[16,1024]{1,0:T(8,128)(2,1)S(1)}, bf16[16,1024]{1,0:T(8,128)(2,1)S(1)}, u32[]{:S(2)}, u32[]{:S(2)}) collective-permute-start(bf16[16,1024]{1,0:T(8,128)(2,1)S(1)} %get-tuple-element.217), channel_id=1, source_target_pairs={{0,1},{1,2},{2,3},{3,4},{4,5},{5,6},{6,7},{7,8},{8,9},{9,10},{10,1... | collective-permute-start | bytes 98312 | tf_op jit(solution)/shard_map/ppermute | solution.py:24
  42.4 5.1 %collective-permute-start.5 = (bf16[528,1024]{1,0:T(8,128)(2,1)}, bf16[528,1024]{1,0:T(8,128)(2,1)}, u32[]{:S(2)}, u32[]{:S(2)}) collective-permute-start(bf16[528,1024]{1,0:T(8,128)(2,1)} %get-tuple-element.93), channel_id=1, source_target_pairs={{0,1},{1,0},{2,3},{3,2},{4,5},{5,4},{6,7},{7,6},{8,9},{9,8},{10,11... | collective-permute-start | bytes 3244040 | tf_op jit(solution)/shard_map/ppermute | solution.py:28
  99.5 150.9 %reduce-scatter.8.cloned.1.call-start = ((), (), s32[]{:S(2)}) async-start(), calls=%async_computation.5 | async-start | bytes 1310720 | tf_op jit(solution)/shard_map/reduce_scatter | solution.py:989
  99.6 29.3 %collective-permute-start.10 = (f32[528,1024]{1,0:T(8,128)}, f32[528,1024]{1,0:T(8,128)}, u32[]{:S(2)}, u32[]{:S(2)}) collective-permute-start(f32[528,1024]{1,0:T(8,128)} %get-tuple-element.97), channel_id=1, source_target_pairs={{0,1},{1,0},{2,3},{3,2},{4,5},{5,4},{6,7},{7,6},{8,9},{9,8},{10,11... | collective-permute-start | bytes 6488072 | tf_op jit(solution)/shard_map/ppermute | solution.py:28
  100.0 26.7 %collective-permute-start.11 = (bf16[8,64,1024]{2,1,0:T(8,128)(2,1)}, bf16[8,64,1024]{2,1,0:T(8,128)(2,1)}, u32[]{:S(2)}, u32[]{:S(2)}) collective-permute-start(bf16[8,64,1024]{2,1,0:T(8,128)(2,1)} %get-tuple-element.103), channel_id=1, source_target_pairs={{0,2},{2,0},{4,6},{6,4},{8,10},{10,8},{12,14},{14,12},{16,18},{18,... | collective-permute-start | bytes 3145736 | tf_op jit(solution)/shard_map/ppermute | solution.py:33
  102.9 25.9 %collective-permute-start.12 = (bf16[4,128,1024]{2,1,0:T(8,128)(2,1)}, bf16[4,128,1024]{2,1,0:T(8,128)(2,1)}, u32[]{:S(2)}, u32[]{:S(2)}) collective-permute-start(bf16[4,128,1024]{2,1,0:T(8,128)(2,1)} %get-tuple-element.104), channel_id=1, source_target_pairs={{0,4},{2,6},{4,0},{6,2},{8,12},{10,14},{12,8},{14,10},{16,20},{18,... | collective-permute-start | bytes 3145736 | tf_op jit(solution)/shard_map/ppermute | solution.py:33
  128.8 32.5 %collective-permute-start.15 = (f32[512,1024]{1,0:T(8,128)}, f32[512,1024]{1,0:T(8,128)}, u32[]{:S(2)}, u32[]{:S(2)}) collective-permute-start(f32[512,1024]{1,0:T(8,128)} %get-tuple-element.124), channel_id=1, source_target_pairs={{0,1},{1,0},{2,3},{3,2},{4,5},{5,4},{6,7},{7,6},{8,9},{9,8},{10,11... | collective-permute-start | bytes 6291464 | tf_op jit(solution)/shard_map/ppermute | solution.py:28
  128.8 32.5 %collective-permute-start.13 = (bf16[4,288,512]{2,1,0:T(8,128)(2,1)}, bf16[4,288,512]{2,1,0:T(8,128)(2,1)}, u32[]{:S(2)}, u32[]{:S(2)}) collective-permute-start(bf16[4,288,512]{2,1,0:T(8,128)(2,1)} %get-tuple-element.122), channel_id=1, source_target_pairs={{0,2},{2,0},{4,6},{6,4},{8,10},{10,8},{12,14},{14,12},{16,18},{18,... | collective-permute-start | bytes 3538952 | tf_op jit(solution)/shard_map/ppermute | solution.py:33
  129.1 32.2 %collective-permute-start.14 = (bf16[2,576,512]{2,1,0:T(8,128)(2,1)}, bf16[2,576,512]{2,1,0:T(8,128)(2,1)}, u32[]{:S(2)}, u32[]{:S(2)}) collective-permute-start(bf16[2,576,512]{2,1,0:T(8,128)(2,1)} %get-tuple-element.123), channel_id=1, source_target_pairs={{0,4},{2,6},{4,0},{6,2},{8,12},{10,14},{12,8},{14,10},{16,20},{18,... | collective-permute-start | bytes 3538952 | tf_op jit(solution)/shard_map/ppermute | solution.py:33
  161.3 7.8 %collective-permute-start.20 = (bf16[16,32,4224]{2,1,0:T(8,128)(2,1)}, bf16[16,32,4224]{2,1,0:T(8,128)(2,1)}, u32[]{:S(2)}, u32[]{:S(2)}) collective-permute-start(bf16[16,32,4224]{2,1,0:T(8,128)(2,1)} %get-tuple-element.133), channel_id=1, source_target_pairs={{0,1},{1,0},{2,3},{3,2},{4,5},{5,4},{6,7},{7,6},{8,9},{9,8},{10,11... | collective-permute-start | bytes 12976136 | tf_op jit(solution)/shard_map/ppermute | solution.py:28
  161.4 15.1 %collective-permute-start.18 = (bf16[4,64,1024]{2,1,0:T(8,128)(2,1)}, bf16[4,64,1024]{2,1,0:T(8,128)(2,1)}, u32[]{:S(2)}, u32[]{:S(2)}) collective-permute-start(bf16[4,64,1024]{2,1,0:T(8,128)(2,1)} %get-tuple-element.110), channel_id=1, source_target_pairs={{0,4},{2,6},{4,0},{6,2},{8,12},{10,14},{12,8},{14,10},{16,20},{18,... | collective-permute-start | bytes 1572872 | tf_op jit(solution)/shard_map/ppermute | solution.py:33
  161.6 15.1 %collective-permute-start.19 = (bf16[4,64,1024]{2,1,0:T(8,128)(2,1)}, bf16[4,64,1024]{2,1,0:T(8,128)(2,1)}, u32[]{:S(2)}, u32[]{:S(2)}) collective-permute-start(bf16[4,64,1024]{2,1,0:T(8,128)(2,1)} %get-tuple-element.111), channel_id=1, source_target_pairs={{0,2},{2,0},{4,6},{6,4},{8,10},{10,8},{12,14},{14,12},{16,18},{18,... | collective-permute-start | bytes 1572872 | tf_op jit(solution)/shard_map/ppermute | solution.py:33
  166.6 22.4 %collective-permute-start.16 = (bf16[2,288,512]{2,1,0:T(8,128)(2,1)}, bf16[2,288,512]{2,1,0:T(8,128)(2,1)S(1)}, u32[]{:S(2)}, u32[]{:S(2)}) collective-permute-start(bf16[2,288,512]{2,1,0:T(8,128)(2,1)} %get-tuple-element.130), channel_id=1, source_target_pairs={{0,4},{2,6},{4,0},{6,2},{8,12},{10,14},{12,8},{14,10},{16,20},{18,... | collective-permute-start | bytes 1769480 | tf_op jit(solution)/shard_map/ppermute | solution.py:33
  168.3 21.0 %collective-permute-start.17 = (bf16[2,288,512]{2,1,0:T(8,128)(2,1)}, bf16[2,288,512]{2,1,0:T(8,128)(2,1)}, u32[]{:S(2)}, u32[]{:S(2)}) collective-permute-start(bf16[2,288,512]{2,1,0:T(8,128)(2,1)} %get-tuple-element.131), channel_id=1, source_target_pairs={{0,2},{2,0},{4,6},{6,4},{8,10},{10,8},{12,14},{14,12},{16,18},{18,... | collective-permute-start | bytes 1769480 | tf_op jit(solution)/shard_map/ppermute | solution.py:33
  173.2 43.1 %collective-permute-start.22 = (bf16[8,32,2176]{2,1,0:T(8,128)(2,1)}, bf16[8,32,2176]{2,1,0:T(8,128)(2,1)}, u32[]{:S(2)}, u32[]{:S(2)}) collective-permute-start(bf16[8,32,2176]{2,1,0:T(8,128)(2,1)} %get-tuple-element.140), channel_id=1, source_target_pairs={{0,4},{2,6},{4,0},{6,2},{8,12},{10,14},{12,8},{14,10},{16,20},{18,... | collective-permute-start | bytes 3342344 | tf_op jit(solution)/shard_map/ppermute | solution.py:33
  180.3 97.0 %reduce-scatter.6.cloned.1.call-start = ((), (), s32[]{:S(2)}) async-start(), calls=%async_computation.4 | async-start | bytes 1351680 | tf_op jit(solution)/shard_map/reduce_scatter | solution.py:989
  180.6 35.8 %collective-permute-start.21 = (bf16[8,32,2048]{2,1,0:T(8,128)(2,1)}, bf16[8,32,2048]{2,1,0:T(8,128)(2,1)}, u32[]{:S(2)}, u32[]{:S(2)}) collective-permute-start(bf16[8,32,2048]{2,1,0:T(8,128)(2,1)} %get-tuple-element.139), channel_id=1, source_target_pairs={{0,2},{2,0},{4,6},{6,4},{8,10},{10,8},{12,14},{14,12},{16,18},{18,... | collective-permute-start | bytes 3145736 | tf_op jit(solution)/shard_map/ppermute | solution.py:33
  192.9 17.5 %collective-permute-start.23 = (bf16[1,288,1024]{2,1,0:T(8,128)(2,1)}, bf16[1,288,1024]{2,1,0:T(8,128)(2,1)S(1)}, u32[]{:S(2)}, u32[]{:S(2)}) collective-permute-start(bf16[1,288,1024]{2,1,0:T(8,128)(2,1)} %combine.13), channel_id=1, source_target_pairs={{0,8},{2,10},{4,12},{6,14},{8,0},{10,2},{12,4},{14,6},{16,24},{18,... | collective-permute-start | bytes 1769480 | tf_op jit(solution)/shard_map/ppermute | solution.py:33
  215.0 27.0 %collective-permute-start.31 = (bf16[288,1024]{1,0:T(8,128)(2,1)}, bf16[288,1024]{1,0:T(8,128)(2,1)}, u32[]{:S(2)}, u32[]{:S(2)}) collective-permute-start(bf16[288,1024]{1,0:T(8,128)(2,1)} %get-tuple-element.149), channel_id=1, source_target_pairs={{1,17},{3,19},{5,21},{7,23},{9,25},{11,27},{13,29},{15,31},{16,0},... | collective-permute-start | bytes 1769480 | tf_op jit(solution)/shard_map/ppermute | solution.py:1105
  220.1 16.9 %collective-permute-start.25 = (bf16[4,32,2176]{2,1,0:T(8,128)(2,1)}, bf16[4,32,2176]{2,1,0:T(8,128)(2,1)S(1)}, u32[]{:S(2)}, u32[]{:S(2)}) collective-permute-start(bf16[4,32,2176]{2,1,0:T(8,128)(2,1)} %get-tuple-element.153), channel_id=1, source_target_pairs={{0,2},{2,0},{4,6},{6,4},{8,10},{10,8},{12,14},{14,12},{16,18},{18,... | collective-permute-start | bytes 1671176 | tf_op jit(solution)/shard_map/ppermute | solution.py:33
  221.8 15.2 %collective-permute-start.24 = (bf16[4,32,2048]{2,1,0:T(8,128)(2,1)}, bf16[4,32,2048]{2,1,0:T(8,128)(2,1)}, u32[]{:S(2)}, u32[]{:S(2)}) collective-permute-start(bf16[4,32,2048]{2,1,0:T(8,128)(2,1)} %get-tuple-element.152), channel_id=1, source_target_pairs={{0,4},{2,6},{4,0},{6,2},{8,12},{10,14},{12,8},{14,10},{16,20},{18,... | collective-permute-start | bytes 1572872 | tf_op jit(solution)/shard_map/ppermute | solution.py:33
  224.4 17.6 %collective-permute-start.26 = (bf16[2,64,1280]{2,1,0:T(8,128)(2,1)}, bf16[2,64,1280]{2,1,0:T(8,128)(2,1)S(1)}, u32[]{:S(2)}, u32[]{:S(2)}) collective-permute-start(bf16[2,64,1280]{2,1,0:T(8,128)(2,1)} %get-tuple-element.156), channel_id=1, source_target_pairs={{0,2},{2,0},{4,6},{6,4},{8,10},{10,8},{12,14},{14,12},{16,18},{18,... | collective-permute-start | bytes 983048 | tf_op jit(solution)/shard_map/ppermute | solution.py:33
  224.8 17.4 %collective-permute-start.27 = (bf16[2,64,1280]{2,1,0:T(8,128)(2,1)}, bf16[2,64,1280]{2,1,0:T(8,128)(2,1)}, u32[]{:S(2)}, u32[]{:S(2)}) collective-permute-start(bf16[2,64,1280]{2,1,0:T(8,128)(2,1)} %get-tuple-element.157), channel_id=1, source_target_pairs={{0,4},{2,6},{4,0},{6,2},{8,12},{10,14},{12,8},{14,10},{16,20},{18,... | collective-permute-start | bytes 983048 | tf_op jit(solution)/shard_map/ppermute | solution.py:33
  245.4 5.5 %collective-permute-start.28 = (bf16[1,64,1280]{2,1,0:T(8,128)(2,1)}, bf16[1,64,1280]{2,1,0:T(8,128)(2,1)S(1)}, u32[]{:S(2)}, u32[]{:S(2)}) collective-permute-start(bf16[1,64,1280]{2,1,0:T(8,128)(2,1)} %get-tuple-element.165), channel_id=1, source_target_pairs={{0,4},{2,6},{4,0},{6,2},{8,12},{10,14},{12,8},{14,10},{16,20},{18,... | collective-permute-start | bytes 491528 | tf_op jit(solution)/shard_map/ppermute | solution.py:33
  245.5 5.9 %collective-permute-start.29 = (bf16[1,64,1280]{2,1,0:T(8,128)(2,1)}, bf16[1,64,1280]{2,1,0:T(8,128)(2,1)S(1)}, u32[]{:S(2)}, u32[]{:S(2)}) collective-permute-start(bf16[1,64,1280]{2,1,0:T(8,128)(2,1)} %get-tuple-element.166), channel_id=1, source_target_pairs={{0,2},{2,0},{4,6},{6,4},{8,10},{10,8},{12,14},{14,12},{16,18},{18,... | collective-permute-start | bytes 491528 | tf_op jit(solution)/shard_map/ppermute | solution.py:33
  250.3 6.1 %collective-permute-start.32 = (f32[144,1024]{1,0:T(8,128)}, f32[144,1024]{1,0:T(8,128)S(1)}, u32[]{:S(2)}, u32[]{:S(2)}) collective-permute-start(f32[144,1024]{1,0:T(8,128)} %dynamic-slice_bitcast_fusion), channel_id=1, source_target_pairs={{0,1},{1,0},{2,3},{3,2},{4,5},{5,4},{6,7},{7,6},{8,9},{9,8},{10,11... | collective-permute-start | bytes 1769480 | tf_op jit(solution)/shard_map/ppermute | solution.py:28
  (14 other events, 29.7 us)
Sparse Core Ops, SparseCore 0:
  99.6 96.3 reduce-scatter.3
  198.3 30.3 reduce-scatter.7
  250.5 26.7 reduce-scatter.5

commit v2 on v1

--- a/solution.py
+++ b/solution.py
@@ -803,6 +803,20 @@
     refs = list(refs)
     inputs = [[[refs.pop(0) for _ in range(count)] for count in counts] for counts, _ in plan]
     for members, (_, kinds) in zip(inputs, plan):
+        if kinds is None:
+            rows = members[0][0].shape[0]
+            value = members[0][0][...].astype(jnp.float32)
+            for term in members[0][1:]:
+                value = value + term[...].astype(jnp.float32)
+            across_rows = lax.broadcasted_iota(jnp.int32, (rows, rows), 0)
+            across_columns = lax.broadcasted_iota(jnp.int32, (rows, rows), 1)
+            for column in range(2):
+                diagonal = jnp.where(
+                    across_rows == across_columns, value[:, column : column + 1], 0.0
+                )
+                refs.pop(0)[...] = jnp.sum(diagonal, axis=0, keepdims=True)
+            refs.pop(0)[...] = value[:, 2:5]
+            continue
         outs = [refs.pop(0) for _ in kinds]
         edge = 0
         for terms in members:
@@ -824,7 +838,11 @@
             specs += view_specs
         rows = views[0].shape[-2]
         width = sum(terms[0][3] for terms in members)
-        shapes += [jax.ShapeDtypeStruct((rows, width), kind) for kind in kinds]
+        if kinds is None:
+            shapes += [jax.ShapeDtypeStruct((1, rows), jnp.float32)] * 2
+            shapes.append(jax.ShapeDtypeStruct((rows, 3), jnp.float32))
+        else:
+            shapes += [jax.ShapeDtypeStruct((rows, width), kind) for kind in kinds]
         plan.append(([len(terms) for terms in members], kinds))
     return pl.pallas_call(
         functools.partial(settle_kernel, plan),
@@ -901,24 +919,31 @@
         )
 
     w_in_other = partner(in_weight)
+    w_out_other = partner(out_weight)
     small = jnp.concatenate([norm_gain[None], ffn_gain[None], conv_taps.T], axis=0)
     small = jnp.pad(small, ((0, 3), (0, 0)))
-    small = both(small, partner(small), 1).astype(jnp.float32)
+    small_other = partner(small)
     before_rows = shifted(tokens[rows - HALO :], 1)
     after_rows = shifted(jnp.concatenate([tokens[:HALO], cotangent[:HALO]], axis=1), -1)
-    w_out_other = partner(out_weight)
     cot_other = partner(cotangent)
     after_other = partner(after_rows)
-    gate_other = partner(gate_weight)
-    up_other = partner(up_weight)
+    early = (w_in_other, w_out_other, small_other, before_rows, cot_other, after_other)
+    w_in_other, w_out_other, small_other, before_rows, cot_other, after_other = ordering(early)
+    small = both(small, small_other, 1).astype(jnp.float32)
+    gate_late, up_late = after((gate_weight, up_weight), early)
+    gate_other = partner(gate_late)
+    up_other = partner(up_late)
 
     place = lax.axis_index(AXES) * rows + jnp.arange(rows + HALO, dtype=jnp.int32)
-    starts = jnp.cumsum(doc_lengths) - doc_lengths
+    earlier = jnp.arange(doc_lengths.shape[0])
+    earlier = earlier[:, None] < earlier[None, :]
+    starts = jnp.sum(jnp.where(earlier, doc_lengths[:, None], 0), axis=0)
     first = jnp.any(place[:, None] == starts[None, :], axis=1)
     before = jnp.any((place - 1)[:, None] == starts[None, :], axis=1)
     keep_one = jnp.where(first, 0.0, 1.0)
     keep_two = jnp.where(jnp.logical_or(first, before), 0.0, 1.0)
-    keeps = jnp.stack([keep_one, keep_two], axis=1).astype(jnp.float32)
+    lane = lax.broadcasted_iota(jnp.int32, (rows + HALO, 128), 1)
+    keeps = jnp.where(lane == 0, keep_one[:, None], keep_two[:, None]).astype(jnp.float32)
     info = [core] + [coords[bit] for bit in lower] + [coords[top], turned[top]]
     info = jnp.stack(info).astype(jnp.int32)
 
@@ -935,6 +960,7 @@
         w_out_other,
     )
     norm_other = partner(norm_send)
+    norm_own, gate_other, up_other = ordering((norm_own, gate_other, up_other))
     per_chip = width // chips
     pers = (per_chip << lower[0], per_chip << lower[1])
     tiles = hidden // TILE
@@ -1091,10 +1117,8 @@
         for terms, got, order in zip(down_terms, down_got, orders)
     ]
     down_sent, down_streams = side_by_side(down_streams, lower[2:])
-    out_came = after(out_came, down_sent)
-    block_out = (hidden_res[:rows] + out_keep + out_came).astype(jnp.bfloat16)
-
-    down_streams = gated(down_streams, block_out)
+
+    down_streams = gated(down_streams, down_sent)
     part, down_last = settle(info, slots, [(down_streams, (jnp.float32, jnp.bfloat16))])
     pairs = [
         (source * 2 + side, (source ^ (1 << top)) * 2 + side)
@@ -1123,7 +1147,9 @@
         [(order[0], [terms]) for terms, order in zip(two_terms, orders)], bits[2:]
     )
     two_got = [got for got, _ in two_got]
-    conv_two = after(conv_two, two_sent)
+    out_came = after(out_came, two_sent)
+    block_out = (hidden_res[:rows] + out_keep + out_came).astype(jnp.bfloat16)
+    conv_two = after(conv_two, two_sent, block_out)
     conv_streams = []
     for members, got, order in zip(conv_members, conv_two, orders):
         edge = 0
@@ -1155,13 +1181,13 @@
         [(conv_done, [], member * width // size, size)]
         for member, size in enumerate([width] * 4 + [128])
     )
-    in_out, out_out, vectors = settle(
+    in_out, out_out, gain_one_out, gain_two_out, taps_out = settle(
         info,
         slots,
         [
             ([b_out, c_out, x_out], (jnp.float32,)),
             ([out_out], (jnp.float32,)),
-            ([vectors], (jnp.float32,)),
+            ([vectors], None),
         ],
     )
 
@@ -1175,11 +1201,11 @@
     return (
         block_out,
         input_grad,
-        vectors[:, 0],
+        gain_one_out.reshape(-1),
         in_out,
-        vectors[:, 2:5],
+        taps_out,
         out_out,
-        vectors[:, 1],
+        gain_two_out.reshape(-1),
         gate_out,
         up_out,
         down_out,

time: 290 us -> 285 us (0.983)
  waiting for transfers between devices: 69.3 us -> 62.1 us
  starting transfers between devices: 29.4 us -> 34.2 us
  local copies, waits for them, and re-layouts: 14.5 us -> 11.4 us
    ppermute x13, starting transfers between devices: 3.41 us -> 8.4 us  [partner(): return lax.ppermute(value, 'wa', [(0, 1), (1, 0)])]
    ppermute x2, waiting for transfers between devices: 5.6 us -> 1.51 us  [shifted(): lax.ppermute(value, AXES, [(source, source + steps) for source in range(f...]
  transfers between devices with their start and end apart: 36 -> 36, of which waited for: 19 -> 16; matrix products, arithmetic and copies ran while one was open for 6% -> 6% of each run, Pallas kernels for 33% -> 34%
where the time goes in v2:
time: 285 us; the launch traced here: 284 us
  Pallas kernels  150 us (53%)
  waiting for transfers between devices  62.1 us (22%)
  starting transfers between devices  34.2 us (12%)
  between operations  14 us (5%)
  other arithmetic  12.2 us (4%)
  local copies, waits for them, and re-layouts  11.4 us (4%)
    pallas_call x1, Pallas kernels, ffn(): pl.pallas_call(functools.partial(ffn_kernel, 2, split), out_shape=shapes,...  51.9 us
    ppermute x17, waiting for transfers between devices, across(): lax.ppermute(value, 'seq', [(place, place ^ 1 << bit) for place in range(...  39 us
    pallas_call x9, Pallas kernels, combine(): pl.pallas_call(functools.partial(combine_kernel, plan), out_shape=shapes,...  30.3 us
    pallas_call x1, Pallas kernels, conv_backward(): pl.pallas_call(backward_kernel, out_shape=[jax.ShapeDtypeStruct((rows, wi...  27.2 us
    ppermute x17, starting transfers between devices, across(): lax.ppermute(value, 'seq', [(place, place ^ 1 << bit) for place in range(...  20.8 us
    pallas_call x1, Pallas kernels, down_part(): pl.pallas_call(down_kernel, out_shape=shapes, grid_spec=pltpu.PrefetchSca...  17.6 us
    reduce_scatter x2, waiting for transfers between devices, upper_sum(): lax.psum_scatter(value, 'seq', scatter_dimension=0, axis_index_groups=gro...  17.3 us
    pallas_call x1, Pallas kernels, conv_forward(): pl.pallas_call(forward_kernel, out_shape=[jax.ShapeDtypeStruct((ext + HAL...  13.9 us
  transfers between devices with their start and end apart: 36, of which 16 were waited for; matrix products, arithmetic and copies ran while one was open for 6% of the time, Pallas kernels for 34%

profile of v2, /device:TPU:0, one launch (start us, length us, event | category | flops | bytes accessed | tf_op | source)
XLA Modules:
  0.0 284.2 jit_solution(3233409254899706754)
XLA Ops:
  13.1 3.2 %collective-permute-start.6 = (bf16[16,2048]{1,0:T(8,128)(2,1)S(1)}, bf16[16,2048]{1,0:T(8,128)(2,1)S(1)}, u32[]{:S(2)}, u32[]{:S(2)}) collective-permute-start(bf16[16,2048]{1,0:T(8,128)(2,1)S(1)} %collective-permute-done.5.after.g_after), channel_id=1, source_target_pairs={{0,1},{1,0},{2,3},{3,2},{4,5},{5,4},{6,7},{7,6},{8,9},{9,8},{10,11... | collective-permute-start | bytes 196616 | tf_op jit(solution)/shard_map/ppermute | solution.py:28
  18.3 2.1 collective-permute-start.3
  21.2 3.1 %collective-permute-start.7 = (bf16[512,4608]{1,0:T(8,128)(2,1)}, bf16[512,4608]{1,0:T(8,128)(2,1)}, u32[]{:S(2)}, u32[]{:S(2)}) collective-permute-start(bf16[512,4608]{1,0:T(8,128)(2,1)} %gate_own.1), channel_id=1, source_target_pairs={{0,1},{1,0},{2,3},{3,2},{4,5},{5,4},{6,7},{7,6},{8,9},{9,8},{10,11... | collective-permute-start | bytes 14155784 | tf_op jit(solution)/shard_map/ppermute | solution.py:28
  27.5 13.9 %conv_forward.1 = (f32[544,1024]{1,0:T(8,128)}, f32[544,1024]{1,0:T(8,128)}, f32[544,1024]{1,0:T(8,128)}, f32[528,1024]{1,0:T(8,128)}, bf16[528,1024]{1,0:T(8,128)(2,1)}, /*index=5*/bf16[528,1024]{1,0:T(8,128)(2,1)}) custom-call(s32[6]{0:T(128)} %stack.27.info, bf16[512,1024]{1,0:T(8,128)(2,1)} %tokens.3, bf16[16,1024]{1,0:T(8,128)(2,1)} %copy-done.9, ...), custom_call_target="tpu_custom_call" | custom-call | flops 1000 | bytes 1000 | tf_op jit(solution)/shard_map/conv_forward/pallas_call | solution.py:191
  41.9 2.7 collective-permute-done.9.n_other
  44.6 51.9 %ffn.1 = (bf16[1056,2304]{1,0:T(8,128)(2,1)}, f32[528,1024]{1,0:T(8,128)}, f32[528,1024]{1,0:T(8,128)}, bf16[8,64,1024]{2,1,0:T(8,128)(2,1)}, bf16[8,64,1024]{2,...) custom-call(s32[6]{0:T(128)} %stack.27.info, ...), custom_call_target="tpu_custom_call" | custom-call | flops 1000 | bytes 1000 | tf_op jit(solution)/shard_map/ffn/pallas_call | solution.py:581
  97.0 2.4 collective-permute-start.11
  99.4 2.4 collective-permute-start.12
  101.9 17.6 %down.1 = (f32[512,1024]{1,0:T(8,128)}, f32[512,1024]{1,0:T(8,128)}, bf16[4,288,512]{2,1,0:T(8,128)(2,1)}, bf16[4,288,512]{2,1,0:T(8,128)(2,1)}, bf16[2,576,512]...) custom-call(s32[6]{0:T(128)} %stack.27.info, bf16[1056,2304]{1,0:T(8,128)(2,1)} %get-tuple-element.118.act, ...), custom_call_target="tpu_custom_call" | custom-call | flops 1000 | bytes 1000 | tf_op jit(solution)/shard_map/down/pallas_call | solution.py:666
  119.5 4.0 %collective-permute-done.11 = bf16[8,64,1024]{2,1,0:T(8,128)(2,1)} collective-permute-done((bf16[8,64,1024]{2,1,0:T(8,128)(2,1)}, bf16[8,64,1024]{2,1,0:T(8,128)(2,1)}, u32[]{:S(2)}, u32[]{:S(2)}) %collective-permute-start.11) | collective-permute-done | bytes 1048608 | tf_op jit(solution)/shard_map/ppermute | solution.py:33
  123.4 2.1 collective-permute-done.12
  127.7 3.1 %combine.9 = (bf16[4,64,1024]{2,1,0:T(8,128)(2,1)}, bf16[4,64,1024]{2,1,0:T(8,128)(2,1)}) custom-call(s32[6]{0:T(128)} %stack.27.info, bf16[2,2,2,64,1024]{4,3,2,1,0:T(8,128)(2,1)} %bitcast.71, bf16[2,2,2,64,1024]{4,3,2,1,0:T(8,128)(2,1)} %bitcast.8.refs_1_, bf16[2,2,2,64,1024]{4,3,2,1,0:T(8,128)(2,1)} %bitcast.73, ...), custom_call_target="tpu_custom_call" | custom-call | flops 1000 | bytes 1000 | tf_op jit(solution)/shard_map/combine/pallas_call | solution.py:752
  130.8 27.2 %conv_backward.1 = (bf16[512,1024]{1,0:T(8,128)(2,1)}, bf16[16,32,4224]{2,1,0:T(8,128)(2,1)}, bf16[16,32,1024]{2,1,0:T(8,128)(2,1)}, bf16[16,32,1024]{2,1,0:T(8,...) custom-call(s32[6]{0:T(128)} %stack.27.info, ...), custom_call_target="tpu_custom_call" | custom-call | flops 1000 | bytes 1000 | tf_op jit(solution)/shard_map/conv_backward/pallas_call | solution.py:403
  160.1 3.2 %combine.10 = (bf16[2,288,512]{2,1,0:T(8,128)(2,1)}, bf16[2,288,512]{2,1,0:T(8,128)(2,1)}) custom-call(s32[6]{0:T(128)} %stack.27.info, bf16[2,2,288,512]{3,2,1,0:T(8,128)(2,1)} %bitcast.47, bf16[2,2,288,512]{3,2,1,0:T(8,128)(2,1)} %bitcast.13.refs_1_, bf16[2,2,288,512]{3,2,1,0:T(8,128)(2,1)} %bitcast.50, ...), custom_call_target="tpu_custom_call" | custom-call | flops 1000 | bytes 1000 | tf_op jit(solution)/shard_map/combine/pallas_call | solution.py:752
  165.8 4.2 %combine.11 = (bf16[8,32,2048]{2,1,0:T(8,128)(2,1)}, bf16[8,32,2176]{2,1,0:T(8,128)(2,1)}) custom-call(s32[6]{0:T(128)} %stack.27.info, bf16[2,2,2,2,32,1024]{5,4,3,2,1,0:T(8,128)(2,1)} %bitcast.53, bf16[2,2,2,2,32,4224]{5,4,3,2,1,0:T(8,128)(2,1)} %bitcast.16.refs_1_.refs_3_.refs_5_.refs_7_.refs_9_.refs_4_.refs_10_.refs_13_.refs_17_, ...), custom_call_target="tpu_custom_call" | custom-call | flops 1000 | bytes 1000 | tf_op jit(solution)/shard_map/combine/pallas_call | solution.py:752
  170.2 3.0 %collective-permute-done.21 = bf16[4,64,1024]{2,1,0:T(8,128)(2,1)} collective-permute-done((bf16[4,64,1024]{2,1,0:T(8,128)(2,1)}, bf16[4,64,1024]{2,1,0:T(8,128)(2,1)}, u32[]{:S(2)}, u32[]{:S(2)}) %collective-permute-start.21) | collective-permute-done | bytes 524320 | tf_op jit(solution)/shard_map/ppermute | solution.py:33
  173.5 3.6 %combine.12 = bf16[4,64,2048]{2,1,0:T(8,128)(2,1)} custom-call(s32[6]{0:T(128)} %stack.27.info, bf16[2,2,2,64,1024]{4,3,2,1,0:T(8,128)(2,1)} %bitcast.72, bf16[2,2,2,64,1024]{4,3,2,1,0:T(8,128)(2,1)} %bitcast.8.refs_1_, bf16[2,2,64,1024]{3,2,1,0:T(8,128)(2,1)} %bitcast.21.refs_2_, bf16[2,2,2,64,1024]{4,3,2,1,0:T(8,128)(2,1)} %bitcast.74, ...), custom_call_target="tpu_custom_call" | custom-call | flops 1000 | bytes 1000 | tf_op jit(solution)/shard_map/combine/pallas_call | solution.py:752
  179.1 6.6 %collective-permute-done.19.refs_2_ = bf16[2,288,512]{2,1,0:T(8,128)(2,1)S(1)} collective-permute-done((bf16[2,288,512]{2,1,0:T(8,128)(2,1)}, bf16[2,288,512]{2,1,0:T(8,128)(2,1)S(1)}, u32[]{:S(2)}, u32[]{:S(2)}) %collective-permute-start.19) | collective-permute-done | bytes 589856 | tf_op jit(solution)/shard_map/ppermute | solution.py:33
  186.6 3.1 %combine.13 = bf16[1,288,1024]{2,1,0:T(8,128)(2,1)} custom-call(s32[6]{0:T(128)} %stack.27.info, bf16[2,2,288,512]{3,2,1,0:T(8,128)(2,1)} %bitcast.48, bf16[2,2,288,512]{3,2,1,0:T(8,128)(2,1)} %bitcast.13.refs_1_, bf16[2,288,512]{2,1,0:T(8,128)(2,1)} %copy-done.2, bf16[2,2,288,512]{3,2,1,0:T(8,128)(2,1)} %bitcast.51, ...), custom_call_target="tpu_custom_call" | custom-call | flops 1000 | bytes 1000 | tf_op jit(solution)/shard_map/combine/pallas_call | solution.py:752
  191.6 15.8 %collective-permute-done.23 = bf16[1,288,1024]{2,1,0:T(8,128)(2,1)S(1)} collective-permute-done((bf16[1,288,1024]{2,1,0:T(8,128)(2,1)}, bf16[1,288,1024]{2,1,0:T(8,128)(2,1)S(1)}, u32[]{:S(2)}, u32[]{:S(2)}) %collective-permute-start.23) | collective-permute-done | bytes 589856 | tf_op jit(solution)/shard_map/ppermute | solution.py:33
  208.3 3.8 %settle.2 = (f32[288,1024]{1,0:T(8,128)}, bf16[288,1024]{1,0:T(8,128)(2,1)}) custom-call(s32[6]{0:T(128)} %stack.27.info, bf16[2,2,288,512]{3,2,1,0:T(8,128)(2,1)} %bitcast.49, bf16[2,2,288,512]{3,2,1,0:T(8,128)(2,1)} %bitcast.13.refs_1_, bf16[2,288,512]{2,1,0:T(8,128)(2,1)} %copy-done.2, bf16[288,1024]{1,0:T(8,128)(2,1)} %bitcast.76, ...), custom_call_target="tpu_custom_call" | custom-call | flops 1000 | bytes 1000 | tf_op jit(solution)/shard_map/settle/pallas_call | solution.py:847
  213.4 3.8 %combine.14 = (bf16[4,32,2048]{2,1,0:T(8,128)(2,1)}, bf16[4,32,2176]{2,1,0:T(8,128)(2,1)}) custom-call(s32[6]{0:T(128)} %stack.27.info, bf16[2,2,2,2,32,1024]{5,4,3,2,1,0:T(8,128)(2,1)} %bitcast.54, bf16[2,2,2,2,32,4224]{5,4,3,2,1,0:T(8,128)(2,1)} %bitcast.16.refs_1_.refs_3_.refs_5_.refs_7_.refs_9_.refs_4_.refs_10_.refs_13_.refs_17_, ...), custom_call_target="tpu_custom_call" | custom-call | flops 1000 | bytes 1000 | tf_op jit(solution)/shard_map/combine/pallas_call | solution.py:752
  218.6 2.6 combine.15
  221.8 2.0 collective-permute-start.27
  223.8 4.4 %add_convert_fusion = bf16[512,1024]{1,0:T(8,128)(2,1)} fusion(f32[512,1024]{1,0:T(8,128)} %collective-permute-done.15, f32[512,1024]{1,0:T(8,128)} %get-tuple-element.119, f32[528,1024]{1,0:T(8,128)} %get-tuple-element.108.hidden), kind=kLoop, calls=%fused_computation | loop fusion | flops 1572864 | bytes 7340032 | tf_op jit(solution)/shard_map/convert_element_type | solution.py:1151
  228.2 5.6 %collective-permute-done.24 = bf16[4,32,2048]{2,1,0:T(8,128)(2,1)} collective-permute-done((bf16[4,32,2048]{2,1,0:T(8,128)(2,1)}, bf16[4,32,2048]{2,1,0:T(8,128)(2,1)}, u32[]{:S(2)}, u32[]{:S(2)}) %collective-permute-start.24) | collective-permute-done | bytes 524320 | tf_op jit(solution)/shard_map/ppermute | solution.py:33
  234.6 4.2 %combine.16 = bf16[4,32,4224]{2,1,0:T(8,128)(2,1)} custom-call(s32[6]{0:T(128)} %stack.27.info, bf16[2,2,2,2,32,1024]{5,4,3,2,1,0:T(8,128)(2,1)} %bitcast.55, bf16[2,2,2,2,32,4224]{5,4,3,2,1,0:T(8,128)(2,1)} %bitcast.16.refs_1_.refs_3_.refs_5_.refs_7_.refs_9_.refs_4_.refs_10_.refs_13_.refs_17_, bf16[2,2,2,32,2048]{4,3,2,1,0:T(8,128)(2,1)} %bitcast.25.refs_2_.refs_5_.refs_6_, ...), custom_call_target="tpu_custom_call" | custom-call | flops 1000 | bytes 1000 | tf_op jit(solution)/shard_map/combine/pallas_call | solution.py:752
  239.6 2.6 combine.17
  249.2 3.3 %finish.1 = (f32[32,4608]{1,0:T(8,128)}, f32[32,4608]{1,0:T(8,128)}) custom-call(s32[6]{0:T(128)} %stack.27.info, bf16[64,2048]{1,0:T(8,128)(2,1)} %reduce-scatter.8.cloned.1.call-done.refs_0_, bf16[2,2,64,2560]{3,2,1,0:T(8,128)(2,1)} %bitcast.45, bf16[2,64,1280]{2,1,0:T(8,128)(2,1)} %copy-done.4, bf16[64,1280]{1,0:T(8,128)(2,1)} %bitcast.81, ...), custom_call_target="tpu_custom_call" | custom-call | flops 1000 | bytes 1000 | tf_op jit(solution)/shard_map/finish/pallas_call | solution.py:869
  253.5 2.0 bitcast_select_fusion
  256.7 17.2 %reduce-scatter.6.cloned.1.call-done.refs_0_.refs_1_.refs_2_.refs_3_.refs_4_ = bf16[32,4224]{1,0:T(8,128)(2,1)} async-done(((bf16[128,4224]{1,0:T(8,128)(2,1)}), bf16[32,4224]{1,0:T(8,128)(2,1)}) %reduce-scatter.6.cloned.1.call-update) | async-done | bytes 270352 | tf_op jit(solution)/shard_map/reduce_scatter | solution.py:1015
  273.9 2.4 settle.3
  (102 shorter events, 41.0 us)
Async XLA Ops:
  7.2 211.5 %reduce-scatter.4.cloned.1.call-start = ((), (), s32[]{:S(2)}) async-start(), calls=%async_computation.3 | async-start | bytes 6553600 | tf_op jit(solution)/shard_map/reduce_scatter | solution.py:987
  7.2 14.0 %collective-permute-start = (bf16[512,3072]{1,0:T(8,128)(2,1)}, bf16[512,3072]{1,0:T(8,128)(2,1)}, u32[]{:S(2)}, u32[]{:S(2)}) collective-permute-start(bf16[512,3072]{1,0:T(8,128)(2,1)} %own_x.3), channel_id=1, source_target_pairs={{0,1},{1,0},{2,3},{3,2},{4,5},{5,4},{6,7},{7,6},{8,9},{9,8},{10,11... | collective-permute-start | bytes 9437192 | tf_op jit(solution)/shard_map/ppermute | solution.py:28
  7.7 13.5 %collective-permute-start.1 = (bf16[512,1024]{1,0:T(8,128)(2,1)}, bf16[512,1024]{1,0:T(8,128)(2,1)}, u32[]{:S(2)}, u32[]{:S(2)}) collective-permute-start(bf16[512,1024]{1,0:T(8,128)(2,1)} %out_own.3), channel_id=1, source_target_pairs={{0,1},{1,0},{2,3},{3,2},{4,5},{5,4},{6,7},{7,6},{8,9},{9,8},{10,11... | collective-permute-start | bytes 3145736 | tf_op jit(solution)/shard_map/ppermute | solution.py:28
  7.8 13.4 %collective-permute-start.4 = (bf16[512,1024]{1,0:T(8,128)(2,1)}, bf16[512,1024]{1,0:T(8,128)(2,1)}, u32[]{:S(2)}, u32[]{:S(2)}) collective-permute-start(bf16[512,1024]{1,0:T(8,128)(2,1)} %cotangent.1), channel_id=1, source_target_pairs={{0,1},{1,0},{2,3},{3,2},{4,5},{5,4},{6,7},{7,6},{8,9},{9,8},{10,11... | collective-permute-start | bytes 3145736 | tf_op jit(solution)/shard_map/ppermute | solution.py:28
  9.8 3.3 %collective-permute-start.5 = (bf16[16,2048]{1,0:T(8,128)(2,1)S(1)}, bf16[16,2048]{1,0:T(8,128)(2,1)S(1)}, u32[]{:S(2)}, u32[]{:S(2)}) collective-permute-start(bf16[16,2048]{1,0:T(8,128)(2,1)S(1)} %pad_maximum_fusion), channel_id=1, source_target_pairs={{1,0},{2,1},{3,2},{4,3},{5,4},{6,5},{7,6},{8,7},{9,8},{10,9},{11,1... | collective-permute-start | bytes 196616 | tf_op jit(solution)/shard_map/ppermute | solution.py:24
  13.1 8.1 %collective-permute-start.6 = (bf16[16,2048]{1,0:T(8,128)(2,1)S(1)}, bf16[16,2048]{1,0:T(8,128)(2,1)S(1)}, u32[]{:S(2)}, u32[]{:S(2)}) collective-permute-start(bf16[16,2048]{1,0:T(8,128)(2,1)S(1)} %collective-permute-done.5.after.g_after), channel_id=1, source_target_pairs={{0,1},{1,0},{2,3},{3,2},{4,5},{5,4},{6,7},{7,6},{8,9},{9,8},{10,11... | collective-permute-start | bytes 196616 | tf_op jit(solution)/shard_map/ppermute | solution.py:28
  21.2 20.6 %collective-permute-start.7 = (bf16[512,4608]{1,0:T(8,128)(2,1)}, bf16[512,4608]{1,0:T(8,128)(2,1)}, u32[]{:S(2)}, u32[]{:S(2)}) collective-permute-start(bf16[512,4608]{1,0:T(8,128)(2,1)} %gate_own.1), channel_id=1, source_target_pairs={{0,1},{1,0},{2,3},{3,2},{4,5},{5,4},{6,7},{7,6},{8,9},{9,8},{10,11... | collective-permute-start | bytes 14155784 | tf_op jit(solution)/shard_map/ppermute | solution.py:28
  24.3 17.5 %collective-permute-start.8 = (bf16[512,4608]{1,0:T(8,128)(2,1)}, bf16[512,4608]{1,0:T(8,128)(2,1)}, u32[]{:S(2)}, u32[]{:S(2)}) collective-permute-start(bf16[512,4608]{1,0:T(8,128)(2,1)} %up_own.1), channel_id=1, source_target_pairs={{0,1},{1,0},{2,3},{3,2},{4,5},{5,4},{6,7},{7,6},{8,9},{9,8},{10,11... | collective-permute-start | bytes 14155784 | tf_op jit(solution)/shard_map/ppermute | solution.py:28
  96.5 150.8 %reduce-scatter.8.cloned.1.call-start = ((), (), s32[]{:S(2)}) async-start(), calls=%async_computation.5 | async-start | bytes 1310720 | tf_op jit(solution)/shard_map/reduce_scatter | solution.py:1015
  96.6 29.0 %collective-permute-start.10 = (f32[528,1024]{1,0:T(8,128)}, f32[528,1024]{1,0:T(8,128)}, u32[]{:S(2)}, u32[]{:S(2)}) collective-permute-start(f32[528,1024]{1,0:T(8,128)} %get-tuple-element.121), channel_id=1, source_target_pairs={{0,1},{1,0},{2,3},{3,2},{4,5},{5,4},{6,7},{7,6},{8,9},{9,8},{10,11... | collective-permute-start | bytes 6488072 | tf_op jit(solution)/shard_map/ppermute | solution.py:28
  97.0 26.4 %collective-permute-start.11 = (bf16[8,64,1024]{2,1,0:T(8,128)(2,1)}, bf16[8,64,1024]{2,1,0:T(8,128)(2,1)}, u32[]{:S(2)}, u32[]{:S(2)}) collective-permute-start(bf16[8,64,1024]{2,1,0:T(8,128)(2,1)} %get-tuple-element.127), channel_id=1, source_target_pairs={{0,2},{2,0},{4,6},{6,4},{8,10},{10,8},{12,14},{14,12},{16,18},{18,... | collective-permute-start | bytes 3145736 | tf_op jit(solution)/shard_map/ppermute | solution.py:33
  99.4 26.1 %collective-permute-start.12 = (bf16[4,128,1024]{2,1,0:T(8,128)(2,1)}, bf16[4,128,1024]{2,1,0:T(8,128)(2,1)}, u32[]{:S(2)}, u32[]{:S(2)}) collective-permute-start(bf16[4,128,1024]{2,1,0:T(8,128)(2,1)} %get-tuple-element.128), channel_id=1, source_target_pairs={{0,4},{2,6},{4,0},{6,2},{8,12},{10,14},{12,8},{14,10},{16,20},{18,... | collective-permute-start | bytes 3145736 | tf_op jit(solution)/shard_map/ppermute | solution.py:33
  125.6 32.5 %collective-permute-start.15 = (f32[512,1024]{1,0:T(8,128)}, f32[512,1024]{1,0:T(8,128)}, u32[]{:S(2)}, u32[]{:S(2)}) collective-permute-start(f32[512,1024]{1,0:T(8,128)} %get-tuple-element.148), channel_id=1, source_target_pairs={{0,1},{1,0},{2,3},{3,2},{4,5},{5,4},{6,7},{7,6},{8,9},{9,8},{10,11... | collective-permute-start | bytes 6291464 | tf_op jit(solution)/shard_map/ppermute | solution.py:28
  125.6 32.4 %collective-permute-start.13 = (bf16[4,288,512]{2,1,0:T(8,128)(2,1)}, bf16[4,288,512]{2,1,0:T(8,128)(2,1)}, u32[]{:S(2)}, u32[]{:S(2)}) collective-permute-start(bf16[4,288,512]{2,1,0:T(8,128)(2,1)} %get-tuple-element.146), channel_id=1, source_target_pairs={{0,2},{2,0},{4,6},{6,4},{8,10},{10,8},{12,14},{14,12},{16,18},{18,... | collective-permute-start | bytes 3538952 | tf_op jit(solution)/shard_map/ppermute | solution.py:33
  125.9 32.2 %collective-permute-start.14 = (bf16[2,576,512]{2,1,0:T(8,128)(2,1)}, bf16[2,576,512]{2,1,0:T(8,128)(2,1)}, u32[]{:S(2)}, u32[]{:S(2)}) collective-permute-start(bf16[2,576,512]{2,1,0:T(8,128)(2,1)} %get-tuple-element.147), channel_id=1, source_target_pairs={{0,4},{2,6},{4,0},{6,2},{8,12},{10,14},{12,8},{14,10},{16,20},{18,... | collective-permute-start | bytes 3538952 | tf_op jit(solution)/shard_map/ppermute | solution.py:33
  158.0 7.8 %collective-permute-start.16 = (bf16[16,32,4224]{2,1,0:T(8,128)(2,1)}, bf16[16,32,4224]{2,1,0:T(8,128)(2,1)}, u32[]{:S(2)}, u32[]{:S(2)}) collective-permute-start(bf16[16,32,4224]{2,1,0:T(8,128)(2,1)} %get-tuple-element.152), channel_id=1, source_target_pairs={{0,1},{1,0},{2,3},{3,2},{4,5},{5,4},{6,7},{7,6},{8,9},{9,8},{10,11... | collective-permute-start | bytes 12976136 | tf_op jit(solution)/shard_map/ppermute | solution.py:28
  158.1 15.1 %collective-permute-start.21 = (bf16[4,64,1024]{2,1,0:T(8,128)(2,1)}, bf16[4,64,1024]{2,1,0:T(8,128)(2,1)}, u32[]{:S(2)}, u32[]{:S(2)}) collective-permute-start(bf16[4,64,1024]{2,1,0:T(8,128)(2,1)} %get-tuple-element.134), channel_id=1, source_target_pairs={{0,4},{2,6},{4,0},{6,2},{8,12},{10,14},{12,8},{14,10},{16,20},{18,... | collective-permute-start | bytes 1572872 | tf_op jit(solution)/shard_map/ppermute | solution.py:33
  158.4 15.1 %collective-permute-start.22 = (bf16[4,64,1024]{2,1,0:T(8,128)(2,1)}, bf16[4,64,1024]{2,1,0:T(8,128)(2,1)}, u32[]{:S(2)}, u32[]{:S(2)}) collective-permute-start(bf16[4,64,1024]{2,1,0:T(8,128)(2,1)} %get-tuple-element.135), channel_id=1, source_target_pairs={{0,2},{2,0},{4,6},{6,4},{8,10},{10,8},{12,14},{14,12},{16,18},{18,... | collective-permute-start | bytes 1572872 | tf_op jit(solution)/shard_map/ppermute | solution.py:33
  163.3 22.4 %collective-permute-start.19 = (bf16[2,288,512]{2,1,0:T(8,128)(2,1)}, bf16[2,288,512]{2,1,0:T(8,128)(2,1)S(1)}, u32[]{:S(2)}, u32[]{:S(2)}) collective-permute-start(bf16[2,288,512]{2,1,0:T(8,128)(2,1)} %get-tuple-element.157), channel_id=1, source_target_pairs={{0,4},{2,6},{4,0},{6,2},{8,12},{10,14},{12,8},{14,10},{16,20},{18,... | collective-permute-start | bytes 1769480 | tf_op jit(solution)/shard_map/ppermute | solution.py:33
  165.1 21.0 %collective-permute-start.20 = (bf16[2,288,512]{2,1,0:T(8,128)(2,1)}, bf16[2,288,512]{2,1,0:T(8,128)(2,1)}, u32[]{:S(2)}, u32[]{:S(2)}) collective-permute-start(bf16[2,288,512]{2,1,0:T(8,128)(2,1)} %get-tuple-element.158), channel_id=1, source_target_pairs={{0,2},{2,0},{4,6},{6,4},{8,10},{10,8},{12,14},{14,12},{16,18},{18,... | collective-permute-start | bytes 1769480 | tf_op jit(solution)/shard_map/ppermute | solution.py:33
  170.0 43.4 %collective-permute-start.18 = (bf16[8,32,2176]{2,1,0:T(8,128)(2,1)}, bf16[8,32,2176]{2,1,0:T(8,128)(2,1)}, u32[]{:S(2)}, u32[]{:S(2)}) collective-permute-start(bf16[8,32,2176]{2,1,0:T(8,128)(2,1)} %get-tuple-element.165), channel_id=1, source_target_pairs={{0,4},{2,6},{4,0},{6,2},{8,12},{10,14},{12,8},{14,10},{16,20},{18,... | collective-permute-start | bytes 3342344 | tf_op jit(solution)/shard_map/ppermute | solution.py:33
  177.1 96.9 %reduce-scatter.6.cloned.1.call-start = ((), (), s32[]{:S(2)}) async-start(), calls=%async_computation.4 | async-start | bytes 1351680 | tf_op jit(solution)/shard_map/reduce_scatter | solution.py:1015
  177.3 36.0 %collective-permute-start.17 = (bf16[8,32,2048]{2,1,0:T(8,128)(2,1)}, bf16[8,32,2048]{2,1,0:T(8,128)(2,1)}, u32[]{:S(2)}, u32[]{:S(2)}) collective-permute-start(bf16[8,32,2048]{2,1,0:T(8,128)(2,1)} %get-tuple-element.164), channel_id=1, source_target_pairs={{0,2},{2,0},{4,6},{6,4},{8,10},{10,8},{12,14},{14,12},{16,18},{18,... | collective-permute-start | bytes 3145736 | tf_op jit(solution)/shard_map/ppermute | solution.py:33
  189.7 17.8 %collective-permute-start.23 = (bf16[1,288,1024]{2,1,0:T(8,128)(2,1)}, bf16[1,288,1024]{2,1,0:T(8,128)(2,1)S(1)}, u32[]{:S(2)}, u32[]{:S(2)}) collective-permute-start(bf16[1,288,1024]{2,1,0:T(8,128)(2,1)} %combine.13), channel_id=1, source_target_pairs={{0,8},{2,10},{4,12},{6,14},{8,0},{10,2},{12,4},{14,6},{16,24},{18,... | collective-permute-start | bytes 1769480 | tf_op jit(solution)/shard_map/ppermute | solution.py:33
  212.0 26.8 %collective-permute-start.31 = (bf16[288,1024]{1,0:T(8,128)(2,1)}, bf16[288,1024]{1,0:T(8,128)(2,1)}, u32[]{:S(2)}, u32[]{:S(2)}) collective-permute-start(bf16[288,1024]{1,0:T(8,128)(2,1)} %get-tuple-element.172), channel_id=1, source_target_pairs={{1,17},{3,19},{5,21},{7,23},{9,25},{11,27},{13,29},{15,31},{16,0},... | collective-permute-start | bytes 1769480 | tf_op jit(solution)/shard_map/ppermute | solution.py:1129
  217.1 16.7 %collective-permute-start.25 = (bf16[4,32,2176]{2,1,0:T(8,128)(2,1)}, bf16[4,32,2176]{2,1,0:T(8,128)(2,1)S(1)}, u32[]{:S(2)}, u32[]{:S(2)}) collective-permute-start(bf16[4,32,2176]{2,1,0:T(8,128)(2,1)} %get-tuple-element.176), channel_id=1, source_target_pairs={{0,2},{2,0},{4,6},{6,4},{8,10},{10,8},{12,14},{14,12},{16,18},{18,... | collective-permute-start | bytes 1671176 | tf_op jit(solution)/shard_map/ppermute | solution.py:33
  218.6 15.2 %collective-permute-start.24 = (bf16[4,32,2048]{2,1,0:T(8,128)(2,1)}, bf16[4,32,2048]{2,1,0:T(8,128)(2,1)}, u32[]{:S(2)}, u32[]{:S(2)}) collective-permute-start(bf16[4,32,2048]{2,1,0:T(8,128)(2,1)} %get-tuple-element.175), channel_id=1, source_target_pairs={{0,4},{2,6},{4,0},{6,2},{8,12},{10,14},{12,8},{14,10},{16,20},{18,... | collective-permute-start | bytes 1572872 | tf_op jit(solution)/shard_map/ppermute | solution.py:33
  221.2 17.7 %collective-permute-start.26 = (bf16[2,64,1280]{2,1,0:T(8,128)(2,1)}, bf16[2,64,1280]{2,1,0:T(8,128)(2,1)S(1)}, u32[]{:S(2)}, u32[]{:S(2)}) collective-permute-start(bf16[2,64,1280]{2,1,0:T(8,128)(2,1)} %get-tuple-element.178), channel_id=1, source_target_pairs={{0,2},{2,0},{4,6},{6,4},{8,10},{10,8},{12,14},{14,12},{16,18},{18,... | collective-permute-start | bytes 983048 | tf_op jit(solution)/shard_map/ppermute | solution.py:33
  221.8 17.1 %collective-permute-start.27 = (bf16[2,64,1280]{2,1,0:T(8,128)(2,1)}, bf16[2,64,1280]{2,1,0:T(8,128)(2,1)}, u32[]{:S(2)}, u32[]{:S(2)}) collective-permute-start(bf16[2,64,1280]{2,1,0:T(8,128)(2,1)} %get-tuple-element.179), channel_id=1, source_target_pairs={{0,4},{2,6},{4,0},{6,2},{8,12},{10,14},{12,8},{14,10},{16,20},{18,... | collective-permute-start | bytes 983048 | tf_op jit(solution)/shard_map/ppermute | solution.py:33
  242.2 5.5 %collective-permute-start.28 = (bf16[1,64,1280]{2,1,0:T(8,128)(2,1)}, bf16[1,64,1280]{2,1,0:T(8,128)(2,1)S(1)}, u32[]{:S(2)}, u32[]{:S(2)}) collective-permute-start(bf16[1,64,1280]{2,1,0:T(8,128)(2,1)} %get-tuple-element.191), channel_id=1, source_target_pairs={{0,4},{2,6},{4,0},{6,2},{8,12},{10,14},{12,8},{14,10},{16,20},{18,... | collective-permute-start | bytes 491528 | tf_op jit(solution)/shard_map/ppermute | solution.py:33
  242.5 6.0 %collective-permute-start.29 = (bf16[1,64,1280]{2,1,0:T(8,128)(2,1)}, bf16[1,64,1280]{2,1,0:T(8,128)(2,1)S(1)}, u32[]{:S(2)}, u32[]{:S(2)}) collective-permute-start(bf16[1,64,1280]{2,1,0:T(8,128)(2,1)} %get-tuple-element.192), channel_id=1, source_target_pairs={{0,2},{2,0},{4,6},{6,4},{8,10},{10,8},{12,14},{14,12},{16,18},{18,... | collective-permute-start | bytes 491528 | tf_op jit(solution)/shard_map/ppermute | solution.py:33
  247.3 6.3 %collective-permute-start.32 = (f32[144,1024]{1,0:T(8,128)}, f32[144,1024]{1,0:T(8,128)S(1)}, u32[]{:S(2)}, u32[]{:S(2)}) collective-permute-start(f32[144,1024]{1,0:T(8,128)} %dynamic-slice_bitcast_fusion), channel_id=1, source_target_pairs={{0,1},{1,0},{2,3},{3,2},{4,5},{5,4},{6,7},{7,6},{8,9},{9,8},{10,11... | collective-permute-start | bytes 1769480 | tf_op jit(solution)/shard_map/ppermute | solution.py:28
  (14 other events, 57.0 us)
Sparse Core Ops, SparseCore 0:
  96.7 96.0 reduce-scatter.3
  195.0 30.4 reduce-scatter.7
  247.4 26.4 reduce-scatter.5

commit v3 on v2

--- a/solution.py
+++ b/solution.py
@@ -296,7 +296,8 @@
     @pl.when(step == 0)
     def _():
         vectors[...] = jnp.zeros(vectors.shape, jnp.float32)
-        grad = in_order(back[:, :half] + came[:, half:], back[:, half:] + came[:, :half])
+        low, high = came[:, half:].astype(jnp.float32), came[:, :half].astype(jnp.float32)
+        grad = in_order(back[:, :half] + low, back[:, half:] + high)
         resid = hidden[...]
         scale = lax.rsqrt(jnp.mean(resid * resid, axis=-1, keepdims=True) + epsilon)
         normed = resid * scale
@@ -552,7 +553,8 @@
     @pl.when(step == pl.num_programs(0) - 1)
     def _():
         for place, which, source, _ in places:
-            (back_keep, back_send)[which][source, :] = back[place, :]
+            out = (back_keep, back_send)[which]
+            out[source, :] = back[place, :].astype(out.dtype)
 
 
 def ffn(info, norms, grads, weights, down, split, pers):
@@ -563,8 +565,8 @@
     column = pl.BlockSpec((half, TILE), lambda j, info: (0, info[0] * count + j))
     shapes = [jax.ShapeDtypeStruct((rows, count * TILE), jnp.bfloat16)]
     specs = [pl.BlockSpec((rows, TILE), lambda j, info: (0, j))]
-    for _ in range(2):
-        shapes.append(jax.ShapeDtypeStruct((ext, width), jnp.float32))
+    for kind in (jnp.float32, jnp.bfloat16):
+        shapes.append(jax.ShapeDtypeStruct((ext, width), kind))
         specs.append(fixed(ext, width))
     for per in pers:
         for _ in range(2):
@@ -579,7 +581,7 @@
     specs.append(pl.BlockSpec((width, 2 * TILE), lambda j, info: (0, jnp.maximum(j - split, 0))))
     after = pl.BlockSpec((HALO, width), lambda j, info: (0, 1))
     return pl.pallas_call(
-        functools.partial(ffn_kernel, 2, split),
+        functools.partial(ffn_kernel, 3, split),
         out_shape=shapes,
         grid_spec=pltpu.PrefetchScalarGridSpec(
             num_scalar_prefetch=1,
@@ -624,7 +626,7 @@
     rhs[block:, :] = g_other[...]
     result = dot(act[:real, :], down_ref[...], NN)
     out_keep[...] = result[:block]
-    out_send[...] = result[block:]
+    out_send[...] = result[block:].astype(out_send.dtype)
     grad[...] = dot(act[:real, :], rhs[...], TN).astype(grad.dtype)
     here = pl.num_programs(0) // 2
     outs = ((step < here, low_send, low_keep, info[1]), (step >= here, high_send, high_keep, info[2]))
@@ -647,7 +649,7 @@
     block = g_own.shape[0]
     kind = jnp.bfloat16 if min(pers) % 16 == 0 else jnp.float32
     tile = pl.BlockSpec((block, TILE), lambda j, info: (0, j))
-    shapes = [jax.ShapeDtypeStruct((block, width), jnp.float32)] * 2
+    shapes = [jax.ShapeDtypeStruct((block, width), kind) for kind in (jnp.float32, jnp.bfloat16)]
     specs = [tile] * 2
     for index, per in enumerate(pers):
         groups = hidden // (2 * per)

time: 285 us -> 284 us (level)
  transfers between devices with their start and end apart: 36 -> 36, of which waited for: 16 -> 17; matrix products, arithmetic and copies ran while one was open for 6% -> 6% of each run, Pallas kernels for 34% -> 34%
where the time goes in v3:
time: 284 us; the launch traced here: 283 us
  Pallas kernels  149 us (52%)
  waiting for transfers between devices  63.5 us (22%)
  starting transfers between devices  33.8 us (12%)
  between operations  14 us (5%)
  other arithmetic  11.9 us (4%)
  local copies, waits for them, and re-layouts  11.1 us (4%)
    pallas_call x1, Pallas kernels, ffn(): pl.pallas_call(functools.partial(ffn_kernel, 3, split), out_shape=shapes,...  50.9 us
    ppermute x17, waiting for transfers between devices, across(): lax.ppermute(value, 'seq', [(place, place ^ 1 << bit) for place in range(...  40.3 us
    pallas_call x9, Pallas kernels, combine(): pl.pallas_call(functools.partial(combine_kernel, plan), out_shape=shapes,...  30.2 us
    pallas_call x1, Pallas kernels, conv_backward(): pl.pallas_call(backward_kernel, out_shape=[jax.ShapeDtypeStruct((rows, wi...  27.1 us
    ppermute x17, starting transfers between devices, across(): lax.ppermute(value, 'seq', [(place, place ^ 1 << bit) for place in range(...  20.6 us
    pallas_call x1, Pallas kernels, down_part(): pl.pallas_call(down_kernel, out_shape=shapes, grid_spec=pltpu.PrefetchSca...  17.4 us
    reduce_scatter x2, waiting for transfers between devices, upper_sum(): lax.psum_scatter(value, 'seq', scatter_dimension=0, axis_index_groups=gro...  17.3 us
    pallas_call x1, Pallas kernels, conv_forward(): pl.pallas_call(forward_kernel, out_shape=[jax.ShapeDtypeStruct((ext + HAL...  14.1 us
  transfers between devices with their start and end apart: 36, of which 17 were waited for; matrix products, arithmetic and copies ran while one was open for 6% of the time, Pallas kernels for 34%

profile of v3, /device:TPU:0, one launch (start us, length us, event | category | flops | bytes accessed | tf_op | source)
XLA Modules:
  0.0 283.3 jit_solution(1716555682958125620)
XLA Ops:
  13.1 3.2 %collective-permute-start.6 = (bf16[16,2048]{1,0:T(8,128)(2,1)S(1)}, bf16[16,2048]{1,0:T(8,128)(2,1)S(1)}, u32[]{:S(2)}, u32[]{:S(2)}) collective-permute-start(bf16[16,2048]{1,0:T(8,128)(2,1)S(1)} %collective-permute-done.5.after.g_after), channel_id=1, source_target_pairs={{0,1},{1,0},{2,3},{3,2},{4,5},{5,4},{6,7},{7,6},{8,9},{9,8},{10,11... | collective-permute-start | bytes 196616 | tf_op jit(solution)/shard_map/ppermute | solution.py:28
  18.3 2.1 collective-permute-start.3
  21.2 3.1 %collective-permute-start.7 = (bf16[512,4608]{1,0:T(8,128)(2,1)}, bf16[512,4608]{1,0:T(8,128)(2,1)}, u32[]{:S(2)}, u32[]{:S(2)}) collective-permute-start(bf16[512,4608]{1,0:T(8,128)(2,1)} %gate_own.1), channel_id=1, source_target_pairs={{0,1},{1,0},{2,3},{3,2},{4,5},{5,4},{6,7},{7,6},{8,9},{9,8},{10,11... | collective-permute-start | bytes 14155784 | tf_op jit(solution)/shard_map/ppermute | solution.py:28
  27.5 14.1 %conv_forward.1 = (f32[544,1024]{1,0:T(8,128)}, f32[544,1024]{1,0:T(8,128)}, f32[544,1024]{1,0:T(8,128)}, f32[528,1024]{1,0:T(8,128)}, bf16[528,1024]{1,0:T(8,128)(2,1)}, /*index=5*/bf16[528,1024]{1,0:T(8,128)(2,1)}) custom-call(s32[6]{0:T(128)} %stack.27.info, bf16[512,1024]{1,0:T(8,128)(2,1)} %tokens.3, bf16[16,1024]{1,0:T(8,128)(2,1)} %copy-done.9, ...), custom_call_target="tpu_custom_call" | custom-call | flops 1000 | bytes 1000 | tf_op jit(solution)/shard_map/conv_forward/pallas_call | solution.py:191
  41.9 2.8 collective-permute-done.9.n_other
  44.7 50.9 %ffn.1 = (bf16[1056,2304]{1,0:T(8,128)(2,1)}, f32[528,1024]{1,0:T(8,128)}, bf16[528,1024]{1,0:T(8,128)(2,1)}, bf16[8,64,1024]{2,1,0:T(8,128)(2,1)}, bf16[8,64,10...) custom-call(s32[6]{0:T(128)} %stack.27.info, ...), custom_call_target="tpu_custom_call" | custom-call | flops 1000 | bytes 1000 | tf_op jit(solution)/shard_map/ffn/pallas_call | solution.py:583
  95.9 2.5 collective-permute-start.11
  98.5 2.4 collective-permute-start.12
  100.9 17.4 %down.1 = (f32[512,1024]{1,0:T(8,128)}, bf16[512,1024]{1,0:T(8,128)(2,1)}, bf16[4,288,512]{2,1,0:T(8,128)(2,1)}, bf16[4,288,512]{2,1,0:T(8,128)(2,1)}, bf16[2,57...) custom-call(s32[6]{0:T(128)} %stack.27.info, bf16[1056,2304]{1,0:T(8,128)(2,1)} %get-tuple-element.118.act, ...), custom_call_target="tpu_custom_call" | custom-call | flops 1000 | bytes 1000 | tf_op jit(solution)/shard_map/down/pallas_call | solution.py:668
  118.3 4.1 %collective-permute-done.11 = bf16[8,64,1024]{2,1,0:T(8,128)(2,1)} collective-permute-done((bf16[8,64,1024]{2,1,0:T(8,128)(2,1)}, bf16[8,64,1024]{2,1,0:T(8,128)(2,1)}, u32[]{:S(2)}, u32[]{:S(2)}) %collective-permute-start.11) | collective-permute-done | bytes 1048608 | tf_op jit(solution)/shard_map/ppermute | solution.py:33
  122.4 2.1 collective-permute-done.12
  126.6 3.1 %combine.9 = (bf16[4,64,1024]{2,1,0:T(8,128)(2,1)}, bf16[4,64,1024]{2,1,0:T(8,128)(2,1)}) custom-call(s32[6]{0:T(128)} %stack.27.info, bf16[2,2,2,64,1024]{4,3,2,1,0:T(8,128)(2,1)} %bitcast.71, bf16[2,2,2,64,1024]{4,3,2,1,0:T(8,128)(2,1)} %bitcast.8.refs_1_, bf16[2,2,2,64,1024]{4,3,2,1,0:T(8,128)(2,1)} %bitcast.73, ...), custom_call_target="tpu_custom_call" | custom-call | flops 1000 | bytes 1000 | tf_op jit(solution)/shard_map/combine/pallas_call | solution.py:754
  129.7 27.1 %conv_backward.1 = (bf16[512,1024]{1,0:T(8,128)(2,1)}, bf16[16,32,4224]{2,1,0:T(8,128)(2,1)}, bf16[16,32,1024]{2,1,0:T(8,128)(2,1)}, bf16[16,32,1024]{2,1,0:T(8,...) custom-call(s32[6]{0:T(128)} %stack.27.info, ...), custom_call_target="tpu_custom_call" | custom-call | flops 1000 | bytes 1000 | tf_op jit(solution)/shard_map/conv_backward/pallas_call | solution.py:404
  159.0 3.2 %combine.10 = (bf16[2,288,512]{2,1,0:T(8,128)(2,1)}, bf16[2,288,512]{2,1,0:T(8,128)(2,1)}) custom-call(s32[6]{0:T(128)} %stack.27.info, bf16[2,2,288,512]{3,2,1,0:T(8,128)(2,1)} %bitcast.47, bf16[2,2,288,512]{3,2,1,0:T(8,128)(2,1)} %bitcast.13.refs_1_, bf16[2,2,288,512]{3,2,1,0:T(8,128)(2,1)} %bitcast.50, ...), custom_call_target="tpu_custom_call" | custom-call | flops 1000 | bytes 1000 | tf_op jit(solution)/shard_map/combine/pallas_call | solution.py:754
  164.6 4.1 %combine.11 = (bf16[8,32,2048]{2,1,0:T(8,128)(2,1)}, bf16[8,32,2176]{2,1,0:T(8,128)(2,1)}) custom-call(s32[6]{0:T(128)} %stack.27.info, bf16[2,2,2,2,32,1024]{5,4,3,2,1,0:T(8,128)(2,1)} %bitcast.53, bf16[2,2,2,2,32,4224]{5,4,3,2,1,0:T(8,128)(2,1)} %bitcast.16.refs_1_.refs_3_.refs_5_.refs_7_.refs_9_.refs_4_.refs_10_.refs_13_.refs_17_, ...), custom_call_target="tpu_custom_call" | custom-call | flops 1000 | bytes 1000 | tf_op jit(solution)/shard_map/combine/pallas_call | solution.py:754
  169.0 3.0 %collective-permute-done.21 = bf16[4,64,1024]{2,1,0:T(8,128)(2,1)} collective-permute-done((bf16[4,64,1024]{2,1,0:T(8,128)(2,1)}, bf16[4,64,1024]{2,1,0:T(8,128)(2,1)}, u32[]{:S(2)}, u32[]{:S(2)}) %collective-permute-start.21) | collective-permute-done | bytes 524320 | tf_op jit(solution)/shard_map/ppermute | solution.py:33
  172.3 3.6 %combine.12 = bf16[4,64,2048]{2,1,0:T(8,128)(2,1)} custom-call(s32[6]{0:T(128)} %stack.27.info, bf16[2,2,2,64,1024]{4,3,2,1,0:T(8,128)(2,1)} %bitcast.72, bf16[2,2,2,64,1024]{4,3,2,1,0:T(8,128)(2,1)} %bitcast.8.refs_1_, bf16[2,2,64,1024]{3,2,1,0:T(8,128)(2,1)} %bitcast.21.refs_2_, bf16[2,2,2,64,1024]{4,3,2,1,0:T(8,128)(2,1)} %bitcast.74, ...), custom_call_target="tpu_custom_call" | custom-call | flops 1000 | bytes 1000 | tf_op jit(solution)/shard_map/combine/pallas_call | solution.py:754
  178.0 6.5 %collective-permute-done.19.refs_2_ = bf16[2,288,512]{2,1,0:T(8,128)(2,1)S(1)} collective-permute-done((bf16[2,288,512]{2,1,0:T(8,128)(2,1)}, bf16[2,288,512]{2,1,0:T(8,128)(2,1)S(1)}, u32[]{:S(2)}, u32[]{:S(2)}) %collective-permute-start.19) | collective-permute-done | bytes 589856 | tf_op jit(solution)/shard_map/ppermute | solution.py:33
  185.4 3.1 %combine.13 = bf16[1,288,1024]{2,1,0:T(8,128)(2,1)} custom-call(s32[6]{0:T(128)} %stack.27.info, bf16[2,2,288,512]{3,2,1,0:T(8,128)(2,1)} %bitcast.48, bf16[2,2,288,512]{3,2,1,0:T(8,128)(2,1)} %bitcast.13.refs_1_, bf16[2,288,512]{2,1,0:T(8,128)(2,1)} %copy-done.2, bf16[2,2,288,512]{3,2,1,0:T(8,128)(2,1)} %bitcast.51, ...), custom_call_target="tpu_custom_call" | custom-call | flops 1000 | bytes 1000 | tf_op jit(solution)/shard_map/combine/pallas_call | solution.py:754
  188.5 2.0 collective-permute-start.23
  190.5 15.1 %collective-permute-done.23 = bf16[1,288,1024]{2,1,0:T(8,128)(2,1)S(1)} collective-permute-done((bf16[1,288,1024]{2,1,0:T(8,128)(2,1)}, bf16[1,288,1024]{2,1,0:T(8,128)(2,1)S(1)}, u32[]{:S(2)}, u32[]{:S(2)}) %collective-permute-start.23) | collective-permute-done | bytes 589856 | tf_op jit(solution)/shard_map/ppermute | solution.py:33
  206.4 3.7 %settle.2 = (f32[288,1024]{1,0:T(8,128)}, bf16[288,1024]{1,0:T(8,128)(2,1)}) custom-call(s32[6]{0:T(128)} %stack.27.info, bf16[2,2,288,512]{3,2,1,0:T(8,128)(2,1)} %bitcast.49, bf16[2,2,288,512]{3,2,1,0:T(8,128)(2,1)} %bitcast.13.refs_1_, bf16[2,288,512]{2,1,0:T(8,128)(2,1)} %copy-done.2, bf16[288,1024]{1,0:T(8,128)(2,1)} %bitcast.76, ...), custom_call_target="tpu_custom_call" | custom-call | flops 1000 | bytes 1000 | tf_op jit(solution)/shard_map/settle/pallas_call | solution.py:849
  211.5 3.8 %combine.14 = (bf16[4,32,2048]{2,1,0:T(8,128)(2,1)}, bf16[4,32,2176]{2,1,0:T(8,128)(2,1)}) custom-call(s32[6]{0:T(128)} %stack.27.info, bf16[2,2,2,2,32,1024]{5,4,3,2,1,0:T(8,128)(2,1)} %bitcast.54, bf16[2,2,2,2,32,4224]{5,4,3,2,1,0:T(8,128)(2,1)} %bitcast.16.refs_1_.refs_3_.refs_5_.refs_7_.refs_9_.refs_4_.refs_10_.refs_13_.refs_17_, ...), custom_call_target="tpu_custom_call" | custom-call | flops 1000 | bytes 1000 | tf_op jit(solution)/shard_map/combine/pallas_call | solution.py:754
  215.2 2.0 collective-permute-start.25
  217.2 2.6 combine.15
  221.9 4.1 %add_convert_fusion = bf16[512,1024]{1,0:T(8,128)(2,1)} fusion(bf16[512,1024]{1,0:T(8,128)(2,1)} %collective-permute-done.15, f32[512,1024]{1,0:T(8,128)} %get-tuple-element.119, f32[528,1024]{1,0:T(8,128)} %get-tuple-element.108.hidden), kind=kLoop, calls=%fused_computation | loop fusion | flops 2097152 | bytes 6291456 | tf_op jit(solution)/shard_map/convert_element_type | solution.py:1153
  226.0 6.4 %collective-permute-done.24 = bf16[4,32,2048]{2,1,0:T(8,128)(2,1)} collective-permute-done((bf16[4,32,2048]{2,1,0:T(8,128)(2,1)}, bf16[4,32,2048]{2,1,0:T(8,128)(2,1)}, u32[]{:S(2)}, u32[]{:S(2)}) %collective-permute-start.24) | collective-permute-done | bytes 524320 | tf_op jit(solution)/shard_map/ppermute | solution.py:33
  233.2 4.2 %combine.16 = bf16[4,32,4224]{2,1,0:T(8,128)(2,1)} custom-call(s32[6]{0:T(128)} %stack.27.info, bf16[2,2,2,2,32,1024]{5,4,3,2,1,0:T(8,128)(2,1)} %bitcast.55, bf16[2,2,2,2,32,4224]{5,4,3,2,1,0:T(8,128)(2,1)} %bitcast.16.refs_1_.refs_3_.refs_5_.refs_7_.refs_9_.refs_4_.refs_10_.refs_13_.refs_17_, bf16[2,2,2,32,2048]{4,3,2,1,0:T(8,128)(2,1)} %bitcast.25.refs_2_.refs_5_.refs_6_, ...), custom_call_target="tpu_custom_call" | custom-call | flops 1000 | bytes 1000 | tf_op jit(solution)/shard_map/combine/pallas_call | solution.py:754
  238.2 2.6 combine.17
  248.2 3.3 %finish.1 = (f32[32,4608]{1,0:T(8,128)}, f32[32,4608]{1,0:T(8,128)}) custom-call(s32[6]{0:T(128)} %stack.27.info, bf16[64,2048]{1,0:T(8,128)(2,1)} %reduce-scatter.8.cloned.1.call-done.refs_0_, bf16[2,2,64,2560]{3,2,1,0:T(8,128)(2,1)} %bitcast.45, bf16[2,64,1280]{2,1,0:T(8,128)(2,1)} %copy-done.4, bf16[64,1280]{1,0:T(8,128)(2,1)} %bitcast.81, ...), custom_call_target="tpu_custom_call" | custom-call | flops 1000 | bytes 1000 | tf_op jit(solution)/shard_map/finish/pallas_call | solution.py:871
  255.7 17.3 %reduce-scatter.6.cloned.1.call-done.refs_0_.refs_1_.refs_2_.refs_3_.refs_4_ = bf16[32,4224]{1,0:T(8,128)(2,1)} async-done(((bf16[128,4224]{1,0:T(8,128)(2,1)}), bf16[32,4224]{1,0:T(8,128)(2,1)}) %reduce-scatter.6.cloned.1.call-update) | async-done | bytes 270352 | tf_op jit(solution)/shard_map/reduce_scatter | solution.py:1017
  273.0 2.4 settle.3
  (102 shorter events, 41.4 us)
Async XLA Ops:
  7.2 210.1 %reduce-scatter.4.cloned.1.call-start = ((), (), s32[]{:S(2)}) async-start(), calls=%async_computation.3 | async-start | bytes 6553600 | tf_op jit(solution)/shard_map/reduce_scatter | solution.py:989
  7.2 14.0 %collective-permute-start = (bf16[512,3072]{1,0:T(8,128)(2,1)}, bf16[512,3072]{1,0:T(8,128)(2,1)}, u32[]{:S(2)}, u32[]{:S(2)}) collective-permute-start(bf16[512,3072]{1,0:T(8,128)(2,1)} %own_x.3), channel_id=1, source_target_pairs={{0,1},{1,0},{2,3},{3,2},{4,5},{5,4},{6,7},{7,6},{8,9},{9,8},{10,11... | collective-permute-start | bytes 9437192 | tf_op jit(solution)/shard_map/ppermute | solution.py:28
  7.7 13.5 %collective-permute-start.1 = (bf16[512,1024]{1,0:T(8,128)(2,1)}, bf16[512,1024]{1,0:T(8,128)(2,1)}, u32[]{:S(2)}, u32[]{:S(2)}) collective-permute-start(bf16[512,1024]{1,0:T(8,128)(2,1)} %out_own.3), channel_id=1, source_target_pairs={{0,1},{1,0},{2,3},{3,2},{4,5},{5,4},{6,7},{7,6},{8,9},{9,8},{10,11... | collective-permute-start | bytes 3145736 | tf_op jit(solution)/shard_map/ppermute | solution.py:28
  7.8 13.4 %collective-permute-start.4 = (bf16[512,1024]{1,0:T(8,128)(2,1)}, bf16[512,1024]{1,0:T(8,128)(2,1)}, u32[]{:S(2)}, u32[]{:S(2)}) collective-permute-start(bf16[512,1024]{1,0:T(8,128)(2,1)} %cotangent.1), channel_id=1, source_target_pairs={{0,1},{1,0},{2,3},{3,2},{4,5},{5,4},{6,7},{7,6},{8,9},{9,8},{10,11... | collective-permute-start | bytes 3145736 | tf_op jit(solution)/shard_map/ppermute | solution.py:28
  9.8 3.3 %collective-permute-start.5 = (bf16[16,2048]{1,0:T(8,128)(2,1)S(1)}, bf16[16,2048]{1,0:T(8,128)(2,1)S(1)}, u32[]{:S(2)}, u32[]{:S(2)}) collective-permute-start(bf16[16,2048]{1,0:T(8,128)(2,1)S(1)} %pad_maximum_fusion), channel_id=1, source_target_pairs={{1,0},{2,1},{3,2},{4,3},{5,4},{6,5},{7,6},{8,7},{9,8},{10,9},{11,1... | collective-permute-start | bytes 196616 | tf_op jit(solution)/shard_map/ppermute | solution.py:24
  13.1 8.1 %collective-permute-start.6 = (bf16[16,2048]{1,0:T(8,128)(2,1)S(1)}, bf16[16,2048]{1,0:T(8,128)(2,1)S(1)}, u32[]{:S(2)}, u32[]{:S(2)}) collective-permute-start(bf16[16,2048]{1,0:T(8,128)(2,1)S(1)} %collective-permute-done.5.after.g_after), channel_id=1, source_target_pairs={{0,1},{1,0},{2,3},{3,2},{4,5},{5,4},{6,7},{7,6},{8,9},{9,8},{10,11... | collective-permute-start | bytes 196616 | tf_op jit(solution)/shard_map/ppermute | solution.py:28
  21.2 20.7 %collective-permute-start.7 = (bf16[512,4608]{1,0:T(8,128)(2,1)}, bf16[512,4608]{1,0:T(8,128)(2,1)}, u32[]{:S(2)}, u32[]{:S(2)}) collective-permute-start(bf16[512,4608]{1,0:T(8,128)(2,1)} %gate_own.1), channel_id=1, source_target_pairs={{0,1},{1,0},{2,3},{3,2},{4,5},{5,4},{6,7},{7,6},{8,9},{9,8},{10,11... | collective-permute-start | bytes 14155784 | tf_op jit(solution)/shard_map/ppermute | solution.py:28
  24.3 17.5 %collective-permute-start.8 = (bf16[512,4608]{1,0:T(8,128)(2,1)}, bf16[512,4608]{1,0:T(8,128)(2,1)}, u32[]{:S(2)}, u32[]{:S(2)}) collective-permute-start(bf16[512,4608]{1,0:T(8,128)(2,1)} %up_own.1), channel_id=1, source_target_pairs={{0,1},{1,0},{2,3},{3,2},{4,5},{5,4},{6,7},{7,6},{8,9},{9,8},{10,11... | collective-permute-start | bytes 14155784 | tf_op jit(solution)/shard_map/ppermute | solution.py:28
  95.6 149.9 %reduce-scatter.8.cloned.1.call-start = ((), (), s32[]{:S(2)}) async-start(), calls=%async_computation.5 | async-start | bytes 1310720 | tf_op jit(solution)/shard_map/reduce_scatter | solution.py:1017
  95.6 29.0 %collective-permute-start.10 = (bf16[528,1024]{1,0:T(8,128)(2,1)}, bf16[528,1024]{1,0:T(8,128)(2,1)}, u32[]{:S(2)}, u32[]{:S(2)}) collective-permute-start(bf16[528,1024]{1,0:T(8,128)(2,1)} %get-tuple-element.121), channel_id=1, source_target_pairs={{0,1},{1,0},{2,3},{3,2},{4,5},{5,4},{6,7},{7,6},{8,9},{9,8},{10,11... | collective-permute-start | bytes 3244040 | tf_op jit(solution)/shard_map/ppermute | solution.py:28
  95.9 26.5 %collective-permute-start.11 = (bf16[8,64,1024]{2,1,0:T(8,128)(2,1)}, bf16[8,64,1024]{2,1,0:T(8,128)(2,1)}, u32[]{:S(2)}, u32[]{:S(2)}) collective-permute-start(bf16[8,64,1024]{2,1,0:T(8,128)(2,1)} %get-tuple-element.127), channel_id=1, source_target_pairs={{0,2},{2,0},{4,6},{6,4},{8,10},{10,8},{12,14},{14,12},{16,18},{18,... | collective-permute-start | bytes 3145736 | tf_op jit(solution)/shard_map/ppermute | solution.py:33
  98.5 26.1 %collective-permute-start.12 = (bf16[4,128,1024]{2,1,0:T(8,128)(2,1)}, bf16[4,128,1024]{2,1,0:T(8,128)(2,1)}, u32[]{:S(2)}, u32[]{:S(2)}) collective-permute-start(bf16[4,128,1024]{2,1,0:T(8,128)(2,1)} %get-tuple-element.128), channel_id=1, source_target_pairs={{0,4},{2,6},{4,0},{6,2},{8,12},{10,14},{12,8},{14,10},{16,20},{18,... | collective-permute-start | bytes 3145736 | tf_op jit(solution)/shard_map/ppermute | solution.py:33
  124.6 32.2 %collective-permute-start.13 = (bf16[4,288,512]{2,1,0:T(8,128)(2,1)}, bf16[4,288,512]{2,1,0:T(8,128)(2,1)}, u32[]{:S(2)}, u32[]{:S(2)}) collective-permute-start(bf16[4,288,512]{2,1,0:T(8,128)(2,1)} %get-tuple-element.146), channel_id=1, source_target_pairs={{0,2},{2,0},{4,6},{6,4},{8,10},{10,8},{12,14},{14,12},{16,18},{18,... | collective-permute-start | bytes 3538952 | tf_op jit(solution)/shard_map/ppermute | solution.py:33
  124.9 31.9 %collective-permute-start.14 = (bf16[2,576,512]{2,1,0:T(8,128)(2,1)}, bf16[2,576,512]{2,1,0:T(8,128)(2,1)}, u32[]{:S(2)}, u32[]{:S(2)}) collective-permute-start(bf16[2,576,512]{2,1,0:T(8,128)(2,1)} %get-tuple-element.147), channel_id=1, source_target_pairs={{0,4},{2,6},{4,0},{6,2},{8,12},{10,14},{12,8},{14,10},{16,20},{18,... | collective-permute-start | bytes 3538952 | tf_op jit(solution)/shard_map/ppermute | solution.py:33
  126.6 30.2 %collective-permute-start.15 = (bf16[512,1024]{1,0:T(8,128)(2,1)}, bf16[512,1024]{1,0:T(8,128)(2,1)}, u32[]{:S(2)}, u32[]{:S(2)}) collective-permute-start(bf16[512,1024]{1,0:T(8,128)(2,1)} %get-tuple-element.148), channel_id=1, source_target_pairs={{0,1},{1,0},{2,3},{3,2},{4,5},{5,4},{6,7},{7,6},{8,9},{9,8},{10,11... | collective-permute-start | bytes 3145736 | tf_op jit(solution)/shard_map/ppermute | solution.py:28
  156.8 7.8 %collective-permute-start.16 = (bf16[16,32,4224]{2,1,0:T(8,128)(2,1)}, bf16[16,32,4224]{2,1,0:T(8,128)(2,1)}, u32[]{:S(2)}, u32[]{:S(2)}) collective-permute-start(bf16[16,32,4224]{2,1,0:T(8,128)(2,1)} %get-tuple-element.152), channel_id=1, source_target_pairs={{0,1},{1,0},{2,3},{3,2},{4,5},{5,4},{6,7},{7,6},{8,9},{9,8},{10,11... | collective-permute-start | bytes 12976136 | tf_op jit(solution)/shard_map/ppermute | solution.py:28
  156.9 15.1 %collective-permute-start.21 = (bf16[4,64,1024]{2,1,0:T(8,128)(2,1)}, bf16[4,64,1024]{2,1,0:T(8,128)(2,1)}, u32[]{:S(2)}, u32[]{:S(2)}) collective-permute-start(bf16[4,64,1024]{2,1,0:T(8,128)(2,1)} %get-tuple-element.134), channel_id=1, source_target_pairs={{0,4},{2,6},{4,0},{6,2},{8,12},{10,14},{12,8},{14,10},{16,20},{18,... | collective-permute-start | bytes 1572872 | tf_op jit(solution)/shard_map/ppermute | solution.py:33
  157.2 15.1 %collective-permute-start.22 = (bf16[4,64,1024]{2,1,0:T(8,128)(2,1)}, bf16[4,64,1024]{2,1,0:T(8,128)(2,1)}, u32[]{:S(2)}, u32[]{:S(2)}) collective-permute-start(bf16[4,64,1024]{2,1,0:T(8,128)(2,1)} %get-tuple-element.135), channel_id=1, source_target_pairs={{0,2},{2,0},{4,6},{6,4},{8,10},{10,8},{12,14},{14,12},{16,18},{18,... | collective-permute-start | bytes 1572872 | tf_op jit(solution)/shard_map/ppermute | solution.py:33
  162.2 22.4 %collective-permute-start.19 = (bf16[2,288,512]{2,1,0:T(8,128)(2,1)}, bf16[2,288,512]{2,1,0:T(8,128)(2,1)S(1)}, u32[]{:S(2)}, u32[]{:S(2)}) collective-permute-start(bf16[2,288,512]{2,1,0:T(8,128)(2,1)} %get-tuple-element.157), channel_id=1, source_target_pairs={{0,4},{2,6},{4,0},{6,2},{8,12},{10,14},{12,8},{14,10},{16,20},{18,... | collective-permute-start | bytes 1769480 | tf_op jit(solution)/shard_map/ppermute | solution.py:33
  163.9 21.0 %collective-permute-start.20 = (bf16[2,288,512]{2,1,0:T(8,128)(2,1)}, bf16[2,288,512]{2,1,0:T(8,128)(2,1)}, u32[]{:S(2)}, u32[]{:S(2)}) collective-permute-start(bf16[2,288,512]{2,1,0:T(8,128)(2,1)} %get-tuple-element.158), channel_id=1, source_target_pairs={{0,2},{2,0},{4,6},{6,4},{8,10},{10,8},{12,14},{14,12},{16,18},{18,... | collective-permute-start | bytes 1769480 | tf_op jit(solution)/shard_map/ppermute | solution.py:33
  168.7 42.7 %collective-permute-start.18 = (bf16[8,32,2176]{2,1,0:T(8,128)(2,1)}, bf16[8,32,2176]{2,1,0:T(8,128)(2,1)}, u32[]{:S(2)}, u32[]{:S(2)}) collective-permute-start(bf16[8,32,2176]{2,1,0:T(8,128)(2,1)} %get-tuple-element.165), channel_id=1, source_target_pairs={{0,4},{2,6},{4,0},{6,2},{8,12},{10,14},{12,8},{14,10},{16,20},{18,... | collective-permute-start | bytes 3342344 | tf_op jit(solution)/shard_map/ppermute | solution.py:33
  175.9 97.0 %reduce-scatter.6.cloned.1.call-start = ((), (), s32[]{:S(2)}) async-start(), calls=%async_computation.4 | async-start | bytes 1351680 | tf_op jit(solution)/shard_map/reduce_scatter | solution.py:1017
  176.2 35.2 %collective-permute-start.17 = (bf16[8,32,2048]{2,1,0:T(8,128)(2,1)}, bf16[8,32,2048]{2,1,0:T(8,128)(2,1)}, u32[]{:S(2)}, u32[]{:S(2)}) collective-permute-start(bf16[8,32,2048]{2,1,0:T(8,128)(2,1)} %get-tuple-element.164), channel_id=1, source_target_pairs={{0,2},{2,0},{4,6},{6,4},{8,10},{10,8},{12,14},{14,12},{16,18},{18,... | collective-permute-start | bytes 3145736 | tf_op jit(solution)/shard_map/ppermute | solution.py:33
  188.5 17.1 %collective-permute-start.23 = (bf16[1,288,1024]{2,1,0:T(8,128)(2,1)}, bf16[1,288,1024]{2,1,0:T(8,128)(2,1)S(1)}, u32[]{:S(2)}, u32[]{:S(2)}) collective-permute-start(bf16[1,288,1024]{2,1,0:T(8,128)(2,1)} %combine.13), channel_id=1, source_target_pairs={{0,8},{2,10},{4,12},{6,14},{8,0},{10,2},{12,4},{14,6},{16,24},{18,... | collective-permute-start | bytes 1769480 | tf_op jit(solution)/shard_map/ppermute | solution.py:33
  210.1 27.3 %collective-permute-start.31 = (bf16[288,1024]{1,0:T(8,128)(2,1)}, bf16[288,1024]{1,0:T(8,128)(2,1)}, u32[]{:S(2)}, u32[]{:S(2)}) collective-permute-start(bf16[288,1024]{1,0:T(8,128)(2,1)} %get-tuple-element.172), channel_id=1, source_target_pairs={{1,17},{3,19},{5,21},{7,23},{9,25},{11,27},{13,29},{15,31},{16,0},... | collective-permute-start | bytes 1769480 | tf_op jit(solution)/shard_map/ppermute | solution.py:1131
  215.2 17.2 %collective-permute-start.25 = (bf16[4,32,2176]{2,1,0:T(8,128)(2,1)}, bf16[4,32,2176]{2,1,0:T(8,128)(2,1)S(1)}, u32[]{:S(2)}, u32[]{:S(2)}) collective-permute-start(bf16[4,32,2176]{2,1,0:T(8,128)(2,1)} %get-tuple-element.176), channel_id=1, source_target_pairs={{0,2},{2,0},{4,6},{6,4},{8,10},{10,8},{12,14},{14,12},{16,18},{18,... | collective-permute-start | bytes 1671176 | tf_op jit(solution)/shard_map/ppermute | solution.py:33
  217.2 15.2 %collective-permute-start.24 = (bf16[4,32,2048]{2,1,0:T(8,128)(2,1)}, bf16[4,32,2048]{2,1,0:T(8,128)(2,1)}, u32[]{:S(2)}, u32[]{:S(2)}) collective-permute-start(bf16[4,32,2048]{2,1,0:T(8,128)(2,1)} %get-tuple-element.175), channel_id=1, source_target_pairs={{0,4},{2,6},{4,0},{6,2},{8,12},{10,14},{12,8},{14,10},{16,20},{18,... | collective-permute-start | bytes 1572872 | tf_op jit(solution)/shard_map/ppermute | solution.py:33
  219.8 17.6 %collective-permute-start.26 = (bf16[2,64,1280]{2,1,0:T(8,128)(2,1)}, bf16[2,64,1280]{2,1,0:T(8,128)(2,1)S(1)}, u32[]{:S(2)}, u32[]{:S(2)}) collective-permute-start(bf16[2,64,1280]{2,1,0:T(8,128)(2,1)} %get-tuple-element.178), channel_id=1, source_target_pairs={{0,2},{2,0},{4,6},{6,4},{8,10},{10,8},{12,14},{14,12},{16,18},{18,... | collective-permute-start | bytes 983048 | tf_op jit(solution)/shard_map/ppermute | solution.py:33
  219.9 17.9 %collective-permute-start.27 = (bf16[2,64,1280]{2,1,0:T(8,128)(2,1)}, bf16[2,64,1280]{2,1,0:T(8,128)(2,1)}, u32[]{:S(2)}, u32[]{:S(2)}) collective-permute-start(bf16[2,64,1280]{2,1,0:T(8,128)(2,1)} %get-tuple-element.179), channel_id=1, source_target_pairs={{0,4},{2,6},{4,0},{6,2},{8,12},{10,14},{12,8},{14,10},{16,20},{18,... | collective-permute-start | bytes 983048 | tf_op jit(solution)/shard_map/ppermute | solution.py:33
  240.8 5.5 %collective-permute-start.28 = (bf16[1,64,1280]{2,1,0:T(8,128)(2,1)}, bf16[1,64,1280]{2,1,0:T(8,128)(2,1)S(1)}, u32[]{:S(2)}, u32[]{:S(2)}) collective-permute-start(bf16[1,64,1280]{2,1,0:T(8,128)(2,1)} %get-tuple-element.191), channel_id=1, source_target_pairs={{0,4},{2,6},{4,0},{6,2},{8,12},{10,14},{12,8},{14,10},{16,20},{18,... | collective-permute-start | bytes 491528 | tf_op jit(solution)/shard_map/ppermute | solution.py:33
  241.4 6.1 %collective-permute-start.29 = (bf16[1,64,1280]{2,1,0:T(8,128)(2,1)}, bf16[1,64,1280]{2,1,0:T(8,128)(2,1)S(1)}, u32[]{:S(2)}, u32[]{:S(2)}) collective-permute-start(bf16[1,64,1280]{2,1,0:T(8,128)(2,1)} %get-tuple-element.192), channel_id=1, source_target_pairs={{0,2},{2,0},{4,6},{6,4},{8,10},{10,8},{12,14},{14,12},{16,18},{18,... | collective-permute-start | bytes 491528 | tf_op jit(solution)/shard_map/ppermute | solution.py:33
  245.5 7.1 %collective-permute-start.32 = (f32[144,1024]{1,0:T(8,128)}, f32[144,1024]{1,0:T(8,128)S(1)}, u32[]{:S(2)}, u32[]{:S(2)}) collective-permute-start(f32[144,1024]{1,0:T(8,128)} %dynamic-slice_bitcast_fusion), channel_id=1, source_target_pairs={{0,1},{1,0},{2,3},{3,2},{4,5},{5,4},{6,7},{7,6},{8,9},{9,8},{10,11... | collective-permute-start | bytes 1769480 | tf_op jit(solution)/shard_map/ppermute | solution.py:28
  (14 other events, 57.5 us)
Sparse Core Ops, SparseCore 0:
  95.7 95.9 reduce-scatter.3
  194.0 30.2 reduce-scatter.7
  245.6 27.2 reduce-scatter.5

commit v4 on v3

--- a/solution.py
+++ b/solution.py
@@ -133,12 +133,12 @@
     join_rows(weights, (own_b, own_c, own_x), (other_b, other_c, other_x))
     proj = dot(normed[...], weights[...], NN)
     b_part, c_part, x_part = proj[:, :TILE], proj[:, TILE : 2 * TILE], proj[:, 2 * TILE :]
-    b_ref[...] = b_part
-    c_ref[...] = c_part
-    x_ref[...] = x_part
+    b_ref[...] = b_part.astype(b_ref.dtype)
+    c_ref[...] = c_part.astype(c_ref.dtype)
+    x_ref[...] = x_part.astype(x_ref.dtype)
     mixed[...] = b_part * x_part
     conv = conv_rows(mixed, keeps[:, 0:1], keeps[:, 1:2], taps, ext)[3]
-    gated[...] = (c_ref[pl.ds(HALO, ext), :] * conv).astype(jnp.bfloat16)
+    gated[...] = (c_part[HALO:, :] * conv).astype(jnp.bfloat16)
     here = pl.num_programs(0) // 2
 
     @pl.when(step < here)
@@ -190,7 +190,7 @@
     column = pl.BlockSpec((ext + HALO, TILE), lambda j, info: (0, at(j, info)))
     return pl.pallas_call(
         forward_kernel,
-        out_shape=[jax.ShapeDtypeStruct((ext + HALO, width), jnp.float32)] * 3
+        out_shape=[jax.ShapeDtypeStruct((ext + HALO, width), jnp.bfloat16)] * 3
         + [jax.ShapeDtypeStruct((ext, width), jnp.float32)]
         + [jax.ShapeDtypeStruct((ext, width), jnp.bfloat16)] * 2,
         grid_spec=pltpu.PrefetchScalarGridSpec(
@@ -320,9 +320,9 @@
         d_gated[...] = dot(d_branch[...], out_other[...], NT)
 
     join_rows(weights, (own_b, own_c, own_x), (other_b, other_c, other_x))
-    mixed[...] = b_ref[...] * x_ref[...]
+    mixed[...] = b_ref[...].astype(jnp.float32) * x_ref[...].astype(jnp.float32)
     now, one, two, conv = conv_rows(mixed, keeps[:, 0:1], keeps[:, 1:2], taps, ext)
-    c_part = c_ref[pl.ds(HALO, ext), :]
+    c_part = c_ref[pl.ds(HALO, ext), :].astype(jnp.float32)
     grad = d_gated[...]
     gated = (c_part[:rows] * conv[:rows]).astype(jnp.bfloat16)
     d_conv = grad * c_part
@@ -337,9 +337,9 @@
     d_mixed = (
         taps[2:3, :] * d_conv[:rows] + along_one[pl.ds(1, rows), :] + along_two[pl.ds(2, rows), :]
     )
-    d_proj[:, :TILE] = (d_mixed * x_ref[pl.ds(HALO, rows), :]).astype(jnp.bfloat16)
+    d_proj[:, :TILE] = (d_mixed * x_ref[pl.ds(HALO, rows), :].astype(jnp.float32)).astype(jnp.bfloat16)
     d_proj[:, TILE : 2 * TILE] = (grad[:rows] * conv[:rows]).astype(jnp.bfloat16)
-    d_proj[:, 2 * TILE :] = (d_mixed * b_ref[pl.ds(HALO, rows), :]).astype(jnp.bfloat16)
+    d_proj[:, 2 * TILE :] = (d_mixed * b_ref[pl.ds(HALO, rows), :].astype(jnp.float32)).astype(jnp.bfloat16)
     out_grad = dot(gated, d_branch[:rows, :], TN)
     in_grad = dot(norm_in[...], d_proj[...], TN)
     d_norm_in[...] += dot(d_proj[...], weights[...], NT)
@@ -1073,9 +1073,7 @@
         w_out_other,
         2 * chips,
     )
-    conv_send, conv_keeps, down_x, down_y, out_came = ordering(
-        (conv_send, conv_keeps, down_x, down_y, out_came)
-    )
+    conv_send, conv_keeps, down_x, down_y = ordering((conv_send, conv_keeps, down_x, down_y))
     conv_came = partner(conv_send)
 
     down_bits = bits[1:]

time: 284 us -> 283 us (level)
  transfers between devices with their start and end apart: 36 -> 36, of which waited for: 17 -> 18; matrix products, arithmetic and copies ran while one was open for 6% -> 6% of each run, Pallas kernels for 34% -> 34%
where the time goes in v4:
time: 283 us; the launch traced here: 282 us
  Pallas kernels  148 us (52%)
  waiting for transfers between devices  63.5 us (22%)
  starting transfers between devices  34.1 us (12%)
  between operations  14 us (5%)
  local copies, waits for them, and re-layouts  11 us (4%)
  other arithmetic  10.8 us (4%)
    pallas_call x1, Pallas kernels, ffn(): pl.pallas_call(functools.partial(ffn_kernel, 3, split), out_shape=shapes,...  50.8 us
    ppermute x17, waiting for transfers between devices, across(): lax.ppermute(value, 'seq', [(place, place ^ 1 << bit) for place in range(...  39.7 us
    pallas_call x9, Pallas kernels, combine(): pl.pallas_call(functools.partial(combine_kernel, plan), out_shape=shapes,...  30.2 us
    pallas_call x1, Pallas kernels, conv_backward(): pl.pallas_call(backward_kernel, out_shape=[jax.ShapeDtypeStruct((rows, wi...  26.7 us
    ppermute x17, starting transfers between devices, across(): lax.ppermute(value, 'seq', [(place, place ^ 1 << bit) for place in range(...  21 us
    reduce_scatter x2, waiting for transfers between devices, upper_sum(): lax.psum_scatter(value, 'seq', scatter_dimension=0, axis_index_groups=gro...  17.8 us
    pallas_call x1, Pallas kernels, down_part(): pl.pallas_call(down_kernel, out_shape=shapes, grid_spec=pltpu.PrefetchSca...  17.5 us
    pallas_call x1, Pallas kernels, conv_forward(): pl.pallas_call(forward_kernel, out_shape=[jax.ShapeDtypeStruct((ext + HAL...  13.8 us
  transfers between devices with their start and end apart: 36, of which 18 were waited for; matrix products, arithmetic and copies ran while one was open for 6% of the time, Pallas kernels for 34%

profile of v4, /device:TPU:0, one launch (start us, length us, event | category | flops | bytes accessed | tf_op | source)
XLA Modules:
  0.0 282.0 jit_solution(18012498971134796918)
XLA Ops:
  13.1 3.2 %collective-permute-start.6 = (bf16[16,2048]{1,0:T(8,128)(2,1)S(1)}, bf16[16,2048]{1,0:T(8,128)(2,1)S(1)}, u32[]{:S(2)}, u32[]{:S(2)}) collective-permute-start(bf16[16,2048]{1,0:T(8,128)(2,1)S(1)} %collective-permute-done.5.after.g_after), channel_id=1, source_target_pairs={{0,1},{1,0},{2,3},{3,2},{4,5},{5,4},{6,7},{7,6},{8,9},{9,8},{10,11... | collective-permute-start | bytes 196616 | tf_op jit(solution)/shard_map/ppermute | solution.py:28
  18.3 2.1 collective-permute-start.3
  21.2 3.1 %collective-permute-start.7 = (bf16[512,4608]{1,0:T(8,128)(2,1)}, bf16[512,4608]{1,0:T(8,128)(2,1)}, u32[]{:S(2)}, u32[]{:S(2)}) collective-permute-start(bf16[512,4608]{1,0:T(8,128)(2,1)} %gate_own.1), channel_id=1, source_target_pairs={{0,1},{1,0},{2,3},{3,2},{4,5},{5,4},{6,7},{7,6},{8,9},{9,8},{10,11... | collective-permute-start | bytes 14155784 | tf_op jit(solution)/shard_map/ppermute | solution.py:28
  27.5 13.8 %conv_forward.1 = (bf16[544,1024]{1,0:T(8,128)(2,1)}, bf16[544,1024]{1,0:T(8,128)(2,1)}, bf16[544,1024]{1,0:T(8,128)(2,1)}, f32[528,1024]{1,0:T(8,128)}, bf16[52...) custom-call(s32[6]{0:T(128)} %stack.27.info, bf16[512,1024]{1,0:T(8,128)(2,1)} %tokens.3, bf16[16,1024]{1,0:T(8,128)(2,1)} %copy-done.10, ...), custom_call_target="tpu_custom_call" | custom-call | flops 1000 | bytes 1000 | tf_op jit(solution)/shard_map/conv_forward/pallas_call | solution.py:191
  41.6 2.9 %collective-permute-done.9.n_other = bf16[528,1024]{1,0:T(8,128)(2,1)} collective-permute-done((bf16[528,1024]{1,0:T(8,128)(2,1)}, bf16[528,1024]{1,0:T(8,128)(2,1)}, u32[]{:S(2)}, u32[]{:S(2)}) %collective-permute-start.9) | collective-permute-done | bytes 1081376 | tf_op jit(solution)/shard_map/ppermute | solution.py:28
  44.4 50.8 %ffn.1 = (bf16[1056,2304]{1,0:T(8,128)(2,1)}, f32[528,1024]{1,0:T(8,128)}, bf16[528,1024]{1,0:T(8,128)(2,1)}, bf16[8,64,1024]{2,1,0:T(8,128)(2,1)}, bf16[8,64,10...) custom-call(s32[6]{0:T(128)} %stack.27.info, ...), custom_call_target="tpu_custom_call" | custom-call | flops 1000 | bytes 1000 | tf_op jit(solution)/shard_map/ffn/pallas_call | solution.py:583
  95.6 2.6 collective-permute-start.11
  98.2 2.4 collective-permute-start.12
  100.6 17.5 %down.1 = (f32[512,1024]{1,0:T(8,128)}, bf16[512,1024]{1,0:T(8,128)(2,1)}, bf16[4,288,512]{2,1,0:T(8,128)(2,1)}, bf16[4,288,512]{2,1,0:T(8,128)(2,1)}, bf16[2,57...) custom-call(s32[6]{0:T(128)} %stack.27.info, bf16[1056,2304]{1,0:T(8,128)(2,1)} %get-tuple-element.117.act, ...), custom_call_target="tpu_custom_call" | custom-call | flops 1000 | bytes 1000 | tf_op jit(solution)/shard_map/down/pallas_call | solution.py:668
  118.1 4.0 %collective-permute-done.11 = bf16[8,64,1024]{2,1,0:T(8,128)(2,1)} collective-permute-done((bf16[8,64,1024]{2,1,0:T(8,128)(2,1)}, bf16[8,64,1024]{2,1,0:T(8,128)(2,1)}, u32[]{:S(2)}, u32[]{:S(2)}) %collective-permute-start.11) | collective-permute-done | bytes 1048608 | tf_op jit(solution)/shard_map/ppermute | solution.py:33
  122.2 2.2 collective-permute-done.12
  126.4 3.1 %combine.9 = (bf16[4,64,1024]{2,1,0:T(8,128)(2,1)}, bf16[4,64,1024]{2,1,0:T(8,128)(2,1)}) custom-call(s32[6]{0:T(128)} %stack.27.info, bf16[2,2,2,64,1024]{4,3,2,1,0:T(8,128)(2,1)} %bitcast.71, bf16[2,2,2,64,1024]{4,3,2,1,0:T(8,128)(2,1)} %bitcast.8.refs_1_, bf16[2,2,2,64,1024]{4,3,2,1,0:T(8,128)(2,1)} %bitcast.73, ...), custom_call_target="tpu_custom_call" | custom-call | flops 1000 | bytes 1000 | tf_op jit(solution)/shard_map/combine/pallas_call | solution.py:754
  129.4 26.7 %conv_backward.1 = (bf16[512,1024]{1,0:T(8,128)(2,1)}, bf16[16,32,4224]{2,1,0:T(8,128)(2,1)}, bf16[16,32,1024]{2,1,0:T(8,128)(2,1)}, bf16[16,32,1024]{2,1,0:T(8,...) custom-call(s32[6]{0:T(128)} %stack.27.info, ...), custom_call_target="tpu_custom_call" | custom-call | flops 1000 | bytes 1000 | tf_op jit(solution)/shard_map/conv_backward/pallas_call | solution.py:404
  158.3 3.2 %combine.10 = (bf16[2,288,512]{2,1,0:T(8,128)(2,1)}, bf16[2,288,512]{2,1,0:T(8,128)(2,1)}) custom-call(s32[6]{0:T(128)} %stack.27.info, bf16[2,2,288,512]{3,2,1,0:T(8,128)(2,1)} %bitcast.47, bf16[2,2,288,512]{3,2,1,0:T(8,128)(2,1)} %bitcast.13.refs_1_, bf16[2,2,288,512]{3,2,1,0:T(8,128)(2,1)} %bitcast.50, ...), custom_call_target="tpu_custom_call" | custom-call | flops 1000 | bytes 1000 | tf_op jit(solution)/shard_map/combine/pallas_call | solution.py:754
  163.9 4.1 %combine.11 = (bf16[8,32,2048]{2,1,0:T(8,128)(2,1)}, bf16[8,32,2176]{2,1,0:T(8,128)(2,1)}) custom-call(s32[6]{0:T(128)} %stack.27.info, bf16[2,2,2,2,32,1024]{5,4,3,2,1,0:T(8,128)(2,1)} %bitcast.53, bf16[2,2,2,2,32,4224]{5,4,3,2,1,0:T(8,128)(2,1)} %bitcast.16.refs_1_.refs_3_.refs_5_.refs_7_.refs_9_.refs_4_.refs_10_.refs_13_.refs_17_, ...), custom_call_target="tpu_custom_call" | custom-call | flops 1000 | bytes 1000 | tf_op jit(solution)/shard_map/combine/pallas_call | solution.py:754
  168.4 3.0 %collective-permute-done.21 = bf16[4,64,1024]{2,1,0:T(8,128)(2,1)} collective-permute-done((bf16[4,64,1024]{2,1,0:T(8,128)(2,1)}, bf16[4,64,1024]{2,1,0:T(8,128)(2,1)}, u32[]{:S(2)}, u32[]{:S(2)}) %collective-permute-start.21) | collective-permute-done | bytes 524320 | tf_op jit(solution)/shard_map/ppermute | solution.py:33
  171.7 3.6 %combine.12 = bf16[4,64,2048]{2,1,0:T(8,128)(2,1)} custom-call(s32[6]{0:T(128)} %stack.27.info, bf16[2,2,2,64,1024]{4,3,2,1,0:T(8,128)(2,1)} %bitcast.72, bf16[2,2,2,64,1024]{4,3,2,1,0:T(8,128)(2,1)} %bitcast.8.refs_1_, bf16[2,2,64,1024]{3,2,1,0:T(8,128)(2,1)} %bitcast.21.refs_2_, bf16[2,2,2,64,1024]{4,3,2,1,0:T(8,128)(2,1)} %bitcast.74, ...), custom_call_target="tpu_custom_call" | custom-call | flops 1000 | bytes 1000 | tf_op jit(solution)/shard_map/combine/pallas_call | solution.py:754
  177.3 6.6 %collective-permute-done.19.refs_2_ = bf16[2,288,512]{2,1,0:T(8,128)(2,1)S(1)} collective-permute-done((bf16[2,288,512]{2,1,0:T(8,128)(2,1)}, bf16[2,288,512]{2,1,0:T(8,128)(2,1)S(1)}, u32[]{:S(2)}, u32[]{:S(2)}) %collective-permute-start.19) | collective-permute-done | bytes 589856 | tf_op jit(solution)/shard_map/ppermute | solution.py:33
  184.7 3.1 %combine.13 = bf16[1,288,1024]{2,1,0:T(8,128)(2,1)} custom-call(s32[6]{0:T(128)} %stack.27.info, bf16[2,2,288,512]{3,2,1,0:T(8,128)(2,1)} %bitcast.48, bf16[2,2,288,512]{3,2,1,0:T(8,128)(2,1)} %bitcast.13.refs_1_, bf16[2,288,512]{2,1,0:T(8,128)(2,1)} %copy-done.3, bf16[2,2,288,512]{3,2,1,0:T(8,128)(2,1)} %bitcast.51, ...), custom_call_target="tpu_custom_call" | custom-call | flops 1000 | bytes 1000 | tf_op jit(solution)/shard_map/combine/pallas_call | solution.py:754
  187.8 2.0 collective-permute-start.23
  189.8 14.0 %collective-permute-done.23 = bf16[1,288,1024]{2,1,0:T(8,128)(2,1)S(1)} collective-permute-done((bf16[1,288,1024]{2,1,0:T(8,128)(2,1)}, bf16[1,288,1024]{2,1,0:T(8,128)(2,1)S(1)}, u32[]{:S(2)}, u32[]{:S(2)}) %collective-permute-start.23) | collective-permute-done | bytes 589856 | tf_op jit(solution)/shard_map/ppermute | solution.py:33
  204.6 3.7 %settle.2 = (f32[288,1024]{1,0:T(8,128)}, bf16[288,1024]{1,0:T(8,128)(2,1)}) custom-call(s32[6]{0:T(128)} %stack.27.info, bf16[2,2,288,512]{3,2,1,0:T(8,128)(2,1)} %bitcast.49, bf16[2,2,288,512]{3,2,1,0:T(8,128)(2,1)} %bitcast.13.refs_1_, bf16[2,288,512]{2,1,0:T(8,128)(2,1)} %copy-done.3, bf16[288,1024]{1,0:T(8,128)(2,1)} %bitcast.76, ...), custom_call_target="tpu_custom_call" | custom-call | flops 1000 | bytes 1000 | tf_op jit(solution)/shard_map/settle/pallas_call | solution.py:849
  209.7 3.8 %combine.14 = (bf16[4,32,2048]{2,1,0:T(8,128)(2,1)}, bf16[4,32,2176]{2,1,0:T(8,128)(2,1)}) custom-call(s32[6]{0:T(128)} %stack.27.info, bf16[2,2,2,2,32,1024]{5,4,3,2,1,0:T(8,128)(2,1)} %bitcast.54, bf16[2,2,2,2,32,4224]{5,4,3,2,1,0:T(8,128)(2,1)} %bitcast.16.refs_1_.refs_3_.refs_5_.refs_7_.refs_9_.refs_4_.refs_10_.refs_13_.refs_17_, ...), custom_call_target="tpu_custom_call" | custom-call | flops 1000 | bytes 1000 | tf_op jit(solution)/shard_map/combine/pallas_call | solution.py:754
  213.5 2.0 collective-permute-start.25
  215.5 2.6 combine.15
  220.2 4.1 %add_convert_fusion = bf16[512,1024]{1,0:T(8,128)(2,1)} fusion(bf16[512,1024]{1,0:T(8,128)(2,1)} %collective-permute-done.13, f32[512,1024]{1,0:T(8,128)} %get-tuple-element.118, f32[528,1024]{1,0:T(8,128)} %get-tuple-element.107.hidden), kind=kLoop, calls=%fused_computation | loop fusion | flops 2097152 | bytes 6291456 | tf_op jit(solution)/shard_map/convert_element_type | solution.py:1151
  224.3 6.2 %collective-permute-done.24 = bf16[4,32,2048]{2,1,0:T(8,128)(2,1)} collective-permute-done((bf16[4,32,2048]{2,1,0:T(8,128)(2,1)}, bf16[4,32,2048]{2,1,0:T(8,128)(2,1)}, u32[]{:S(2)}, u32[]{:S(2)}) %collective-permute-start.24) | collective-permute-done | bytes 524320 | tf_op jit(solution)/shard_map/ppermute | solution.py:33
  231.4 4.2 %combine.16 = bf16[4,32,4224]{2,1,0:T(8,128)(2,1)} custom-call(s32[6]{0:T(128)} %stack.27.info, bf16[2,2,2,2,32,1024]{5,4,3,2,1,0:T(8,128)(2,1)} %bitcast.55, bf16[2,2,2,2,32,4224]{5,4,3,2,1,0:T(8,128)(2,1)} %bitcast.16.refs_1_.refs_3_.refs_5_.refs_7_.refs_9_.refs_4_.refs_10_.refs_13_.refs_17_, bf16[2,2,2,32,2048]{4,3,2,1,0:T(8,128)(2,1)} %bitcast.25.refs_2_.refs_5_.refs_6_, ...), custom_call_target="tpu_custom_call" | custom-call | flops 1000 | bytes 1000 | tf_op jit(solution)/shard_map/combine/pallas_call | solution.py:754
  237.3 2.6 combine.17
  247.1 3.3 %finish.1 = (f32[32,4608]{1,0:T(8,128)}, f32[32,4608]{1,0:T(8,128)}) custom-call(s32[6]{0:T(128)} %stack.27.info, bf16[64,2048]{1,0:T(8,128)(2,1)} %reduce-scatter.8.cloned.1.call-done.refs_0_, bf16[2,2,64,2560]{3,2,1,0:T(8,128)(2,1)} %bitcast.45, bf16[2,64,1280]{2,1,0:T(8,128)(2,1)} %copy-done.5, bf16[64,1280]{1,0:T(8,128)(2,1)} %bitcast.81, ...), custom_call_target="tpu_custom_call" | custom-call | flops 1000 | bytes 1000 | tf_op jit(solution)/shard_map/finish/pallas_call | solution.py:871
  253.9 17.8 %reduce-scatter.6.cloned.1.call-done.refs_0_.refs_1_.refs_2_.refs_3_.refs_4_ = bf16[32,4224]{1,0:T(8,128)(2,1)} async-done(((bf16[128,4224]{1,0:T(8,128)(2,1)}), bf16[32,4224]{1,0:T(8,128)(2,1)}) %reduce-scatter.6.cloned.1.call-update) | async-done | bytes 270352 | tf_op jit(solution)/shard_map/reduce_scatter | solution.py:1017
  271.6 2.4 settle.3
  (104 shorter events, 41.4 us)
Async XLA Ops:
  7.2 208.3 %reduce-scatter.4.cloned.1.call-start = ((), (), s32[]{:S(2)}) async-start(), calls=%async_computation.3 | async-start | bytes 6553600 | tf_op jit(solution)/shard_map/reduce_scatter | solution.py:989
  7.2 14.0 %collective-permute-start = (bf16[512,3072]{1,0:T(8,128)(2,1)}, bf16[512,3072]{1,0:T(8,128)(2,1)}, u32[]{:S(2)}, u32[]{:S(2)}) collective-permute-start(bf16[512,3072]{1,0:T(8,128)(2,1)} %own_x.3), channel_id=1, source_target_pairs={{0,1},{1,0},{2,3},{3,2},{4,5},{5,4},{6,7},{7,6},{8,9},{9,8},{10,11... | collective-permute-start | bytes 9437192 | tf_op jit(solution)/shard_map/ppermute | solution.py:28
  7.7 13.5 %collective-permute-start.1 = (bf16[512,1024]{1,0:T(8,128)(2,1)}, bf16[512,1024]{1,0:T(8,128)(2,1)}, u32[]{:S(2)}, u32[]{:S(2)}) collective-permute-start(bf16[512,1024]{1,0:T(8,128)(2,1)} %out_own.3), channel_id=1, source_target_pairs={{0,1},{1,0},{2,3},{3,2},{4,5},{5,4},{6,7},{7,6},{8,9},{9,8},{10,11... | collective-permute-start | bytes 3145736 | tf_op jit(solution)/shard_map/ppermute | solution.py:28
  7.8 13.4 %collective-permute-start.4 = (bf16[512,1024]{1,0:T(8,128)(2,1)}, bf16[512,1024]{1,0:T(8,128)(2,1)}, u32[]{:S(2)}, u32[]{:S(2)}) collective-permute-start(bf16[512,1024]{1,0:T(8,128)(2,1)} %cotangent.1), channel_id=1, source_target_pairs={{0,1},{1,0},{2,3},{3,2},{4,5},{5,4},{6,7},{7,6},{8,9},{9,8},{10,11... | collective-permute-start | bytes 3145736 | tf_op jit(solution)/shard_map/ppermute | solution.py:28
  9.8 3.3 %collective-permute-start.5 = (bf16[16,2048]{1,0:T(8,128)(2,1)S(1)}, bf16[16,2048]{1,0:T(8,128)(2,1)S(1)}, u32[]{:S(2)}, u32[]{:S(2)}) collective-permute-start(bf16[16,2048]{1,0:T(8,128)(2,1)S(1)} %pad_maximum_fusion), channel_id=1, source_target_pairs={{1,0},{2,1},{3,2},{4,3},{5,4},{6,5},{7,6},{8,7},{9,8},{10,9},{11,1... | collective-permute-start | bytes 196616 | tf_op jit(solution)/shard_map/ppermute | solution.py:24
  13.1 8.1 %collective-permute-start.6 = (bf16[16,2048]{1,0:T(8,128)(2,1)S(1)}, bf16[16,2048]{1,0:T(8,128)(2,1)S(1)}, u32[]{:S(2)}, u32[]{:S(2)}) collective-permute-start(bf16[16,2048]{1,0:T(8,128)(2,1)S(1)} %collective-permute-done.5.after.g_after), channel_id=1, source_target_pairs={{0,1},{1,0},{2,3},{3,2},{4,5},{5,4},{6,7},{7,6},{8,9},{9,8},{10,11... | collective-permute-start | bytes 196616 | tf_op jit(solution)/shard_map/ppermute | solution.py:28
  21.2 20.3 %collective-permute-start.7 = (bf16[512,4608]{1,0:T(8,128)(2,1)}, bf16[512,4608]{1,0:T(8,128)(2,1)}, u32[]{:S(2)}, u32[]{:S(2)}) collective-permute-start(bf16[512,4608]{1,0:T(8,128)(2,1)} %gate_own.1), channel_id=1, source_target_pairs={{0,1},{1,0},{2,3},{3,2},{4,5},{5,4},{6,7},{7,6},{8,9},{9,8},{10,11... | collective-permute-start | bytes 14155784 | tf_op jit(solution)/shard_map/ppermute | solution.py:28
  24.3 17.2 %collective-permute-start.8 = (bf16[512,4608]{1,0:T(8,128)(2,1)}, bf16[512,4608]{1,0:T(8,128)(2,1)}, u32[]{:S(2)}, u32[]{:S(2)}) collective-permute-start(bf16[512,4608]{1,0:T(8,128)(2,1)} %up_own.1), channel_id=1, source_target_pairs={{0,1},{1,0},{2,3},{3,2},{4,5},{5,4},{6,7},{7,6},{8,9},{9,8},{10,11... | collective-permute-start | bytes 14155784 | tf_op jit(solution)/shard_map/ppermute | solution.py:28
  95.3 149.7 %reduce-scatter.8.cloned.1.call-start = ((), (), s32[]{:S(2)}) async-start(), calls=%async_computation.5 | async-start | bytes 1310720 | tf_op jit(solution)/shard_map/reduce_scatter | solution.py:1017
  95.4 29.0 %collective-permute-start.10 = (bf16[528,1024]{1,0:T(8,128)(2,1)}, bf16[528,1024]{1,0:T(8,128)(2,1)}, u32[]{:S(2)}, u32[]{:S(2)}) collective-permute-start(bf16[528,1024]{1,0:T(8,128)(2,1)} %get-tuple-element.119), channel_id=1, source_target_pairs={{0,1},{1,0},{2,3},{3,2},{4,5},{5,4},{6,7},{7,6},{8,9},{9,8},{10,11... | collective-permute-start | bytes 3244040 | tf_op jit(solution)/shard_map/ppermute | solution.py:28
  95.6 26.5 %collective-permute-start.11 = (bf16[8,64,1024]{2,1,0:T(8,128)(2,1)}, bf16[8,64,1024]{2,1,0:T(8,128)(2,1)}, u32[]{:S(2)}, u32[]{:S(2)}) collective-permute-start(bf16[8,64,1024]{2,1,0:T(8,128)(2,1)} %get-tuple-element.125), channel_id=1, source_target_pairs={{0,2},{2,0},{4,6},{6,4},{8,10},{10,8},{12,14},{14,12},{16,18},{18,... | collective-permute-start | bytes 3145736 | tf_op jit(solution)/shard_map/ppermute | solution.py:33
  98.2 26.1 %collective-permute-start.12 = (bf16[4,128,1024]{2,1,0:T(8,128)(2,1)}, bf16[4,128,1024]{2,1,0:T(8,128)(2,1)}, u32[]{:S(2)}, u32[]{:S(2)}) collective-permute-start(bf16[4,128,1024]{2,1,0:T(8,128)(2,1)} %get-tuple-element.126), channel_id=1, source_target_pairs={{0,4},{2,6},{4,0},{6,2},{8,12},{10,14},{12,8},{14,10},{16,20},{18,... | collective-permute-start | bytes 3145736 | tf_op jit(solution)/shard_map/ppermute | solution.py:33
  124.3 31.8 %collective-permute-start.14 = (bf16[4,288,512]{2,1,0:T(8,128)(2,1)}, bf16[4,288,512]{2,1,0:T(8,128)(2,1)}, u32[]{:S(2)}, u32[]{:S(2)}) collective-permute-start(bf16[4,288,512]{2,1,0:T(8,128)(2,1)} %get-tuple-element.147), channel_id=1, source_target_pairs={{0,2},{2,0},{4,6},{6,4},{8,10},{10,8},{12,14},{14,12},{16,18},{18,... | collective-permute-start | bytes 3538952 | tf_op jit(solution)/shard_map/ppermute | solution.py:33
  124.6 31.5 %collective-permute-start.15 = (bf16[2,576,512]{2,1,0:T(8,128)(2,1)}, bf16[2,576,512]{2,1,0:T(8,128)(2,1)}, u32[]{:S(2)}, u32[]{:S(2)}) collective-permute-start(bf16[2,576,512]{2,1,0:T(8,128)(2,1)} %get-tuple-element.148), channel_id=1, source_target_pairs={{0,4},{2,6},{4,0},{6,2},{8,12},{10,14},{12,8},{14,10},{16,20},{18,... | collective-permute-start | bytes 3538952 | tf_op jit(solution)/shard_map/ppermute | solution.py:33
  156.2 7.8 %collective-permute-start.16 = (bf16[16,32,4224]{2,1,0:T(8,128)(2,1)}, bf16[16,32,4224]{2,1,0:T(8,128)(2,1)}, u32[]{:S(2)}, u32[]{:S(2)}) collective-permute-start(bf16[16,32,4224]{2,1,0:T(8,128)(2,1)} %get-tuple-element.150), channel_id=1, source_target_pairs={{0,1},{1,0},{2,3},{3,2},{4,5},{5,4},{6,7},{7,6},{8,9},{9,8},{10,11... | collective-permute-start | bytes 12976136 | tf_op jit(solution)/shard_map/ppermute | solution.py:28
  156.2 15.1 %collective-permute-start.21 = (bf16[4,64,1024]{2,1,0:T(8,128)(2,1)}, bf16[4,64,1024]{2,1,0:T(8,128)(2,1)}, u32[]{:S(2)}, u32[]{:S(2)}) collective-permute-start(bf16[4,64,1024]{2,1,0:T(8,128)(2,1)} %get-tuple-element.135), channel_id=1, source_target_pairs={{0,4},{2,6},{4,0},{6,2},{8,12},{10,14},{12,8},{14,10},{16,20},{18,... | collective-permute-start | bytes 1572872 | tf_op jit(solution)/shard_map/ppermute | solution.py:33
  156.6 15.1 %collective-permute-start.22 = (bf16[4,64,1024]{2,1,0:T(8,128)(2,1)}, bf16[4,64,1024]{2,1,0:T(8,128)(2,1)}, u32[]{:S(2)}, u32[]{:S(2)}) collective-permute-start(bf16[4,64,1024]{2,1,0:T(8,128)(2,1)} %get-tuple-element.136), channel_id=1, source_target_pairs={{0,2},{2,0},{4,6},{6,4},{8,10},{10,8},{12,14},{14,12},{16,18},{18,... | collective-permute-start | bytes 1572872 | tf_op jit(solution)/shard_map/ppermute | solution.py:33
  161.5 22.4 %collective-permute-start.19 = (bf16[2,288,512]{2,1,0:T(8,128)(2,1)}, bf16[2,288,512]{2,1,0:T(8,128)(2,1)S(1)}, u32[]{:S(2)}, u32[]{:S(2)}) collective-permute-start(bf16[2,288,512]{2,1,0:T(8,128)(2,1)} %get-tuple-element.155), channel_id=1, source_target_pairs={{0,4},{2,6},{4,0},{6,2},{8,12},{10,14},{12,8},{14,10},{16,20},{18,... | collective-permute-start | bytes 1769480 | tf_op jit(solution)/shard_map/ppermute | solution.py:33
  163.3 21.0 %collective-permute-start.20 = (bf16[2,288,512]{2,1,0:T(8,128)(2,1)}, bf16[2,288,512]{2,1,0:T(8,128)(2,1)}, u32[]{:S(2)}, u32[]{:S(2)}) collective-permute-start(bf16[2,288,512]{2,1,0:T(8,128)(2,1)} %get-tuple-element.156), channel_id=1, source_target_pairs={{0,2},{2,0},{4,6},{6,4},{8,10},{10,8},{12,14},{14,12},{16,18},{18,... | collective-permute-start | bytes 1769480 | tf_op jit(solution)/shard_map/ppermute | solution.py:33
  168.1 41.6 %collective-permute-start.18 = (bf16[8,32,2176]{2,1,0:T(8,128)(2,1)}, bf16[8,32,2176]{2,1,0:T(8,128)(2,1)}, u32[]{:S(2)}, u32[]{:S(2)}) collective-permute-start(bf16[8,32,2176]{2,1,0:T(8,128)(2,1)} %get-tuple-element.163), channel_id=1, source_target_pairs={{0,4},{2,6},{4,0},{6,2},{8,12},{10,14},{12,8},{14,10},{16,20},{18,... | collective-permute-start | bytes 3342344 | tf_op jit(solution)/shard_map/ppermute | solution.py:33
  175.2 96.4 %reduce-scatter.6.cloned.1.call-start = ((), (), s32[]{:S(2)}) async-start(), calls=%async_computation.4 | async-start | bytes 1351680 | tf_op jit(solution)/shard_map/reduce_scatter | solution.py:1017
  175.5 34.2 %collective-permute-start.17 = (bf16[8,32,2048]{2,1,0:T(8,128)(2,1)}, bf16[8,32,2048]{2,1,0:T(8,128)(2,1)}, u32[]{:S(2)}, u32[]{:S(2)}) collective-permute-start(bf16[8,32,2048]{2,1,0:T(8,128)(2,1)} %get-tuple-element.162), channel_id=1, source_target_pairs={{0,2},{2,0},{4,6},{6,4},{8,10},{10,8},{12,14},{14,12},{16,18},{18,... | collective-permute-start | bytes 3145736 | tf_op jit(solution)/shard_map/ppermute | solution.py:33
  177.3 41.1 %collective-permute-start.13 = (bf16[512,1024]{1,0:T(8,128)(2,1)}, bf16[512,1024]{1,0:T(8,128)(2,1)}, u32[]{:S(2)}, u32[]{:S(2)}) collective-permute-start(bf16[512,1024]{1,0:T(8,128)(2,1)} %get-tuple-element.127), channel_id=1, source_target_pairs={{0,1},{1,0},{2,3},{3,2},{4,5},{5,4},{6,7},{7,6},{8,9},{9,8},{10,11... | collective-permute-start | bytes 3145736 | tf_op jit(solution)/shard_map/ppermute | solution.py:28
  187.8 16.0 %collective-permute-start.23 = (bf16[1,288,1024]{2,1,0:T(8,128)(2,1)}, bf16[1,288,1024]{2,1,0:T(8,128)(2,1)S(1)}, u32[]{:S(2)}, u32[]{:S(2)}) collective-permute-start(bf16[1,288,1024]{2,1,0:T(8,128)(2,1)} %combine.13), channel_id=1, source_target_pairs={{0,8},{2,10},{4,12},{6,14},{8,0},{10,2},{12,4},{14,6},{16,24},{18,... | collective-permute-start | bytes 1769480 | tf_op jit(solution)/shard_map/ppermute | solution.py:33
  208.4 27.2 %collective-permute-start.31 = (bf16[288,1024]{1,0:T(8,128)(2,1)}, bf16[288,1024]{1,0:T(8,128)(2,1)}, u32[]{:S(2)}, u32[]{:S(2)}) collective-permute-start(bf16[288,1024]{1,0:T(8,128)(2,1)} %get-tuple-element.170), channel_id=1, source_target_pairs={{1,17},{3,19},{5,21},{7,23},{9,25},{11,27},{13,29},{15,31},{16,0},... | collective-permute-start | bytes 1769480 | tf_op jit(solution)/shard_map/ppermute | solution.py:1129
  213.5 17.1 %collective-permute-start.25 = (bf16[4,32,2176]{2,1,0:T(8,128)(2,1)}, bf16[4,32,2176]{2,1,0:T(8,128)(2,1)S(1)}, u32[]{:S(2)}, u32[]{:S(2)}) collective-permute-start(bf16[4,32,2176]{2,1,0:T(8,128)(2,1)} %get-tuple-element.174), channel_id=1, source_target_pairs={{0,2},{2,0},{4,6},{6,4},{8,10},{10,8},{12,14},{14,12},{16,18},{18,... | collective-permute-start | bytes 1671176 | tf_op jit(solution)/shard_map/ppermute | solution.py:33
  215.4 15.1 %collective-permute-start.24 = (bf16[4,32,2048]{2,1,0:T(8,128)(2,1)}, bf16[4,32,2048]{2,1,0:T(8,128)(2,1)}, u32[]{:S(2)}, u32[]{:S(2)}) collective-permute-start(bf16[4,32,2048]{2,1,0:T(8,128)(2,1)} %get-tuple-element.173), channel_id=1, source_target_pairs={{0,4},{2,6},{4,0},{6,2},{8,12},{10,14},{12,8},{14,10},{16,20},{18,... | collective-permute-start | bytes 1572872 | tf_op jit(solution)/shard_map/ppermute | solution.py:33
  218.0 17.9 %collective-permute-start.26 = (bf16[2,64,1280]{2,1,0:T(8,128)(2,1)}, bf16[2,64,1280]{2,1,0:T(8,128)(2,1)S(1)}, u32[]{:S(2)}, u32[]{:S(2)}) collective-permute-start(bf16[2,64,1280]{2,1,0:T(8,128)(2,1)} %get-tuple-element.176), channel_id=1, source_target_pairs={{0,2},{2,0},{4,6},{6,4},{8,10},{10,8},{12,14},{14,12},{16,18},{18,... | collective-permute-start | bytes 983048 | tf_op jit(solution)/shard_map/ppermute | solution.py:33
  218.4 18.9 %collective-permute-start.27 = (bf16[2,64,1280]{2,1,0:T(8,128)(2,1)}, bf16[2,64,1280]{2,1,0:T(8,128)(2,1)}, u32[]{:S(2)}, u32[]{:S(2)}) collective-permute-start(bf16[2,64,1280]{2,1,0:T(8,128)(2,1)} %get-tuple-element.177), channel_id=1, source_target_pairs={{0,4},{2,6},{4,0},{6,2},{8,12},{10,14},{12,8},{14,10},{16,20},{18,... | collective-permute-start | bytes 983048 | tf_op jit(solution)/shard_map/ppermute | solution.py:33
  239.9 6.2 %collective-permute-start.28 = (bf16[1,64,1280]{2,1,0:T(8,128)(2,1)}, bf16[1,64,1280]{2,1,0:T(8,128)(2,1)S(1)}, u32[]{:S(2)}, u32[]{:S(2)}) collective-permute-start(bf16[1,64,1280]{2,1,0:T(8,128)(2,1)} %get-tuple-element.189), channel_id=1, source_target_pairs={{0,4},{2,6},{4,0},{6,2},{8,12},{10,14},{12,8},{14,10},{16,20},{18,... | collective-permute-start | bytes 491528 | tf_op jit(solution)/shard_map/ppermute | solution.py:33
  239.9 6.5 %collective-permute-start.29 = (bf16[1,64,1280]{2,1,0:T(8,128)(2,1)}, bf16[1,64,1280]{2,1,0:T(8,128)(2,1)S(1)}, u32[]{:S(2)}, u32[]{:S(2)}) collective-permute-start(bf16[1,64,1280]{2,1,0:T(8,128)(2,1)} %get-tuple-element.190), channel_id=1, source_target_pairs={{0,2},{2,0},{4,6},{6,4},{8,10},{10,8},{12,14},{14,12},{16,18},{18,... | collective-permute-start | bytes 491528 | tf_op jit(solution)/shard_map/ppermute | solution.py:33
  245.0 6.5 %collective-permute-start.32 = (f32[144,1024]{1,0:T(8,128)}, f32[144,1024]{1,0:T(8,128)S(1)}, u32[]{:S(2)}, u32[]{:S(2)}) collective-permute-start(f32[144,1024]{1,0:T(8,128)} %dynamic-slice_bitcast_fusion), channel_id=1, source_target_pairs={{0,1},{1,0},{2,3},{3,2},{4,5},{5,4},{6,7},{7,6},{8,9},{9,8},{10,11... | collective-permute-start | bytes 1769480 | tf_op jit(solution)/shard_map/ppermute | solution.py:28
  (15 other events, 58.0 us)
Sparse Core Ops, SparseCore 0:
  95.4 96.0 reduce-scatter.3
  193.8 30.3 reduce-scatter.7
  245.1 26.4 reduce-scatter.5
